TPU v7x, 256 devices: a whole 4x4x8 slice. The times are simulated.
256 devices in a mesh: seq: 32 (over y, z), head: 8 (over x, core).
Axes of the slice: x: 4, y: 4, z: 8, core: 2. Of those that a mesh axis runs over, the one named last changes fastest.
Arguments:
- queries: bfloat16 [8192, 4096], P('seq', 'head'), may hold values from -140 to 140
- key_rows: bfloat16 [8192, 1024], P('seq', 'head'), may hold values from -15 to 15
- value_rows: bfloat16 [8192, 1024], P('seq', 'head'), may hold values from -4.5 to 4.5
- span_place: int32 [64], replicated, may hold values from 0 to 63, as said below
- block_lists: int32 [64, 8], replicated, may hold values from 0 to 62, as said below
- cotangent: bfloat16 [8192, 4096], P(('seq', 'head')), may hold values from -4.5 to 4.5
Outputs:
- attended: bfloat16 [8192, 4096], P(('seq', 'head'))
- query_grad: bfloat16 [8192, 4096], P('seq', 'head')
- key_grad: bfloat16 [8192, 1024], P('seq', 'head')
- value_grad: bfloat16 [8192, 1024], P('seq', 'head')
Inputs may be any that keep to these rules, and one draw needn't show every extreme that they name: `span_place`: storage slots 2i and 2i+1 hold blocks c and 63 - c for some c below 32; each block is held once. `block_lists`: call blocks c and 63 - c a pair. Each entry of row b is an earlier block or b itself. Among the entries of the two rows of one pair, those that are not their own row's block lie in distinct pairs, none of them that pair.
All inputs are finite; a program needn't handle non-finite values.
Results may differ from a plain program's by a relative error of at most 0.035.
Values may be sent and summed in bfloat16 or wider, within the bound.
No kernel may reach another device: no remote copies, remote signals or barrier semaphores. Data moves between devices by JAX's collectives and lax.ppermute only.
A program may use at most 64 MiB of HBM per device.

v0:
```python
import math

import jax
import jax.numpy as jnp
from jax import lax
from jax.sharding import PartitionSpec as P

HEAD_DIM = 128


def lookup(lookup_table, selector, table_rows):
    matches = selector[..., None] == jnp.arange(table_rows, dtype=jnp.int32)
    return jnp.sum(jnp.where(matches[..., None], lookup_table, 0), axis=-2)


def block_layout(span_place, block_lists):
    slot_total = span_place.shape[0]
    slot_ids = jnp.arange(slot_total, dtype=jnp.int32)
    slot_of = jnp.sum(
        jnp.where(span_place[:, None] == slot_ids[None, :], slot_ids[:, None], 0), axis=0
    )
    pick_blocks = lookup(block_lists, span_place, slot_total)
    valid_cols = []
    for column in range(pick_blocks.shape[1]):
        kept_pick = pick_blocks[:, column] != span_place
        for before in range(column):
            kept_pick = kept_pick & (pick_blocks[:, column] != pick_blocks[:, before])
        valid_cols.append(kept_pick)
    pick_valid = jnp.stack(valid_cols, axis=1)
    pick_slots = lookup(slot_of[:, None], pick_blocks, slot_total)[..., 0]
    return (pick_slots, pick_valid)


def attend_block(query_block, key_set, value_set, grad_block, visible_picks, score_scale):
    span_rows = query_block.shape[0]
    set_count = key_set.shape[0]
    scores = (
        jnp.einsum("ckgd,jekd->kgcje", query_block, key_set, preferred_element_type=jnp.float32)
        * score_scale
    )
    causal = jnp.arange(span_rows)[None, :] <= jnp.arange(span_rows)[:, None]
    others = jnp.broadcast_to(visible_picks[None, :, None], (span_rows, set_count - 1, span_rows))
    allowed = jnp.concatenate([causal[:, None, :], others], axis=1)
    scores = jnp.where(allowed, scores, -jnp.inf)
    row_top = jnp.max(scores, axis=(3, 4), keepdims=True)
    row_total = jnp.sum(jnp.exp(scores - row_top), axis=(3, 4), keepdims=True)
    log_total = row_top + jnp.log(row_total)
    probabilities = jnp.exp(scores - log_total)
    weights = probabilities.astype(jnp.bfloat16)
    attended = jnp.einsum(
        "kgcje,jekd->ckgd", weights, value_set, preferred_element_type=jnp.float32
    ).astype(jnp.bfloat16)
    attended_wide = lax.optimization_barrier(attended).astype(jnp.float32)
    row_delta = jnp.sum(grad_block.astype(jnp.float32) * attended_wide, axis=-1)
    slopes = jnp.einsum(
        "ckgd,jekd->kgcje", grad_block, value_set, preferred_element_type=jnp.float32
    )
    shifted = slopes - jnp.transpose(row_delta, (1, 2, 0))[..., None, None]
    dscores = (probabilities * shifted * score_scale).astype(jnp.bfloat16)
    query_grad = jnp.einsum(
        "kgcje,jekd->ckgd", dscores, key_set, preferred_element_type=jnp.float32
    ).astype(jnp.bfloat16)
    key_part = jnp.einsum(
        "kgcje,ckgd->jekd", dscores, query_block, preferred_element_type=jnp.float32
    )
    value_part = jnp.einsum(
        "kgcje,ckgd->jekd", weights, grad_block, preferred_element_type=jnp.float32
    )
    return (attended, query_grad, key_part, value_part)


def body(queries, key_rows, value_rows, span_place, block_lists, cotangent):
    seq_count = lax.axis_size("seq")
    seq_index = lax.axis_index("seq")
    slot_total = span_place.shape[0]
    pick_count = block_lists.shape[1]
    span_rows = queries.shape[0] // 2
    kv_local = key_rows.shape[1] // HEAD_DIM
    group_size = queries.shape[1] // HEAD_DIM // kv_local
    kv_width = key_rows.shape[1]
    score_scale = 1.0 / math.sqrt(HEAD_DIM)
    grad_heads = lax.all_to_all(cotangent, "head", split_axis=1, concat_axis=0, tiled=True)
    pick_slots, pick_valid = block_layout(span_place, block_lists)
    owners = pick_slots // 2
    halves = pick_slots % 2
    req_owner = owners.reshape(seq_count, 2 * pick_count)
    req_half = halves.reshape(seq_count, 2 * pick_count)
    req_valid = pick_valid.reshape(seq_count, 2 * pick_count)
    served = req_valid & (req_owner == seq_index)
    paired = jnp.concatenate([key_rows, value_rows], axis=1)
    local_pair = paired.reshape(2, span_rows, 2 * kv_width)
    own_slots = seq_index * 2 + jnp.arange(2, dtype=jnp.int32)
    my_slots = lookup(pick_slots, own_slots, slot_total)
    my_valid = lookup(pick_valid.astype(jnp.int32), own_slots, slot_total) > 0
    my_owner = (my_slots // 2).reshape(-1)
    starts = my_slots.reshape(-1) * span_rows
    blank_set = jnp.zeros((2 * pick_count, span_rows, 2 * kv_width), paired.dtype)
    shard_part = lax.all_gather(paired, "seq", axis=0, tiled=True)
    piece_rows = shard_part.shape[0]
    row_index = starts[:, None] + jnp.arange(span_rows, dtype=jnp.int32)[None, :]
    inside = (row_index >= 0) & (row_index < piece_rows)
    taken_rows = jnp.take(shard_part, jnp.clip(row_index, 0, piece_rows - 1).reshape(-1), axis=0)
    fetched = jnp.where(inside[:, :, None], taken_rows.reshape(blank_set.shape), blank_set)
    fetched = fetched.reshape(2, pick_count, span_rows, 2 * kv_width)
    query_sets = queries.reshape(2, span_rows, kv_local, group_size, HEAD_DIM)
    grad_sets = grad_heads.reshape(2, span_rows, kv_local, group_size, HEAD_DIM)
    outputs = []
    query_grads = []
    own_parts = []
    sent_parts = []
    for which_half in range(2):
        key_set = jnp.concatenate([local_pair[which_half][None], fetched[which_half]], axis=0)
        keys_here = key_set[:, :, :kv_width].reshape(pick_count + 1, span_rows, kv_local, HEAD_DIM)
        values_here = key_set[:, :, kv_width:].reshape(
            pick_count + 1, span_rows, kv_local, HEAD_DIM
        )
        attended, query_grad, key_part, value_part = attend_block(
            query_sets[which_half],
            keys_here,
            values_here,
            grad_sets[which_half],
            my_valid[which_half],
            score_scale,
        )
        outputs.append(attended)
        query_grads.append(query_grad)
        grad_parts = jnp.concatenate(
            [
                key_part.reshape(pick_count + 1, span_rows, kv_width),
                value_part.reshape(pick_count + 1, span_rows, kv_width),
            ],
            axis=2,
        )
        own_parts.append(grad_parts[0])
        sent_parts.append(grad_parts[1:].astype(jnp.bfloat16))
    outgoing_grads = jnp.concatenate(sent_parts, axis=0)
    routing = (
        (my_owner[None, :] == jnp.arange(seq_count, dtype=jnp.int32)[:, None])
        & my_valid.reshape(-1)[None, :]
    ).astype(jnp.bfloat16)
    bundle = jnp.einsum(
        "op,pcw->ocw", routing, outgoing_grads, preferred_element_type=jnp.float32
    ).astype(jnp.bfloat16)
    returned = lax.all_to_all(bundle, "seq", split_axis=0, concat_axis=0, tiled=True)
    take_half = jnp.stack([jnp.any(served & (req_half == side), axis=1) for side in range(2)])
    gathered = jnp.einsum(
        "hr,rcw->hcw", take_half.astype(jnp.bfloat16), returned, preferred_element_type=jnp.float32
    )
    totals = jnp.stack(own_parts) + gathered
    key_grad = totals[:, :, :kv_width].reshape(2 * span_rows, kv_width).astype(jnp.bfloat16)
    value_grad = totals[:, :, kv_width:].reshape(2 * span_rows, kv_width).astype(jnp.bfloat16)
    attended_all = jnp.stack(outputs).reshape(2 * span_rows, queries.shape[1])
    query_grad_all = jnp.stack(query_grads).reshape(2 * span_rows, queries.shape[1])
    attended_out = lax.all_to_all(attended_all, "head", split_axis=0, concat_axis=1, tiled=True)
    return (attended_out, query_grad_all, key_grad, value_grad)


def solution(mesh):
    in_specs = (
        P("seq", "head"),
        P("seq", "head"),
        P("seq", "head"),
        P(),
        P(),
        P(("seq", "head"), None),
    )
    out_specs = (P(("seq", "head"), None), P("seq", "head"), P("seq", "head"), P("seq", "head"))
    return jax.shard_map(body, mesh=mesh, in_specs=in_specs, out_specs=out_specs, check_vma=False)
```

profile of v0, /device:TPU:1, one launch (start us, length us, event | category | flops | bytes accessed | tf_op | source)
XLA Modules:
  0.0 198.0 jit_solution(1944021725059806626)
XLA Ops:
  7.2 0.9 constant_dynamic-update-slice_fusion.1
  8.1 0.9 constant_dynamic-update-slice_fusion
  9.0 0.6 copy-done.17
  9.6 1.7 copy.343
  11.4 6.6 %all-to-all-start.1 = ((bf16[32,8,512]{2,0,1:T(8,128)(2,1)}), bf16[32,8,512]{2,0,1:T(8,128)(2,1)S(1)}, u32[]{:S(2)}, u32[]{:S(2)}) async-start(bf16[32,8,512]{2,0,1:T(8,128)(2,1)} %bitcast.241), calls=%async_computation.1 | async-start | bytes 524288 | tf_op jit(solution)/shard_map/all_to_all | solution.py:82
  17.9 0.7 select_reduce_fusion.2
  18.7 0.7 iota_compare_fusion.2
  19.4 1.8 select_reduce_fusion.1
  21.2 1.2 select_reduce_fusion
  22.9 0.7 and_bitcast_fusion
  24.3 0.8 pad_add_fusion.1
  25.1 0.6 gt.11
  25.9 0.8 copy.326
  26.8 0.8 copy.278
  28.1 0.8 copy.269
  29.0 64.7 %all-gather.2.cloned.1.call-done = bf16[8192,256]{1,0:T(8,128)(2,1)} async-done(((bf16[256,256]{1,0:T(8,128)(2,1)}), bf16[8192,256]{1,0:T(8,128)(2,1)}) %all-gather.2.cloned.1.call-update) | async-done | bytes 4194320 | tf_op jit(solution)/shard_map/all_gather | solution.py:98
  93.6 9.4 %gather_fusion = bf16[2048,256]{1,0:T(8,128)(2,1)S(1)} fusion(bf16[8192,256]{1,0:T(8,128)(2,1)} %all-gather.2.cloned.1.call-done, s32[2048]{0:T(1024)S(1)} %broadcast_clamp_fusion), kind=kCustom, calls=%fused_computation | custom fusion | bytes 2105344 | tf_op jit(solution)/shard_map/jit(_take)/gather | solution.py:102
  103.0 0.7 select_select_fusion
  103.8 0.5 fusion.78
  104.6 0.6 fusion.14
  105.2 1.4 convolution_bitcast_fusion.2
  106.6 0.7 fusion.10
  107.3 1.3 convolution_bitcast_fusion.3
  108.7 0.5 fusion.77
  109.5 0.6 fusion.15
  110.1 0.6 copy-done.14
  110.7 0.7 pad_maximum_fusion.5
  111.4 1.8 copy.261
  113.2 1.8 all_to_all.29
  115.0 7.6 %all-to-all-start = ((bf16[8,32,512]{2,1,0:T(8,128)(2,1)}), bf16[8,32,512]{2,1,0:T(8,128)(2,1)}, u32[]{:S(2)}, u32[]{:S(2)}) async-start(bf16[8,32,512]{2,1,0:T(8,128)(2,1)} %all_to_all.29), calls=%async_computation | async-start | bytes 524288 | tf_op jit(solution)/shard_map/all_to_all | solution.py:154
  122.6 1.5 convolution_bitcast_fusion
  124.2 0.7 fusion.11
  124.9 1.0 copy-done.2
  125.9 0.5 convolution_bitcast_fusion.1
  126.7 0.7 copy-done.9
  127.4 0.9 copy.283
  128.4 0.8 convolution_convert_fusion
  129.2 2.5 %copy.284 = bf16[32,128,256]{2,1,0:T(8,128)(2,1)} copy(bf16[32,128,256]{2,0,1:T(8,128)(2,1)S(1)} %convolution_convert_fusion) | data formatting | bytes 4194304 | tf_op jit(solution)/shard_map/convert_element_type | solution.py:143
  131.7 5.8 %all-to-all-start.2 = ((bf16[32,128,256]{2,1,0:T(8,128)(2,1)}), bf16[32,128,256]{2,1,0:T(8,128)(2,1)}, u32[]{:S(2)}, u32[]{:S(2)}) async-start(bf16[32,128,256]{2,1,0:T(8,128)(2,1)} %copy.284), calls=%async_computation.2 | async-start | bytes 4194304 | tf_op jit(solution)/shard_map/all_to_all | solution.py:144
  138.0 0.4 fusion.19
  138.4 0.4 fusion.18
  139.0 0.7 copy.342
  139.8 0.9 fusion.33
  140.7 1.7 copy.328
  142.3 44.3 %all-to-all-done.2 = bf16[32,128,256]{2,1,0:T(8,128)(2,1)} async-done(((bf16[32,128,256]{2,1,0:T(8,128)(2,1)}), bf16[32,128,256]{2,1,0:T(8,128)(2,1)}, u32[]{:S(2)}, u32[]{:S(2)}) %all-to-all-start.2) | async-done | bytes 2097184 | tf_op jit(solution)/shard_map/all_to_all | solution.py:144
  186.6 2.8 %fusion.6 = f32[2,128,256]{2,0,1:T(2,128)S(1)} fusion(bf16[32,128,256]{2,1,0:T(8,128)(2,1)} %all-to-all-done.2, pred[1,32]{1,0:T(4,128)(4,1)S(1)} %bitcast.263, pred[1,32]{1,0:T(4,128)(4,1)S(1)} %bitcast.262), kind=kOutput, calls=%fused_computation.15 | convolution fusion | flops 4194368 | bytes 2359360 | tf_op jit(solution)/shard_map/hr,rcw->hcw/dot_general | solution.py:146
  189.7 0.7 copy.288
  190.4 0.7 copy.287
  (91 shorter events, 4.0 us)
Async XLA Ops:
  7.2 17.9 %copy-start.20 = (bf16[256,512]{1,0:T(8,128)(2,1)S(1)}, bf16[256,512]{1,0:T(8,128)(2,1)}, u32[]{:S(2)}) copy-start(bf16[256,512]{1,0:T(8,128)(2,1)} %param.6) | copy-start | bytes 786436
  7.2 86.4 %all-gather.2.cloned.1.call-start = ((), (), s32[]{:S(2)}) async-start(), calls=%async_computation.3 | async-start | bytes 4325376 | tf_op jit(solution)/shard_map/all_gather | solution.py:98
  9.0 0.6 copy-start.17
  9.6 17.0 %copy-start.18 = (bf16[256,256]{1,0:T(8,128)(2,1)S(1)}, bf16[256,256]{1,0:T(8,128)(2,1)}, u32[]{:S(2)}) copy-start(bf16[256,256]{1,0:T(8,128)(2,1)} %copy-done.17) | copy-start | bytes 393220
  11.4 15.3 %all-to-all-start.1 = ((bf16[32,8,512]{2,0,1:T(8,128)(2,1)}), bf16[32,8,512]{2,0,1:T(8,128)(2,1)S(1)}, u32[]{:S(2)}, u32[]{:S(2)}) async-start(bf16[32,8,512]{2,0,1:T(8,128)(2,1)} %bitcast.241), calls=%async_computation.1 | async-start | bytes 524288 | tf_op jit(solution)/shard_map/all_to_all | solution.py:82
  26.8 2.1 %copy-start.10 = (bf16[128,4,128]{2,1,0:T(4,128)(2,1)}, bf16[128,4,128]{2,1,0:T(4,128)(2,1)S(1)}, u32[]{:S(2)}) copy-start(bf16[128,4,128]{2,1,0:T(4,128)(2,1)S(1)} %reshape.415) | copy-start | bytes 393220
  106.6 2.0 %copy-start.12 = (bf16[128,512]{0,1:T(8,128)(2,1)S(1)}, bf16[128,512]{0,1:T(8,128)(2,1)}, u32[]{:S(2)}) copy-start(bf16[128,512]{0,1:T(8,128)(2,1)} %copy.326) | copy-start | bytes 393220
  106.6 2.0 %copy-start.19 = (pred[128,9,128]{0,2,1:T(8,128)(4,1)S(1)}, pred[128,9,128]{0,2,1:T(8,128)(4,1)}, u32[]{:S(2)}) copy-start(pred[128,9,128]{0,2,1:T(8,128)(4,1)} %get-tuple-element.29) | copy-start | bytes 442372
  107.3 1.8 copy-start
  110.1 0.6 copy-start.14
  115.0 16.7 %all-to-all-start = ((bf16[8,32,512]{2,1,0:T(8,128)(2,1)}), bf16[8,32,512]{2,1,0:T(8,128)(2,1)}, u32[]{:S(2)}, u32[]{:S(2)}) async-start(bf16[8,32,512]{2,1,0:T(8,128)(2,1)} %all_to_all.29), calls=%async_computation | async-start | bytes 524288 | tf_op jit(solution)/shard_map/all_to_all | solution.py:154
  122.6 1.5 copy-start.15
  122.6 1.5 copy-start.16
  122.6 1.6 copy-start.11
  124.1 2.3 %copy-start.8 = (f32[9,128,128]{1,2,0:T(8,128)}, f32[9,128,128]{1,2,0:T(8,128)S(1)}, u32[]{:S(2)}) copy-start(f32[9,128,128]{1,2,0:T(8,128)S(1)} %convolution_bitcast_fusion) | copy-start | bytes 1769476
  124.1 1.8 copy-start.13
  124.2 2.3 %copy-start.4 = (f32[9,128,128]{1,2,0:T(8,128)S(1)}, f32[9,128,128]{1,2,0:T(8,128)}, u32[]{:S(2)}) copy-start(f32[9,128,128]{1,2,0:T(8,128)} %convolution_bitcast_fusion.2) | copy-start | bytes 1769476
  124.2 2.3 %copy-start.6 = (f32[9,128,128]{1,2,0:T(8,128)S(1)}, f32[9,128,128]{1,2,0:T(8,128)}, u32[]{:S(2)}) copy-start(f32[9,128,128]{1,2,0:T(8,128)} %convolution_bitcast_fusion.3) | copy-start | bytes 1769476
  124.9 1.1 copy-start.2
  126.5 0.9 copy-start.9
  127.3 1.0 copy-start.21
  131.7 6.3 %copy-start.1 = (bf16[4,128,9,128]{1,3,0,2:T(8,128)(2,1)S(1)}, bf16[4,128,9,128]{1,3,0,2:T(8,128)(2,1)}, u32[]{:S(2)}) copy-start(bf16[4,128,9,128]{1,3,0,2:T(8,128)(2,1)} %copy-done) | copy-start | bytes 3538948
  131.7 6.7 %copy-start.3 = (bf16[4,128,9,128]{1,3,0,2:T(8,128)(2,1)S(1)}, bf16[4,128,9,128]{1,3,0,2:T(8,128)(2,1)}, u32[]{:S(2)}) copy-start(bf16[4,128,9,128]{1,3,0,2:T(8,128)(2,1)} %copy-done.2) | copy-start | bytes 3538948
  131.7 55.0 %all-to-all-start.2 = ((bf16[32,128,256]{2,1,0:T(8,128)(2,1)}), bf16[32,128,256]{2,1,0:T(8,128)(2,1)}, u32[]{:S(2)}, u32[]{:S(2)}) async-start(bf16[32,128,256]{2,1,0:T(8,128)(2,1)} %copy.284), calls=%async_computation.2 | async-start | bytes 4194304 | tf_op jit(solution)/shard_map/all_to_all | solution.py:144
  138.4 1.4 copy-start.5
  138.4 1.4 copy-start.7
Sparse Core Ops, SparseCore 0:
  10.6 82.9 all-gather.1
where the time goes:
time: 199 us; the launch traced here: 198 us
  waiting for transfers between devices  109 us (55%)
  local copies, waits for them, and re-layouts  31.8 us (16%)
  starting transfers between devices  19.9 us (10%)
  between operations  14.6 us (7%)
  matrix products  12.5 us (6%)
  other arithmetic  10.2 us (5%)
    all_gather x1, waiting for transfers between devices, body(): shard_part = lax.all_gather(paired, 'seq', axis=0, tiled=True)  64.7 us
    all_to_all x1, waiting for transfers between devices, body(): lax.all_to_all(bundle, 'seq', split_axis=0, concat_axis=0, tiled=True)  44.3 us
    gather x1, local copies, waits for them, and re-layouts, body(): jnp.take(shard_part, jnp.clip(row_index, 0, piece_rows - 1).reshape(-1),...  9.36 us
    all_to_all x1, starting transfers between devices, body(): lax.all_to_all(attended_all, 'head', split_axis=0, concat_axis=1, tiled=T...  7.56 us
    all_to_all x1, starting transfers between devices, body(): lax.all_to_all(cotangent, 'head', split_axis=1, concat_axis=0, tiled=True)  6.55 us
    all_to_all x1, starting transfers between devices, body(): lax.all_to_all(bundle, 'seq', split_axis=0, concat_axis=0, tiled=True)  5.8 us
    unnamed x48, local copies, waits for them, and re-layouts  5.61 us
  transfers between devices with their start and end apart: 4, of which 2 were waited for; matrix products, arithmetic and copies ran while one was open for 12% of the time, Pallas kernels for 0%

commit v1 on v0

v1 whole, which is shorter than its diff:
```python
import math

import jax
import jax.numpy as jnp
from jax import lax
from jax.experimental import pallas as pl
from jax.experimental.pallas import tpu as pltpu
from jax.sharding import PartitionSpec as P

HEAD_DIM = 128
SPAN = 128
HIDDEN = -1.0e30
SMEM = pl.BlockSpec(memory_space=pltpu.SMEM)
VMEM = pl.BlockSpec(memory_space=pltpu.VMEM)
NT = (((1,), (1,)), ((), ()))
TN = (((0,), (0,)), ((), ()))


def params(mib=40):
    return pltpu.CompilerParams(vmem_limit_bytes=mib * 1024 * 1024)


def pack_kernel(me_ref, place_ref, lists_ref, key_ref, value_ref, packed_ref, serve_ref, picks_ref, slot_of):
    pairs = packed_ref.shape[0]
    picked = lists_ref.shape[1]
    me = me_ref[0]
    first, second = place_ref[2 * me], place_ref[2 * me + 1]

    @pl.loop(0, 2 * pairs)
    def _(slot):
        slot_of[place_ref[slot]] = slot

    for side in range(2):
        block = place_ref[2 * me + side]
        for j in range(picked):
            pick = lists_ref[block, j]
            picks_ref[side * picked + j] = jnp.where(pick == block, -1, slot_of[pick] // 2)

    @pl.loop(0, pairs)
    def _(other):
        half = jnp.int32(-1)
        for side in range(2):
            block = place_ref[2 * other + side]
            for j in range(picked):
                pick = lists_ref[block, j]
                half = jnp.where(pick == first, 0, half)
                half = jnp.where(pick == second, 1, half)
        half = jnp.where(other == me, -1, half)
        serve_ref[other] = half
        start = pl.multiple_of(jnp.maximum(half, 0) * SPAN, SPAN)
        packed_ref[other, :, :HEAD_DIM] = key_ref[pl.ds(start, SPAN), :]
        packed_ref[other, :, HEAD_DIM:] = value_ref[pl.ds(start, SPAN), :]


def attend_kernel(
    picks_ref, q_ref, g_ref, k_ref, v_ref, got_ref, out_ref, dq_ref, own_ref, sent_ref,
    keys, values, scores, weights, slopes,
):
    slot = pl.program_id(0)
    picked = picks_ref.shape[0] // 2
    heads = q_ref.shape[1] // HEAD_DIM
    scale = 1.0 / math.sqrt(HEAD_DIM)
    owners = [picks_ref[slot * picked + j] for j in range(picked)]
    keys[:SPAN] = k_ref[...]
    values[:SPAN] = v_ref[...]
    for j, owner in enumerate(owners):
        rows = pl.ds((j + 1) * SPAN, SPAN)
        at = jnp.maximum(owner, 0)
        keys[rows, :] = got_ref[at, :, :HEAD_DIM]
        values[rows, :] = got_ref[at, :, HEAD_DIM:]
    columns = [slice(h * HEAD_DIM, (h + 1) * HEAD_DIM) for h in range(heads)]
    q = jnp.concatenate([q_ref[:, c] for c in columns], axis=0)
    g = jnp.concatenate([g_ref[:, c] for c in columns], axis=0)
    rows_all = heads * SPAN
    top = None
    for j in range(picked + 1):
        rows = pl.ds(j * SPAN, SPAN)
        part = lax.dot_general(keys[rows, :], q, NT, preferred_element_type=jnp.float32)
        part = part * (scale * math.log2(math.e))
        if j == 0:
            key_at = lax.broadcasted_iota(jnp.int32, (SPAN, rows_all), 0)
            query_at = lax.broadcasted_iota(jnp.int32, (SPAN, rows_all), 1) % SPAN
            part = jnp.where(key_at <= query_at, part, HIDDEN)
        else:
            part = jnp.where(owners[j - 1] >= 0, part, HIDDEN)
        scores[rows, :] = part
        here = jnp.max(part, axis=0, keepdims=True)
        top = here if top is None else jnp.maximum(top, here)
    total = jnp.zeros_like(top)
    for j in range(picked + 1):
        rows = pl.ds(j * SPAN, SPAN)
        part = jnp.exp2(scores[rows, :] - top)
        scores[rows, :] = part
        total = total + jnp.sum(part, axis=0, keepdims=True)
    inverse = 1.0 / total
    for j in range(picked + 1):
        rows = pl.ds(j * SPAN, SPAN)
        weights[rows, :] = (scores[rows, :] * inverse).astype(jnp.bfloat16)
    out_t = lax.dot_general(values[...], weights[...], TN, preferred_element_type=jnp.float32)
    out_t = out_t.astype(jnp.bfloat16).astype(jnp.float32)
    out = out_t.T.astype(jnp.bfloat16)
    for h, c in enumerate(columns):
        out_ref[:, c] = out[h * SPAN:(h + 1) * SPAN, :]
    delta = jnp.sum(g.astype(jnp.float32).T * out_t, axis=0, keepdims=True)
    inverse = inverse * scale
    for j in range(picked + 1):
        rows = pl.ds(j * SPAN, SPAN)
        part = lax.dot_general(values[rows, :], g, NT, preferred_element_type=jnp.float32)
        slopes[rows, :] = (scores[rows, :] * inverse * (part - delta)).astype(jnp.bfloat16)
    dq_t = lax.dot_general(keys[...], slopes[...], TN, preferred_element_type=jnp.float32)
    dq = dq_t.T.astype(jnp.bfloat16)
    for h, c in enumerate(columns):
        dq_ref[:, c] = dq[h * SPAN:(h + 1) * SPAN, :]
    key_part = jnp.dot(slopes[...], q, preferred_element_type=jnp.float32)
    value_part = jnp.dot(weights[...], g, preferred_element_type=jnp.float32)
    own_ref[:, :HEAD_DIM] = key_part[:SPAN]
    own_ref[:, HEAD_DIM:] = value_part[:SPAN]
    for j, owner in enumerate(owners):
        @pl.when(owner >= 0)
        def _():
            rows = slice((j + 1) * SPAN, (j + 2) * SPAN)
            sent_ref[owner, :, :HEAD_DIM] = key_part[rows].astype(jnp.bfloat16)
            sent_ref[owner, :, HEAD_DIM:] = value_part[rows].astype(jnp.bfloat16)


def add_kernel(serve_ref, own_ref, back_ref, dk_ref, dv_ref, total):
    total[...] = own_ref[...]

    @pl.loop(0, back_ref.shape[0])
    def _(other):
        half = serve_ref[other]

        @pl.when(half >= 0)
        def _():
            start = pl.multiple_of(half * SPAN, SPAN)
            total[pl.ds(start, SPAN), :] += back_ref[other].astype(jnp.float32)

    dk_ref[...] = total[:, :HEAD_DIM].astype(jnp.bfloat16)
    dv_ref[...] = total[:, HEAD_DIM:].astype(jnp.bfloat16)


def body(queries, key_rows, value_rows, span_place, block_lists, cotangent):
    pairs = lax.axis_size("seq")
    picked = block_lists.shape[1]
    width = queries.shape[1]
    bf16 = jnp.bfloat16
    me = lax.axis_index("seq").astype(jnp.int32)[None]
    moved = jax.ShapeDtypeStruct((pairs, SPAN, 2 * HEAD_DIM), bf16)
    packed, serve, picks = pl.pallas_call(
        pack_kernel,
        out_shape=(
            moved,
            jax.ShapeDtypeStruct((pairs,), jnp.int32),
            jax.ShapeDtypeStruct((2 * picked,), jnp.int32),
        ),
        in_specs=[SMEM, SMEM, SMEM, VMEM, VMEM],
        out_specs=(VMEM, SMEM, SMEM),
        scratch_shapes=[pltpu.SMEM((2 * pairs,), jnp.int32)],
        compiler_params=params(),
        name="pack",
    )(me, span_place, block_lists, key_rows, value_rows)
    got = lax.all_to_all(packed, "seq", split_axis=0, concat_axis=0, tiled=True)
    grad_heads = lax.all_to_all(cotangent, "head", split_axis=1, concat_axis=0, tiled=True)
    rows_all = (picked + 1) * SPAN
    half_wide = pl.BlockSpec((SPAN, width), lambda i: (i, 0))
    half_head = pl.BlockSpec((SPAN, HEAD_DIM), lambda i: (i, 0))
    whole = pl.BlockSpec(moved.shape, lambda i: (0, 0, 0))
    attended, query_grad, own, sent = pl.pallas_call(
        attend_kernel,
        grid=(2,),
        out_shape=(
            jax.ShapeDtypeStruct(queries.shape, bf16),
            jax.ShapeDtypeStruct(queries.shape, bf16),
            jax.ShapeDtypeStruct((2 * SPAN, 2 * HEAD_DIM), jnp.float32),
            moved,
        ),
        in_specs=[SMEM, half_wide, half_wide, half_head, half_head, whole],
        out_specs=(half_wide, half_wide, pl.BlockSpec((SPAN, 2 * HEAD_DIM), lambda i: (i, 0)), whole),
        scratch_shapes=[
            pltpu.VMEM((rows_all, HEAD_DIM), bf16),
            pltpu.VMEM((rows_all, HEAD_DIM), bf16),
            pltpu.VMEM((rows_all, width), jnp.float32),
            pltpu.VMEM((rows_all, width), bf16),
            pltpu.VMEM((rows_all, width), bf16),
        ],
        compiler_params=params(),
        name="attend",
    )(picks, queries, grad_heads, key_rows, value_rows, got)
    back = lax.all_to_all(sent, "seq", split_axis=0, concat_axis=0, tiled=True)
    attended_out = lax.all_to_all(attended, "head", split_axis=0, concat_axis=1, tiled=True)
    key_grad, value_grad = pl.pallas_call(
        add_kernel,
        out_shape=(
            jax.ShapeDtypeStruct(key_rows.shape, bf16),
            jax.ShapeDtypeStruct(value_rows.shape, bf16),
        ),
        in_specs=[SMEM, VMEM, VMEM],
        out_specs=(VMEM, VMEM),
        scratch_shapes=[pltpu.VMEM((2 * SPAN, 2 * HEAD_DIM), jnp.float32)],
        compiler_params=params(),
        name="add",
    )(serve, own, back)
    return (attended_out, query_grad, key_grad, value_grad)


def solution(mesh):
    in_specs = (
        P("seq", "head"),
        P("seq", "head"),
        P("seq", "head"),
        P(),
        P(),
        P(("seq", "head"), None),
    )
    out_specs = (P(("seq", "head"), None), P("seq", "head"), P("seq", "head"), P("seq", "head"))
    return jax.shard_map(body, mesh=mesh, in_specs=in_specs, out_specs=out_specs, check_vma=False)
```

time: 199 us -> 153 us (0.77)
  blocking collectives: 0 us -> 73.1 us
  waiting for transfers between devices: 109 us -> 47.9 us
  local copies, waits for them, and re-layouts: 31.8 us -> 6.85 us
  between operations: 14.6 us -> 0.69 us
  matrix products: 12.5 us -> 0 us
  Pallas kernels: 0 us -> 12.4 us
  other arithmetic: 10.2 us -> 0 us
  starting transfers between devices: 19.9 us -> 11.4 us
    all_to_all x0 -> x2, blocking collectives: none -> 73.1 us  [the longest x1 58.1 us: body(): got = lax.all_to_all(packed, 'seq', split_axis=0, concat_axis=0, tiled=True)]
    all_gather x1 -> x0, waiting for transfers between devices: 64.7 us -> none  [body(): shard_part = lax.all_gather(paired, 'seq', axis=0, tiled=True)]
    dot_general x14 -> x0, matrix products: 12.5 us -> none  [the longest x2 2.87 us: attend_block(): jnp.einsum('kgcje,ckgd->jekd', weights, grad_block, preferred_element_typ...]
    pallas_call x0 -> x3, Pallas kernels: none -> 12.4 us  [the longest x1 6.58 us: body(): pl.pallas_call(attend_kernel, grid=(2,), out_shape=(jax.ShapeDtypeStruct(...]
    gather x1 -> x0, local copies, waits for them, and re-layouts: 9.36 us -> none  [body(): jnp.take(shard_part, jnp.clip(row_index, 0, piece_rows - 1).reshape(-1),...]
    all_to_all x2 -> x1, starting transfers between devices: 13.4 us -> 4.82 us  [body(): back = lax.all_to_all(sent, 'seq', split_axis=0, concat_axis=0, tiled=True)]
    reduce_sum x8 -> x0, other arithmetic: 4.75 us -> none  [the longest x3 3.23 us: lookup(): return jnp.sum(jnp.where(matches[..., None], lookup_table, 0), axis=-2)]
    convert_element_type x5 -> x0, local copies, waits for them, and re-layouts: 3.65 us -> none  [the longest x1 2.49 us: body(): bundle = jnp.einsum('op,pcw->ocw', routing, outgoing_grads, preferred_ele...]
  transfers between devices with their start and end apart: 4 -> 2, of which waited for: 2 -> 1; matrix products, arithmetic and copies ran while one was open for 12% -> 1% of each run, Pallas kernels for 0% -> 3%
where the time goes in v1:
time: 153 us; the launch traced here: 152 us
  blocking collectives  73.1 us (48%)
  waiting for transfers between devices  47.9 us (31%)
  Pallas kernels  12.4 us (8%)
  starting transfers between devices  11.4 us (7%)
  local copies, waits for them, and re-layouts  6.85 us (4%)
    all_to_all x1, blocking collectives, body(): got = lax.all_to_all(packed, 'seq', split_axis=0, concat_axis=0, tiled=True)  58.1 us
    all_to_all x1, waiting for transfers between devices, body(): back = lax.all_to_all(sent, 'seq', split_axis=0, concat_axis=0, tiled=True)  47.9 us
    all_to_all x1, blocking collectives, body(): lax.all_to_all(attended, 'head', split_axis=0, concat_axis=1, tiled=True)  15.1 us
    pallas_call x1, Pallas kernels, body(): pl.pallas_call(attend_kernel, grid=(2,), out_shape=(jax.ShapeDtypeStruct(...  6.58 us
    all_to_all x1, starting transfers between devices, body(): lax.all_to_all(cotangent, 'head', split_axis=1, concat_axis=0, tiled=True)  6.55 us
    all_to_all x1, starting transfers between devices, body(): back = lax.all_to_all(sent, 'seq', split_axis=0, concat_axis=0, tiled=True)  4.82 us
    unnamed x15, local copies, waits for them, and re-layouts  4.45 us
    pallas_call x1, Pallas kernels, body(): pl.pallas_call(pack_kernel, out_shape=(moved, jax.ShapeDtypeStruct((pairs...  3.98 us
  transfers between devices with their start and end apart: 2, of which 1 were waited for; matrix products, arithmetic and copies ran while one was open for 1% of the time, Pallas kernels for 3%

profile of v1, /device:TPU:1, one launch (start us, length us, event | category | flops | bytes accessed | tf_op | source)
XLA Modules:
  0.0 152.3 jit_solution(8736857008487216282)
XLA Ops:
  0.6 1.7 %copy.16 = bf16[4,8,8,512]{3,2,0,1:T(8,128)(2,1)} copy(bf16[4,8,8,512]{3,2,1,0:T(8,128)(2,1)} %bitcast.15) | data formatting | bytes 524288 | tf_op jit(solution)/shard_map/all_to_all | solution.py:163
  2.3 6.6 %all-to-all-start = ((bf16[32,8,512]{2,0,1:T(8,128)(2,1)}), bf16[32,8,512]{2,0,1:T(8,128)(2,1)S(1)}, u32[]{:S(2)}, u32[]{:S(2)}) async-start(bf16[32,8,512]{2,0,1:T(8,128)(2,1)} %bitcast.11), calls=%async_computation | async-start | bytes 524288 | tf_op jit(solution)/shard_map/all_to_all | solution.py:163
  8.9 0.8 copy.10.lists_ref
  9.6 0.0 copy-start.2
  9.6 0.8 copy-done.2
  10.5 0.0 copy-start.4
  10.5 0.8 copy-done.4
  11.3 0.0 copy-start.6
  11.3 0.7 copy-done.6
  12.0 4.0 %pack.1 = (bf16[32,128,256]{2,1,0:T(8,128)(2,1)S(1)}, s32[32]{0:T(128)S(1)}, s32[16]{0:T(128)S(1)}) custom-call(s32[1]{0:T(128)} %bitcast.me_ref, s32[64]{0:T(128)S(1)} %copy-done.6, s32[64,8]{1,0:T(8,128)S(1)} %copy.10.lists_ref, bf16[256,128]{1,0:T(8,128)(2,1)S(1)} %copy-done.2, bf16[256,128]{1,0:T(8,128)(2,1)S(1)} %copy-done.4), custom_call_target="tpu_custom_call" | custom-call | tf_op jit(solution)/shard_map/pack/pallas_call | solution.py:149
  15.9 0.0 all-to-all-done
  16.0 0.0 copy-start.1
  16.0 0.0 copy-start.3
  16.0 0.0 copy-start.5
  16.0 58.1 %all_to_all.48.got_ref = bf16[32,128,256]{2,1,0:T(8,128)(2,1)S(1)} all-to-all(bf16[32,128,256]{2,1,0:T(8,128)(2,1)S(1)} %get-tuple-element.14), channel_id=1, replica_groups=mesh['seq'=32,'head'=8] {'seq'}, dimensions={0} | all-to-all | bytes 4194304 | tf_op jit(solution)/shard_map/all_to_all | solution.py:162
  74.1 0.0 copy-done.1
  74.1 0.0 copy-done.3
  74.1 0.0 copy-done.5
  74.1 6.6 %attend.1 = (bf16[256,512]{1,0:T(8,128)(2,1)S(1)}, bf16[256,512]{1,0:T(8,128)(2,1)}, f32[256,256]{1,0:T(8,128)S(1)}, bf16[32,128,256]{2,1,0:T(8,128)(2,1)S(1)}) custom-call(s32[16]{0:T(128)S(1)} %get-tuple-element.13.picks_ref, bf16[256,512]{1,0:T(8,128)(2,1)S(1)} %copy-done.1, bf16[256,512]{1,0:T(8,128)(2,1)S(1)} %bitcast.12, ...), custom_call_target="tpu_custom_call" | custom-call | tf_op jit(solution)/shard_map/attend/pallas_call | solution.py:168
  80.7 0.0 copy-start
  80.7 1.3 copy-done
  82.0 15.1 %all_to_all.49 = bf16[8,32,512]{2,1,0:T(8,128)(2,1)S(1)} all-to-all(bf16[8,32,512]{2,1,0:T(8,128)(2,1)S(1)} %bitcast.13), channel_id=1, replica_groups=mesh['seq'=32,'head'=8] {'head'}, dimensions={0} | all-to-all | bytes 524288 | tf_op jit(solution)/shard_map/all_to_all | solution.py:190
  97.1 4.8 %all-to-all-start.3 = ((bf16[32,128,256]{2,1,0:T(8,128)(2,1)}), bf16[32,128,256]{2,1,0:T(8,128)(2,1)S(1)}, u32[]{:S(2)}, u32[]{:S(2)}) async-start(bf16[32,128,256]{2,1,0:T(8,128)(2,1)} %copy-done), calls=%async_computation.3 | async-start | bytes 4194304 | tf_op jit(solution)/shard_map/all_to_all | solution.py:189
  101.9 0.7 copy.14
  102.6 47.9 %all-to-all-done.3.back_ref = bf16[32,128,256]{2,1,0:T(8,128)(2,1)S(1)} async-done(((bf16[32,128,256]{2,1,0:T(8,128)(2,1)}), bf16[32,128,256]{2,1,0:T(8,128)(2,1)S(1)}, u32[]{:S(2)}, u32[]{:S(2)}) %all-to-all-start.3) | async-done | bytes 2097184 | tf_op jit(solution)/shard_map/all_to_all | solution.py:189
  150.5 1.8 %add.1 = (bf16[256,128]{1,0:T(8,128)(2,1)}, bf16[256,128]{1,0:T(8,128)(2,1)}) custom-call(s32[32]{0:T(128)S(1)} %get-tuple-element.17.serve_ref, f32[256,256]{1,0:T(8,128)S(1)} %get-tuple-element.18.own_ref, bf16[32,128,256]{2,1,0:T(8,128)(2,1)S(1)} %all-to-all-done.3.back_ref), custom_call_target="tpu_custom_call" | custom-call | tf_op jit(solution)/shard_map/add/pallas_call | solution.py:191
Async XLA Ops:
  2.3 13.6 %all-to-all-start = ((bf16[32,8,512]{2,0,1:T(8,128)(2,1)}), bf16[32,8,512]{2,0,1:T(8,128)(2,1)S(1)}, u32[]{:S(2)}, u32[]{:S(2)}) async-start(bf16[32,8,512]{2,0,1:T(8,128)(2,1)} %bitcast.11), calls=%async_computation | async-start | bytes 524288 | tf_op jit(solution)/shard_map/all_to_all | solution.py:163
  9.6 0.8 copy-start.2
  10.5 0.8 copy-start.4
  11.3 0.7 copy-start.6
  16.0 58.1 %copy-start.1 = (bf16[256,512]{1,0:T(8,128)(2,1)S(1)}, bf16[256,512]{1,0:T(8,128)(2,1)}, u32[]{:S(2)}) copy-start(bf16[256,512]{1,0:T(8,128)(2,1)} %q_ref.1) | copy-start | bytes 786436
  16.0 58.1 %copy-start.3 = (bf16[256,128]{1,0:T(8,128)(2,1)S(1)}, bf16[256,128]{1,0:T(8,128)(2,1)}, u32[]{:S(2)}) copy-start(bf16[256,128]{1,0:T(8,128)(2,1)} %k_ref.1) | copy-start | bytes 196612
  16.0 58.1 %copy-start.5 = (bf16[256,128]{1,0:T(8,128)(2,1)S(1)}, bf16[256,128]{1,0:T(8,128)(2,1)}, u32[]{:S(2)}) copy-start(bf16[256,128]{1,0:T(8,128)(2,1)} %v_ref.1) | copy-start | bytes 196612
  80.7 1.3 copy-start
  97.1 53.4 %all-to-all-start.3 = ((bf16[32,128,256]{2,1,0:T(8,128)(2,1)}), bf16[32,128,256]{2,1,0:T(8,128)(2,1)S(1)}, u32[]{:S(2)}, u32[]{:S(2)}) async-start(bf16[32,128,256]{2,1,0:T(8,128)(2,1)} %copy-done), calls=%async_computation.3 | async-start | bytes 4194304 | tf_op jit(solution)/shard_map/all_to_all | solution.py:189

commit v2 on v1

v2 whole, which is shorter than its diff:
```python
import math

import jax
import jax.numpy as jnp
from jax import lax
from jax.experimental import pallas as pl
from jax.experimental.pallas import tpu as pltpu
from jax.sharding import PartitionSpec as P

HEAD_DIM = 128
SPAN = 128
RING = 8
HIDDEN = -1.0e30
SCALE = 1.0 / math.sqrt(HEAD_DIM)
SMEM = pl.BlockSpec(memory_space=pltpu.SMEM)
VMEM = pl.BlockSpec(memory_space=pltpu.VMEM)
ANY = pl.BlockSpec(memory_space=pl.ANY)
NT = (((1,), (1,)), ((), ()))
TN = (((0,), (0,)), ((), ()))
bf16 = jnp.bfloat16
f32 = jnp.float32


def params(mib=40):
    return pltpu.CompilerParams(vmem_limit_bytes=mib * 1024 * 1024)


def route_kernel(me_ref, place_ref, lists_ref, picks_ref, table_ref, slot_of):
    pairs = place_ref.shape[0] // 2
    picked = lists_ref.shape[1]
    lines = pairs // RING
    me = me_ref[0]
    for slot in range(2 * pairs):
        slot_of[place_ref[slot]] = slot
    for at in range(lines * pairs):
        table_ref[at] = -1
    marks = []
    for line in range(lines):
        other = line * RING + me % RING
        for side in range(2):
            block = place_ref[2 * other + side]
            for j in range(picked):
                pick = lists_ref[block, j]
                slot = slot_of[pick]
                marks.append((jnp.where(pick == block, lines * pairs, line * pairs + slot // 2), slot % 2))
    own = []
    for side in range(2):
        block = place_ref[2 * me + side]
        for j in range(picked):
            pick = lists_ref[block, j]
            own.append(jnp.where(pick == block, -1, slot_of[pick] // 2))
    for at, half in marks:
        table_ref[at] = half
    for at, owner in enumerate(own):
        picks_ref[at] = owner


def columns_kernel(cot_ref, after_ref, cols_ref):
    wide = cols_ref.shape[2]
    for part in range(cols_ref.shape[0]):
        cols_ref[part] = cot_ref[:, part * wide:(part + 1) * wide]


def line_kernel(me_ref, table_ref, *refs):
    blocks, outs = refs[:RING], refs[RING:]
    lines = len(outs)
    pairs = lines * RING
    me = me_ref[0]
    mine, at = me // RING, me % RING
    for shift, block in enumerate(blocks):
        source = (at + shift) % RING
        for step, out in enumerate(outs):
            half = table_ref[(mine + step) % lines * pairs + mine * RING + source]
            out[source] = block[pl.ds(pl.multiple_of(jnp.maximum(half, 0) * SPAN, SPAN), SPAN), :]


def stack_heads(ref):
    return jnp.concatenate(
        [ref[:, h * HEAD_DIM:(h + 1) * HEAD_DIM] for h in range(ref.shape[1] // HEAD_DIM)], axis=0
    )


def store_heads(ref, transposed):
    rows = transposed.T.astype(bf16)
    for h in range(ref.shape[1] // HEAD_DIM):
        ref[:, h * HEAD_DIM:(h + 1) * HEAD_DIM] = rows[h * SPAN:(h + 1) * SPAN, :]


def attend_kernel(me_ref, picks_ref, q_ref, g_ref, k_ref, v_ref, *refs):
    lines = (len(refs) - 10) // 2
    got, (out_ref, dq_ref, ownk_ref, ownv_ref), sent = refs[:lines], refs[lines:lines + 4], refs[lines + 4:-6]
    pool, keys, values, scores, weights, slopes = refs[-6:]
    slot = pl.program_id(0)
    mine = me_ref[0] // RING
    picked = picks_ref.shape[0] // 2
    owners = [picks_ref[slot * picked + j] for j in range(picked)]

    @pl.when(slot == 0)
    def _():
        for far, ref in enumerate(got):
            pool[far] = ref[...]

    keys[:SPAN] = k_ref[...]
    values[:SPAN] = v_ref[...]
    for j, owner in enumerate(owners):
        owner = jnp.maximum(owner, 0)
        far = (mine - owner // RING + lines) % lines
        keys[(j + 1) * SPAN:(j + 2) * SPAN, :] = pool[far, owner % RING, :, :HEAD_DIM]
        values[(j + 1) * SPAN:(j + 2) * SPAN, :] = pool[far, owner % RING, :, HEAD_DIM:]
    q = stack_heads(q_ref)
    across = q.shape[0]
    top = None
    for j in range(picked + 1):
        rows = pl.ds(j * SPAN, SPAN)
        part = lax.dot_general(keys[rows, :], q, NT, preferred_element_type=f32)
        part = part * (SCALE * math.log2(math.e))
        if j == 0:
            key_at = lax.broadcasted_iota(jnp.int32, (SPAN, across), 0)
            query_at = lax.broadcasted_iota(jnp.int32, (SPAN, across), 1) % SPAN
            part = jnp.where(key_at <= query_at, part, HIDDEN)
        else:
            part = jnp.where(owners[j - 1] >= 0, part, HIDDEN)
        scores[rows, :] = part
        here = jnp.max(part, axis=0, keepdims=True)
        top = here if top is None else jnp.maximum(top, here)
    total = jnp.zeros_like(top)
    for j in range(picked + 1):
        rows = pl.ds(j * SPAN, SPAN)
        part = jnp.exp2(scores[rows, :] - top)
        scores[rows, :] = part
        total = total + jnp.sum(part, axis=0, keepdims=True)
    inverse = 1.0 / total
    for j in range(picked + 1):
        rows = pl.ds(j * SPAN, SPAN)
        weights[rows, :] = (scores[rows, :] * inverse).astype(bf16)
    g = stack_heads(g_ref)
    out_t = lax.dot_general(values[...], weights[...], TN, preferred_element_type=f32)
    out_t = out_t.astype(bf16).astype(f32)
    store_heads(out_ref, out_t)
    delta = jnp.sum(g.astype(f32).T * out_t, axis=0, keepdims=True)
    inverse = inverse * SCALE
    for j in range(picked + 1):
        rows = pl.ds(j * SPAN, SPAN)
        part = lax.dot_general(values[rows, :], g, NT, preferred_element_type=f32)
        slopes[rows, :] = (scores[rows, :] * inverse * (part - delta)).astype(bf16)
    store_heads(dq_ref, lax.dot_general(keys[...], slopes[...], TN, preferred_element_type=f32))
    key_part = jnp.dot(slopes[...], q, preferred_element_type=f32)
    value_part = jnp.dot(weights[...], g, preferred_element_type=f32)
    ownk_ref[...] = key_part[:SPAN]
    ownv_ref[...] = value_part[:SPAN]
    for j, owner in enumerate(owners):
        step = (jnp.maximum(owner, 0) // RING - mine + lines) % lines
        rows = slice((j + 1) * SPAN, (j + 2) * SPAN)
        for far in range(lines):
            @pl.when((owner >= 0) & (step == far))
            def _():
                sent[far][owner % RING, :, :HEAD_DIM] = key_part[rows].astype(bf16)
                sent[far][owner % RING, :, HEAD_DIM:] = value_part[rows].astype(bf16)


def line_sum_kernel(me_ref, table_ref, after_ref, *refs):
    backs, outs = refs[:-RING], refs[-RING:]
    lines = len(backs)
    pairs = lines * RING
    me = me_ref[0]
    mine, at = me // RING, me % RING
    for shift, out in enumerate(outs):
        owner = (at + shift) % RING
        halves = [
            table_ref[(mine - step + lines) % lines * pairs + mine * RING + owner] for step in range(lines)
        ]
        parts = [back[owner].astype(f32) for back in backs]
        for side in range(2):
            total = jnp.zeros((SPAN, 2 * HEAD_DIM), f32)
            for half, part in zip(halves, parts):
                total += jnp.where(half == side, part, 0.0)
            out[side * SPAN:(side + 1) * SPAN, :] = total.astype(bf16)


def add_kernel(ownk_ref, ownv_ref, *refs):
    parts, outs = refs[:RING], refs[RING:]
    for which, (own, out) in enumerate(zip((ownk_ref, ownv_ref), outs)):
        total = own[...]
        for part in parts:
            total += part[:, which * HEAD_DIM:(which + 1) * HEAD_DIM].astype(f32)
        out[...] = total.astype(bf16)


def body(queries, key_rows, value_rows, span_place, block_lists, cotangent):
    pairs = lax.axis_size("seq")
    lines = pairs // RING
    head_count = lax.axis_size("head")
    picked = block_lists.shape[1]
    width = queries.shape[1]
    me = lax.axis_index("seq").astype(jnp.int32)[None]
    shape = jax.ShapeDtypeStruct
    lined = shape((RING, SPAN, 2 * HEAD_DIM), bf16)
    both = shape((2 * SPAN, 2 * HEAD_DIM), bf16)

    def shift(array, y_step, z_step):
        moves = [
            (y * RING + z, (y + y_step) % lines * RING + (z + z_step) % RING)
            for y in range(lines)
            for z in range(RING)
        ]
        return lax.ppermute(array, "seq", moves)

    def over_lines(parts):
        got = list(parts)
        for step in (1, lines - 1, *range(2, lines - 1)):
            got[step] = shift(parts[step], step, 0)
        return got

    own = jnp.concatenate([key_rows, value_rows], axis=1)
    below, above = [own], [own]
    for _ in range(RING // 2 - 1):
        below.append(shift(below[-1], 0, 1))
        above.append(shift(above[-1], 0, -1))
    above.append(shift(above[-1], 0, -1))
    picks, table = pl.pallas_call(
        route_kernel,
        out_shape=(shape((2 * picked,), jnp.int32), shape((lines * pairs + 1,), jnp.int32)),
        in_specs=[SMEM, SMEM, SMEM],
        out_specs=(SMEM, SMEM),
        scratch_shapes=[pltpu.SMEM((2 * pairs,), jnp.int32)],
        compiler_params=params(),
        name="route",
    )(me, span_place, block_lists)
    lined_out = pl.pallas_call(
        line_kernel,
        out_shape=[lined] * lines,
        in_specs=[SMEM, SMEM] + [VMEM] * RING,
        out_specs=[VMEM] * lines,
        compiler_params=params(),
        name="line",
    )(me, table, *above, *below[:0:-1])
    got = over_lines(lined_out)
    columns = pl.pallas_call(
        columns_kernel,
        out_shape=shape((head_count, cotangent.shape[0], width), bf16),
        in_specs=[VMEM, ANY],
        out_specs=VMEM,
        compiler_params=params(),
        name="columns",
    )(cotangent, lined_out[0])
    grad_heads = lax.all_to_all(columns, "head", split_axis=0, concat_axis=0, tiled=True)
    grad_heads = grad_heads.reshape(queries.shape)

    rows_all = (picked + 1) * SPAN
    half_wide = pl.BlockSpec((SPAN, width), lambda i: (i, 0))
    half_head = pl.BlockSpec((SPAN, HEAD_DIM), lambda i: (i, 0))
    eighth = pl.BlockSpec(lined.shape, lambda i: (0, 0, 0))
    attended, query_grad, own_keys, own_values, *sent = pl.pallas_call(
        attend_kernel,
        grid=(2,),
        out_shape=[
            shape(queries.shape, bf16),
            shape(queries.shape, bf16),
            shape(key_rows.shape, f32),
            shape(key_rows.shape, f32),
        ] + [lined] * lines,
        in_specs=[SMEM, SMEM, half_wide, half_wide, half_head, half_head] + [eighth] * lines,
        out_specs=[half_wide, half_wide, half_head, half_head] + [eighth] * lines,
        scratch_shapes=[
            pltpu.VMEM((lines, *lined.shape), bf16),
            pltpu.VMEM((rows_all, HEAD_DIM), bf16),
            pltpu.VMEM((rows_all, HEAD_DIM), bf16),
            pltpu.VMEM((rows_all, width), f32),
            pltpu.VMEM((rows_all, width), bf16),
            pltpu.VMEM((rows_all, width), bf16),
        ],
        compiler_params=params(),
        name="attend",
    )(me, picks, queries, grad_heads, key_rows, value_rows, *got)

    back_line = over_lines(sent)
    attended_out = lax.all_to_all(attended, "head", split_axis=0, concat_axis=1, tiled=True)
    line_sums = pl.pallas_call(
        line_sum_kernel,
        out_shape=[both] * RING,
        in_specs=[SMEM, SMEM, ANY] + [VMEM] * lines,
        out_specs=[VMEM] * RING,
        compiler_params=params(),
        name="line_sum",
    )(me, table, attended_out, *back_line)
    back = [line_sums[0]]
    for far in (*(step for near in range(1, RING // 2) for step in (near, RING - near)), RING // 2):
        back.append(shift(line_sums[far], 0, far))
    key_grad, value_grad = pl.pallas_call(
        add_kernel,
        out_shape=(shape(key_rows.shape, bf16), shape(value_rows.shape, bf16)),
        in_specs=[VMEM] * (2 + RING),
        out_specs=(VMEM, VMEM),
        compiler_params=params(),
        name="add",
    )(own_keys, own_values, *back)
    return (attended_out, query_grad, key_grad, value_grad)


def solution(mesh):
    in_specs = (
        P("seq", "head"),
        P("seq", "head"),
        P("seq", "head"),
        P(),
        P(),
        P(("seq", "head"), None),
    )
    out_specs = (P(("seq", "head"), None), P("seq", "head"), P("seq", "head"), P("seq", "head"))
    return jax.shard_map(body, mesh=mesh, in_specs=in_specs, out_specs=out_specs, check_vma=False)
```

time: 153 us -> 117 us (0.76)
  blocking collectives: 73.1 us -> 29.4 us
  starting transfers between devices: 11.4 us -> 38.4 us
  waiting for transfers between devices: 47.9 us -> 33.1 us
  local copies, waits for them, and re-layouts: 6.85 us -> 1.7 us
    all_to_all x2 -> x0, waiting for transfers between devices: 47.9 us -> none  [the longest x1 47.9 us: body(): back = lax.all_to_all(sent, 'seq', split_axis=0, concat_axis=0, tiled=True)]
    all_to_all x1, blocking collectives: 58.1 us -> 15.7 us  [body(): lax.all_to_all(columns, 'head', split_axis=0, concat_axis=0, tiled=True)]
    ppermute x0 -> x20, starting transfers between devices: none -> 38.4 us  [shift(): return lax.ppermute(array, 'seq', moves)]
    ppermute x0 -> x20, waiting for transfers between devices: none -> 33.1 us  [shift(): return lax.ppermute(array, 'seq', moves)]
    all_to_all x2 -> x0, starting transfers between devices: 11.4 us -> none  [the longest x1 6.55 us: body(): lax.all_to_all(cotangent, 'head', split_axis=1, concat_axis=0, tiled=True)]
    unnamed x15 -> x16, local copies, waits for them, and re-layouts: 4.45 us -> 1.66 us
    all_to_all x1 -> x0, local copies, waits for them, and re-layouts: 1.67 us -> none  [body(): lax.all_to_all(cotangent, 'head', split_axis=1, concat_axis=0, tiled=True)]
    pallas_call x3 -> x6, Pallas kernels: 12.4 us -> 12.6 us  [the longest x1 7.14 us: body(): pl.pallas_call(attend_kernel, grid=(2,), out_shape=[shape(queries.shape,...]
  transfers between devices with their start and end apart: 2 -> 20, of which waited for: 1 -> 8; matrix products, arithmetic and copies ran while one was open for 1% -> 0% of each run, Pallas kernels for 3% -> 2%
where the time goes in v2:
time: 117 us; the launch traced here: 116 us
  starting transfers between devices  38.4 us (33%)
  waiting for transfers between devices  33.1 us (28%)
  blocking collectives  29.4 us (25%)
  Pallas kernels  12.6 us (11%)
  local copies, waits for them, and re-layouts  1.7 us (1%)
    ppermute x20, starting transfers between devices, shift(): return lax.ppermute(array, 'seq', moves)  38.4 us
    ppermute x20, waiting for transfers between devices, shift(): return lax.ppermute(array, 'seq', moves)  33.1 us
    all_to_all x1, blocking collectives, body(): lax.all_to_all(columns, 'head', split_axis=0, concat_axis=0, tiled=True)  15.7 us
    all_to_all x1, blocking collectives, body(): lax.all_to_all(attended, 'head', split_axis=0, concat_axis=1, tiled=True)  13.7 us
    pallas_call x1, Pallas kernels, body(): pl.pallas_call(attend_kernel, grid=(2,), out_shape=[shape(queries.shape,...  7.14 us
    pallas_call x1, Pallas kernels, body(): pl.pallas_call(route_kernel, out_shape=(shape((2 * picked,), jnp.int32),...  2.44 us
  transfers between devices with their start and end apart: 20, of which 8 were waited for; matrix products, arithmetic and copies ran while one was open for 0% of the time, Pallas kernels for 2%

profile of v2, /device:TPU:1, one launch (start us, length us, event | category | flops | bytes accessed | tf_op | source)
XLA Modules:
  0.0 116.0 jit_solution(13626347936054850537)
XLA Ops:
  0.6 0.9 constant_dynamic-update-slice_fusion.1
  1.6 0.0 copy-start.6
  1.6 6.5 %collective-permute-start = (bf16[256,256]{1,0:T(8,128)(2,1)S(1)}, bf16[256,256]{1,0:T(8,128)(2,1)S(1)}, u32[]{:S(2)}, u32[]{:S(2)}) collective-permute-start(bf16[256,256]{1,0:T(8,128)(2,1)S(1)} %constant_dynamic-update-slice_fusion.refs_0_), channel_id=1, source_target_pairs={{0,56},{8,0},{16,8},{24,16},{32,24},{40,32},{48,40},{56,48},{64,12... | collective-permute-start | bytes 393224 | tf_op jit(solution)/shard_map/ppermute | solution.py:206
  8.1 0.0 collective-permute-start.4
  8.1 2.2 %collective-permute-done.refs_1_ = bf16[256,256]{1,0:T(8,128)(2,1)S(1)} collective-permute-done((bf16[256,256]{1,0:T(8,128)(2,1)S(1)}, bf16[256,256]{1,0:T(8,128)(2,1)S(1)}, u32[]{:S(2)}, u32[]{:S(2)}) %collective-permute-start) | collective-permute-done | bytes 131104 | tf_op jit(solution)/shard_map/ppermute | solution.py:206
  10.2 3.4 %collective-permute-start.1 = (bf16[256,256]{1,0:T(8,128)(2,1)S(1)}, bf16[256,256]{1,0:T(8,128)(2,1)S(1)}, u32[]{:S(2)}, u32[]{:S(2)}) collective-permute-start(bf16[256,256]{1,0:T(8,128)(2,1)S(1)} %collective-permute-done.refs_1_), channel_id=1, source_target_pairs={{0,56},{8,0},{16,8},{24,16},{32,24},{40,32},{48,40},{56,48},{64,12... | collective-permute-start | bytes 393224 | tf_op jit(solution)/shard_map/ppermute | solution.py:206
  13.6 0.0 collective-permute-done.4.refs_7_
  13.6 0.0 collective-permute-start.5
  13.6 1.9 %collective-permute-done.1.refs_2_ = bf16[256,256]{1,0:T(8,128)(2,1)S(1)} collective-permute-done((bf16[256,256]{1,0:T(8,128)(2,1)S(1)}, bf16[256,256]{1,0:T(8,128)(2,1)S(1)}, u32[]{:S(2)}, u32[]{:S(2)}) %collective-permute-start.1) | collective-permute-done | bytes 131104 | tf_op jit(solution)/shard_map/ppermute | solution.py:206
  15.6 3.1 %collective-permute-start.2 = (bf16[256,256]{1,0:T(8,128)(2,1)S(1)}, bf16[256,256]{1,0:T(8,128)(2,1)S(1)}, u32[]{:S(2)}, u32[]{:S(2)}) collective-permute-start(bf16[256,256]{1,0:T(8,128)(2,1)S(1)} %collective-permute-done.1.refs_2_), channel_id=1, source_target_pairs={{0,56},{8,0},{16,8},{24,16},{32,24},{40,32},{48,40},{56,48},{64,12... | collective-permute-start | bytes 393224 | tf_op jit(solution)/shard_map/ppermute | solution.py:206
  18.7 0.0 collective-permute-done.5.refs_6_
  18.7 0.0 collective-permute-start.6
  18.7 1.9 %collective-permute-done.2.refs_3_ = bf16[256,256]{1,0:T(8,128)(2,1)S(1)} collective-permute-done((bf16[256,256]{1,0:T(8,128)(2,1)S(1)}, bf16[256,256]{1,0:T(8,128)(2,1)S(1)}, u32[]{:S(2)}, u32[]{:S(2)}) %collective-permute-start.2) | collective-permute-done | bytes 131104 | tf_op jit(solution)/shard_map/ppermute | solution.py:206
  20.6 3.1 %collective-permute-start.3 = (bf16[256,256]{1,0:T(8,128)(2,1)S(1)}, bf16[256,256]{1,0:T(8,128)(2,1)S(1)}, u32[]{:S(2)}, u32[]{:S(2)}) collective-permute-start(bf16[256,256]{1,0:T(8,128)(2,1)S(1)} %collective-permute-done.2.refs_3_), channel_id=1, source_target_pairs={{0,56},{8,0},{16,8},{24,16},{32,24},{40,32},{48,40},{56,48},{64,12... | collective-permute-start | bytes 393224 | tf_op jit(solution)/shard_map/ppermute | solution.py:206
  23.7 0.1 copy.12.lists_ref
  23.8 0.7 copy-done.5
  24.4 2.4 %route.1 = (s32[16]{0:T(128)S(1)}, s32[129]{0:T(256)S(1)}) custom-call(s32[1]{0:T(128)} %bitcast.me_ref, s32[64]{0:T(128)S(1)} %copy-done.5, s32[64,8]{1,0:T(8,128)S(1)} %copy.12.lists_ref), custom_call_target="tpu_custom_call" | custom-call | tf_op jit(solution)/shard_map/route/pallas_call | solution.py:220
  26.9 0.0 collective-permute-done.6.refs_5_
  26.9 0.0 collective-permute-done.3.refs_4_
  26.9 0.0 copy-start.4
  26.9 0.8 line.1
  27.8 1.4 %collective-permute-start.7 = (bf16[8,128,256]{2,1,0:T(8,128)(2,1)S(1)}, bf16[8,128,256]{2,1,0:T(8,128)(2,1)S(1)}, u32[]{:S(2)}, u32[]{:S(2)}) collective-permute-start(bf16[8,128,256]{2,1,0:T(8,128)(2,1)S(1)} %get-tuple-element.31), channel_id=1, source_target_pairs={{0,64},{8,72},{16,80},{24,88},{32,96},{40,104},{48,112},{56,120},{... | collective-permute-start | bytes 1572872 | tf_op jit(solution)/shard_map/ppermute | solution.py:206
  29.1 2.6 %collective-permute-start.8 = (bf16[8,128,256]{2,1,0:T(8,128)(2,1)S(1)}, bf16[8,128,256]{2,1,0:T(8,128)(2,1)S(1)}, u32[]{:S(2)}, u32[]{:S(2)}) collective-permute-start(bf16[8,128,256]{2,1,0:T(8,128)(2,1)S(1)} %get-tuple-element.32), channel_id=1, source_target_pairs={{0,128},{8,136},{16,144},{24,152},{32,160},{40,168},{48,176},{56,1... | collective-permute-start | bytes 1572872 | tf_op jit(solution)/shard_map/ppermute | solution.py:206
  31.8 1.1 collective-permute-start.9
  32.9 0.0 copy-start.1
  32.9 0.0 copy-start.2
  32.9 15.7 %all_to_all.24 = bf16[8,32,512]{2,1,0:T(8,128)(2,1)S(1)} all-to-all(bf16[8,32,512]{2,1,0:T(8,128)(2,1)S(1)} %columns.1), channel_id=1, replica_groups=mesh['seq'=32,'head'=8] {'head'}, dimensions={0} | all-to-all | bytes 524288 | tf_op jit(solution)/shard_map/all_to_all | solution.py:246
  48.6 0.0 collective-permute-done.7.refs_1_
  48.6 2.2 %collective-permute-done.8.refs_2_ = bf16[8,128,256]{2,1,0:T(8,128)(2,1)S(1)} collective-permute-done((bf16[8,128,256]{2,1,0:T(8,128)(2,1)S(1)}, bf16[8,128,256]{2,1,0:T(8,128)(2,1)S(1)}, u32[]{:S(2)}, u32[]{:S(2)}) %collective-permute-start.8) | collective-permute-done | bytes 524320 | tf_op jit(solution)/shard_map/ppermute | solution.py:206
  50.8 2.9 %collective-permute-done.9.refs_3_ = bf16[8,128,256]{2,1,0:T(8,128)(2,1)S(1)} collective-permute-done((bf16[8,128,256]{2,1,0:T(8,128)(2,1)S(1)}, bf16[8,128,256]{2,1,0:T(8,128)(2,1)S(1)}, u32[]{:S(2)}, u32[]{:S(2)}) %collective-permute-start.9) | collective-permute-done | bytes 524320 | tf_op jit(solution)/shard_map/ppermute | solution.py:206
  53.7 7.1 %attend.1 = (bf16[256,512]{1,0:T(8,128)(2,1)S(1)}, bf16[256,512]{1,0:T(8,128)(2,1)}, f32[256,128]{1,0:T(8,128)S(1)}, f32[256,128]{1,0:T(8,128)S(1)}, bf16[8,128,...) custom-call(s32[1]{0:T(128)} %bitcast.me_ref, ...), custom_call_target="tpu_custom_call" | custom-call | tf_op jit(solution)/shard_map/attend/pallas_call | solution.py:253
  60.8 1.8 %collective-permute-start.10 = (bf16[8,128,256]{2,1,0:T(8,128)(2,1)S(1)}, bf16[8,128,256]{2,1,0:T(8,128)(2,1)S(1)}, u32[]{:S(2)}, u32[]{:S(2)}) collective-permute-start(bf16[8,128,256]{2,1,0:T(8,128)(2,1)S(1)} %get-tuple-element.39), channel_id=1, source_target_pairs={{0,64},{8,72},{16,80},{24,88},{32,96},{40,104},{48,112},{56,120},{... | collective-permute-start | bytes 1572872 | tf_op jit(solution)/shard_map/ppermute | solution.py:206
  62.7 2.8 %collective-permute-start.11 = (bf16[8,128,256]{2,1,0:T(8,128)(2,1)S(1)}, bf16[8,128,256]{2,1,0:T(8,128)(2,1)S(1)}, u32[]{:S(2)}, u32[]{:S(2)}) collective-permute-start(bf16[8,128,256]{2,1,0:T(8,128)(2,1)S(1)} %get-tuple-element.40), channel_id=1, source_target_pairs={{0,128},{8,136},{16,144},{24,152},{32,160},{40,168},{48,176},{56,1... | collective-permute-start | bytes 1572872 | tf_op jit(solution)/shard_map/ppermute | solution.py:206
  65.4 0.0 collective-permute-start.12
  65.4 13.7 %all_to_all.25 = bf16[8,32,512]{2,1,0:T(8,128)(2,1)S(1)} all-to-all(bf16[8,32,512]{2,1,0:T(8,128)(2,1)S(1)} %bitcast.9), channel_id=1, replica_groups=mesh['seq'=32,'head'=8] {'head'}, dimensions={0} | all-to-all | bytes 524288 | tf_op jit(solution)/shard_map/all_to_all | solution.py:277
  79.1 0.0 copy-start
  79.2 8.8 %collective-permute-done.11.refs_2_ = bf16[8,128,256]{2,1,0:T(8,128)(2,1)S(1)} collective-permute-done((bf16[8,128,256]{2,1,0:T(8,128)(2,1)S(1)}, bf16[8,128,256]{2,1,0:T(8,128)(2,1)S(1)}, u32[]{:S(2)}, u32[]{:S(2)}) %collective-permute-start.11) | collective-permute-done | bytes 524320 | tf_op jit(solution)/shard_map/ppermute | solution.py:206
  88.0 1.4 %line_sum.1 = (bf16[256,256]{1,0:T(8,128)(2,1)S(1)}, bf16[256,256]{1,0:T(8,128)(2,1)S(1)}, bf16[256,256]{1,0:T(8,128)(2,1)S(1)}, bf16[256,256]{1,0:T(8,128)(2,1)...) custom-call(s32[1]{0:T(128)} %bitcast.me_ref, ...), custom_call_target="tpu_custom_call" | custom-call | tf_op jit(solution)/shard_map/line_sum/pallas_call | solution.py:278
  89.4 0.1 collective-permute-start.13
  89.5 2.7 %collective-permute-start.14 = (bf16[256,256]{1,0:T(8,128)(2,1)S(1)}, bf16[256,256]{1,0:T(8,128)(2,1)S(1)}, u32[]{:S(2)}, u32[]{:S(2)}) collective-permute-start(bf16[256,256]{1,0:T(8,128)(2,1)S(1)} %get-tuple-element.44), channel_id=1, source_target_pairs={{0,56},{8,0},{16,8},{24,16},{32,24},{40,32},{48,40},{56,48},{64,12... | collective-permute-start | bytes 393224 | tf_op jit(solution)/shard_map/ppermute | solution.py:206
  92.1 3.6 %collective-permute-start.16 = (bf16[256,256]{1,0:T(8,128)(2,1)S(1)}, bf16[256,256]{1,0:T(8,128)(2,1)S(1)}, u32[]{:S(2)}, u32[]{:S(2)}) collective-permute-start(bf16[256,256]{1,0:T(8,128)(2,1)S(1)} %get-tuple-element.46), channel_id=1, source_target_pairs={{0,48},{8,56},{16,0},{24,8},{32,16},{40,24},{48,32},{56,40},{64,11... | collective-permute-start | bytes 393224 | tf_op jit(solution)/shard_map/ppermute | solution.py:206
  95.7 4.5 %collective-permute-start.18 = (bf16[256,256]{1,0:T(8,128)(2,1)S(1)}, bf16[256,256]{1,0:T(8,128)(2,1)S(1)}, u32[]{:S(2)}, u32[]{:S(2)}) collective-permute-start(bf16[256,256]{1,0:T(8,128)(2,1)S(1)} %get-tuple-element.48), channel_id=1, source_target_pairs={{0,40},{8,48},{16,56},{24,0},{32,8},{40,16},{48,24},{56,32},{64,10... | collective-permute-start | bytes 393224 | tf_op jit(solution)/shard_map/ppermute | solution.py:206
  100.2 0.0 collective-permute-done.14.refs_2_
  100.2 1.9 %collective-permute-start.19 = (bf16[256,256]{1,0:T(8,128)(2,1)S(1)}, bf16[256,256]{1,0:T(8,128)(2,1)S(1)}, u32[]{:S(2)}, u32[]{:S(2)}) collective-permute-start(bf16[256,256]{1,0:T(8,128)(2,1)S(1)} %get-tuple-element.49), channel_id=1, source_target_pairs={{0,32},{8,40},{16,48},{24,56},{32,0},{40,8},{48,16},{56,24},{64,96... | collective-permute-start | bytes 393224 | tf_op jit(solution)/shard_map/ppermute | solution.py:206
  102.1 0.0 collective-permute-done.15.refs_3_
  102.1 4.5 %collective-permute-done.17.refs_5_ = bf16[256,256]{1,0:T(8,128)(2,1)S(1)} collective-permute-done((bf16[256,256]{1,0:T(8,128)(2,1)S(1)}, bf16[256,256]{1,0:T(8,128)(2,1)S(1)}, u32[]{:S(2)}, u32[]{:S(2)}) %collective-permute-start.17) | collective-permute-done | bytes 131104 | tf_op jit(solution)/shard_map/ppermute | solution.py:206
  106.6 8.6 %collective-permute-done.18.refs_6_ = bf16[256,256]{1,0:T(8,128)(2,1)S(1)} collective-permute-done((bf16[256,256]{1,0:T(8,128)(2,1)S(1)}, bf16[256,256]{1,0:T(8,128)(2,1)S(1)}, u32[]{:S(2)}, u32[]{:S(2)}) %collective-permute-start.18) | collective-permute-done | bytes 131104 | tf_op jit(solution)/shard_map/ppermute | solution.py:206
  115.2 0.8 add.1
  (18 shorter events, 0.1 us)
Async XLA Ops:
  0.6 0.9 copy-start.3
  1.6 22.1 %copy-start.6 = (s32[64,8]{0,1:T(8,128)S(1)}, s32[64,8]{0,1:T(8,128)}, u32[]{:S(2)}) copy-start(s32[64,8]{0,1:T(8,128)} %param.10) | copy-start | bytes 6148
  1.6 8.6 %collective-permute-start = (bf16[256,256]{1,0:T(8,128)(2,1)S(1)}, bf16[256,256]{1,0:T(8,128)(2,1)S(1)}, u32[]{:S(2)}, u32[]{:S(2)}) collective-permute-start(bf16[256,256]{1,0:T(8,128)(2,1)S(1)} %constant_dynamic-update-slice_fusion.refs_0_), channel_id=1, source_target_pairs={{0,56},{8,0},{16,8},{24,16},{32,24},{40,32},{48,40},{56,48},{64,12... | collective-permute-start | bytes 393224 | tf_op jit(solution)/shard_map/ppermute | solution.py:206
  8.1 5.6 %collective-permute-start.4 = (bf16[256,256]{1,0:T(8,128)(2,1)S(1)}, bf16[256,256]{1,0:T(8,128)(2,1)S(1)}, u32[]{:S(2)}, u32[]{:S(2)}) collective-permute-start(bf16[256,256]{1,0:T(8,128)(2,1)S(1)} %constant_dynamic-update-slice_fusion.refs_0_), channel_id=1, source_target_pairs={{0,8},{8,16},{16,24},{24,32},{32,40},{40,48},{48,56},{56,0},{64,72... | collective-permute-start | bytes 393224 | tf_op jit(solution)/shard_map/ppermute | solution.py:206
  10.2 5.4 %collective-permute-start.1 = (bf16[256,256]{1,0:T(8,128)(2,1)S(1)}, bf16[256,256]{1,0:T(8,128)(2,1)S(1)}, u32[]{:S(2)}, u32[]{:S(2)}) collective-permute-start(bf16[256,256]{1,0:T(8,128)(2,1)S(1)} %collective-permute-done.refs_1_), channel_id=1, source_target_pairs={{0,56},{8,0},{16,8},{24,16},{32,24},{40,32},{48,40},{56,48},{64,12... | collective-permute-start | bytes 393224 | tf_op jit(solution)/shard_map/ppermute | solution.py:206
  13.6 5.0 %collective-permute-start.5 = (bf16[256,256]{1,0:T(8,128)(2,1)S(1)}, bf16[256,256]{1,0:T(8,128)(2,1)S(1)}, u32[]{:S(2)}, u32[]{:S(2)}) collective-permute-start(bf16[256,256]{1,0:T(8,128)(2,1)S(1)} %collective-permute-done.4.refs_7_), channel_id=1, source_target_pairs={{0,8},{8,16},{16,24},{24,32},{32,40},{40,48},{48,56},{56,0},{64,72... | collective-permute-start | bytes 393224 | tf_op jit(solution)/shard_map/ppermute | solution.py:206
  15.6 5.0 %collective-permute-start.2 = (bf16[256,256]{1,0:T(8,128)(2,1)S(1)}, bf16[256,256]{1,0:T(8,128)(2,1)S(1)}, u32[]{:S(2)}, u32[]{:S(2)}) collective-permute-start(bf16[256,256]{1,0:T(8,128)(2,1)S(1)} %collective-permute-done.1.refs_2_), channel_id=1, source_target_pairs={{0,56},{8,0},{16,8},{24,16},{32,24},{40,32},{48,40},{56,48},{64,12... | collective-permute-start | bytes 393224 | tf_op jit(solution)/shard_map/ppermute | solution.py:206
  18.7 8.2 %collective-permute-start.6 = (bf16[256,256]{1,0:T(8,128)(2,1)S(1)}, bf16[256,256]{1,0:T(8,128)(2,1)S(1)}, u32[]{:S(2)}, u32[]{:S(2)}) collective-permute-start(bf16[256,256]{1,0:T(8,128)(2,1)S(1)} %collective-permute-done.5.refs_6_), channel_id=1, source_target_pairs={{0,8},{8,16},{16,24},{24,32},{32,40},{40,48},{48,56},{56,0},{64,72... | collective-permute-start | bytes 393224 | tf_op jit(solution)/shard_map/ppermute | solution.py:206
  20.6 6.3 %collective-permute-start.3 = (bf16[256,256]{1,0:T(8,128)(2,1)S(1)}, bf16[256,256]{1,0:T(8,128)(2,1)S(1)}, u32[]{:S(2)}, u32[]{:S(2)}) collective-permute-start(bf16[256,256]{1,0:T(8,128)(2,1)S(1)} %collective-permute-done.2.refs_3_), channel_id=1, source_target_pairs={{0,56},{8,0},{16,8},{24,16},{32,24},{40,32},{48,40},{56,48},{64,12... | collective-permute-start | bytes 393224 | tf_op jit(solution)/shard_map/ppermute | solution.py:206
  23.8 0.7 copy-start.5
  26.9 5.9 %copy-start.4 = (bf16[32,4096]{1,0:T(8,128)(2,1)S(1)}, bf16[32,4096]{1,0:T(8,128)(2,1)}, u32[]{:S(2)}) copy-start(bf16[32,4096]{1,0:T(8,128)(2,1)} %cot_ref.1) | copy-start | bytes 786436
  27.8 20.8 %collective-permute-start.7 = (bf16[8,128,256]{2,1,0:T(8,128)(2,1)S(1)}, bf16[8,128,256]{2,1,0:T(8,128)(2,1)S(1)}, u32[]{:S(2)}, u32[]{:S(2)}) collective-permute-start(bf16[8,128,256]{2,1,0:T(8,128)(2,1)S(1)} %get-tuple-element.31), channel_id=1, source_target_pairs={{0,64},{8,72},{16,80},{24,88},{32,96},{40,104},{48,112},{56,120},{... | collective-permute-start | bytes 1572872 | tf_op jit(solution)/shard_map/ppermute | solution.py:206
  29.1 21.7 %collective-permute-start.8 = (bf16[8,128,256]{2,1,0:T(8,128)(2,1)S(1)}, bf16[8,128,256]{2,1,0:T(8,128)(2,1)S(1)}, u32[]{:S(2)}, u32[]{:S(2)}) collective-permute-start(bf16[8,128,256]{2,1,0:T(8,128)(2,1)S(1)} %get-tuple-element.32), channel_id=1, source_target_pairs={{0,128},{8,136},{16,144},{24,152},{32,160},{40,168},{48,176},{56,1... | collective-permute-start | bytes 1572872 | tf_op jit(solution)/shard_map/ppermute | solution.py:206
  31.8 21.9 %collective-permute-start.9 = (bf16[8,128,256]{2,1,0:T(8,128)(2,1)S(1)}, bf16[8,128,256]{2,1,0:T(8,128)(2,1)S(1)}, u32[]{:S(2)}, u32[]{:S(2)}) collective-permute-start(bf16[8,128,256]{2,1,0:T(8,128)(2,1)S(1)} %get-tuple-element.33), channel_id=1, source_target_pairs={{0,192},{8,200},{16,208},{24,216},{32,224},{40,232},{48,240},{56,2... | collective-permute-start | bytes 1572872 | tf_op jit(solution)/shard_map/ppermute | solution.py:206
  32.9 20.8 %copy-start.1 = (bf16[256,512]{1,0:T(8,128)(2,1)S(1)}, bf16[256,512]{1,0:T(8,128)(2,1)}, u32[]{:S(2)}) copy-start(bf16[256,512]{1,0:T(8,128)(2,1)} %q_ref.1) | copy-start | bytes 786436
  32.9 20.8 %copy-start.2 = (bf16[256,128]{1,0:T(8,128)(2,1)S(1)}, bf16[256,128]{1,0:T(8,128)(2,1)}, u32[]{:S(2)}) copy-start(bf16[256,128]{1,0:T(8,128)(2,1)} %k_ref.1) | copy-start | bytes 196612
  60.8 18.3 %collective-permute-start.10 = (bf16[8,128,256]{2,1,0:T(8,128)(2,1)S(1)}, bf16[8,128,256]{2,1,0:T(8,128)(2,1)S(1)}, u32[]{:S(2)}, u32[]{:S(2)}) collective-permute-start(bf16[8,128,256]{2,1,0:T(8,128)(2,1)S(1)} %get-tuple-element.39), channel_id=1, source_target_pairs={{0,64},{8,72},{16,80},{24,88},{32,96},{40,104},{48,112},{56,120},{... | collective-permute-start | bytes 1572872 | tf_op jit(solution)/shard_map/ppermute | solution.py:206
  62.7 25.3 %collective-permute-start.11 = (bf16[8,128,256]{2,1,0:T(8,128)(2,1)S(1)}, bf16[8,128,256]{2,1,0:T(8,128)(2,1)S(1)}, u32[]{:S(2)}, u32[]{:S(2)}) collective-permute-start(bf16[8,128,256]{2,1,0:T(8,128)(2,1)S(1)} %get-tuple-element.40), channel_id=1, source_target_pairs={{0,128},{8,136},{16,144},{24,152},{32,160},{40,168},{48,176},{56,1... | collective-permute-start | bytes 1572872 | tf_op jit(solution)/shard_map/ppermute | solution.py:206
  65.4 22.6 %collective-permute-start.12 = (bf16[8,128,256]{2,1,0:T(8,128)(2,1)S(1)}, bf16[8,128,256]{2,1,0:T(8,128)(2,1)S(1)}, u32[]{:S(2)}, u32[]{:S(2)}) collective-permute-start(bf16[8,128,256]{2,1,0:T(8,128)(2,1)S(1)} %get-tuple-element.41), channel_id=1, source_target_pairs={{0,192},{8,200},{16,208},{24,216},{32,224},{40,232},{48,240},{56,2... | collective-permute-start | bytes 1572872 | tf_op jit(solution)/shard_map/ppermute | solution.py:206
  79.1 10.2 %copy-start = (bf16[8,4,8,512]{3,2,0,1:T(8,128)(2,1)}, bf16[8,4,8,512]{3,2,0,1:T(8,128)(2,1)S(1)}, u32[]{:S(2)}) copy-start(bf16[8,4,8,512]{3,2,0,1:T(8,128)(2,1)S(1)} %copy.14) | copy-start | bytes 786436
  89.4 6.3 %collective-permute-start.13 = (bf16[256,256]{1,0:T(8,128)(2,1)S(1)}, bf16[256,256]{1,0:T(8,128)(2,1)S(1)}, u32[]{:S(2)}, u32[]{:S(2)}) collective-permute-start(bf16[256,256]{1,0:T(8,128)(2,1)S(1)} %get-tuple-element.43), channel_id=1, source_target_pairs={{0,8},{8,16},{16,24},{24,32},{32,40},{40,48},{48,56},{56,0},{64,72... | collective-permute-start | bytes 393224 | tf_op jit(solution)/shard_map/ppermute | solution.py:206
  89.5 10.7 %collective-permute-start.14 = (bf16[256,256]{1,0:T(8,128)(2,1)S(1)}, bf16[256,256]{1,0:T(8,128)(2,1)S(1)}, u32[]{:S(2)}, u32[]{:S(2)}) collective-permute-start(bf16[256,256]{1,0:T(8,128)(2,1)S(1)} %get-tuple-element.44), channel_id=1, source_target_pairs={{0,56},{8,0},{16,8},{24,16},{32,24},{40,32},{48,40},{56,48},{64,12... | collective-permute-start | bytes 393224 | tf_op jit(solution)/shard_map/ppermute | solution.py:206
  92.1 10.0 %collective-permute-start.15 = (bf16[256,256]{1,0:T(8,128)(2,1)S(1)}, bf16[256,256]{1,0:T(8,128)(2,1)S(1)}, u32[]{:S(2)}, u32[]{:S(2)}) collective-permute-start(bf16[256,256]{1,0:T(8,128)(2,1)S(1)} %get-tuple-element.45), channel_id=1, source_target_pairs={{0,16},{8,24},{16,32},{24,40},{32,48},{40,56},{48,0},{56,8},{64,80... | collective-permute-start | bytes 393224 | tf_op jit(solution)/shard_map/ppermute | solution.py:206
  92.1 10.0 %collective-permute-start.16 = (bf16[256,256]{1,0:T(8,128)(2,1)S(1)}, bf16[256,256]{1,0:T(8,128)(2,1)S(1)}, u32[]{:S(2)}, u32[]{:S(2)}) collective-permute-start(bf16[256,256]{1,0:T(8,128)(2,1)S(1)} %get-tuple-element.46), channel_id=1, source_target_pairs={{0,48},{8,56},{16,0},{24,8},{32,16},{40,24},{48,32},{56,40},{64,11... | collective-permute-start | bytes 393224 | tf_op jit(solution)/shard_map/ppermute | solution.py:206
  95.7 10.9 %collective-permute-start.17 = (bf16[256,256]{1,0:T(8,128)(2,1)S(1)}, bf16[256,256]{1,0:T(8,128)(2,1)S(1)}, u32[]{:S(2)}, u32[]{:S(2)}) collective-permute-start(bf16[256,256]{1,0:T(8,128)(2,1)S(1)} %get-tuple-element.47), channel_id=1, source_target_pairs={{0,24},{8,32},{16,40},{24,48},{32,56},{40,0},{48,8},{56,16},{64,88... | collective-permute-start | bytes 393224 | tf_op jit(solution)/shard_map/ppermute | solution.py:206
  95.7 19.5 %collective-permute-start.18 = (bf16[256,256]{1,0:T(8,128)(2,1)S(1)}, bf16[256,256]{1,0:T(8,128)(2,1)S(1)}, u32[]{:S(2)}, u32[]{:S(2)}) collective-permute-start(bf16[256,256]{1,0:T(8,128)(2,1)S(1)} %get-tuple-element.48), channel_id=1, source_target_pairs={{0,40},{8,48},{16,56},{24,0},{32,8},{40,16},{48,24},{56,32},{64,10... | collective-permute-start | bytes 393224 | tf_op jit(solution)/shard_map/ppermute | solution.py:206
  100.2 15.0 %collective-permute-start.19 = (bf16[256,256]{1,0:T(8,128)(2,1)S(1)}, bf16[256,256]{1,0:T(8,128)(2,1)S(1)}, u32[]{:S(2)}, u32[]{:S(2)}) collective-permute-start(bf16[256,256]{1,0:T(8,128)(2,1)S(1)} %get-tuple-element.49), channel_id=1, source_target_pairs={{0,32},{8,40},{16,48},{24,56},{32,0},{40,8},{48,16},{56,24},{64,96... | collective-permute-start | bytes 393224 | tf_op jit(solution)/shard_map/ppermute | solution.py:206

commit v3 on v2

--- a/solution.py
+++ b/solution.py
@@ -1,3 +1,4 @@
+import functools
 import math
 
 import jax
@@ -11,6 +12,7 @@
 SPAN = 128
 RING = 8
 HIDDEN = -1.0e30
+GROUPS = ((3, 5, 2, 6), (4, 1, 7, 0))
 SCALE = 1.0 / math.sqrt(HEAD_DIM)
 SMEM = pl.BlockSpec(memory_space=pltpu.SMEM)
 VMEM = pl.BlockSpec(memory_space=pltpu.VMEM)
@@ -87,11 +89,11 @@
 
 
 def attend_kernel(me_ref, picks_ref, q_ref, g_ref, k_ref, v_ref, *refs):
-    lines = (len(refs) - 10) // 2
+    lines = (len(refs) - 10) // (1 + len(GROUPS))
     got, (out_ref, dq_ref, ownk_ref, ownv_ref), sent = refs[:lines], refs[lines:lines + 4], refs[lines + 4:-6]
     pool, keys, values, scores, weights, slopes = refs[-6:]
     slot = pl.program_id(0)
-    mine = me_ref[0] // RING
+    mine, at = me_ref[0] // RING, me_ref[0] % RING
     picked = picks_ref.shape[0] // 2
     owners = [picks_ref[slot * picked + j] for j in range(picked)]
 
@@ -151,25 +153,34 @@
     for j, owner in enumerate(owners):
         step = (jnp.maximum(owner, 0) // RING - mine + lines) % lines
         rows = slice((j + 1) * SPAN, (j + 2) * SPAN)
-        for far in range(lines):
-            @pl.when((owner >= 0) & (step == far))
-            def _():
-                sent[far][owner % RING, :, :HEAD_DIM] = key_part[rows].astype(bf16)
-                sent[far][owner % RING, :, HEAD_DIM:] = value_part[rows].astype(bf16)
-
-
-def line_sum_kernel(me_ref, table_ref, after_ref, *refs):
-    backs, outs = refs[:-RING], refs[-RING:]
-    lines = len(backs)
+        far = (owner % RING - at + RING) % RING
+        for index, group in enumerate(GROUPS):
+            inside, place = jnp.bool_(False), jnp.int32(0)
+            for entry, member in enumerate(group):
+                inside = inside | (far == member)
+                place = jnp.where(far == member, entry, place)
+            for line in range(lines):
+                @pl.when((owner >= 0) & inside & (step == line))
+                def _():
+                    ref = sent[index * lines + line]
+                    ref[place, :, :HEAD_DIM] = key_part[rows].astype(bf16)
+                    ref[place, :, HEAD_DIM:] = value_part[rows].astype(bf16)
+
+
+def line_sum_kernel(group, passed, me_ref, table_ref, *refs):
+    refs = refs[:len(refs) - passed]
+    outs = refs[-len(group):]
+    lines = math.isqrt((table_ref.shape[0] - 1) // RING)
+    backs = refs[-len(group) - lines:-len(group)]
     pairs = lines * RING
     me = me_ref[0]
     mine, at = me // RING, me % RING
-    for shift, out in enumerate(outs):
-        owner = (at + shift) % RING
+    for entry, (far, out) in enumerate(zip(group, outs)):
+        owner = (at + far) % RING
         halves = [
             table_ref[(mine - step + lines) % lines * pairs + mine * RING + owner] for step in range(lines)
         ]
-        parts = [back[owner].astype(f32) for back in backs]
+        parts = [back[entry].astype(f32) for back in backs]
         for side in range(2):
             total = jnp.zeros((SPAN, 2 * HEAD_DIM), f32)
             for half, part in zip(halves, parts):
@@ -258,9 +269,10 @@
             shape(queries.shape, bf16),
             shape(key_rows.shape, f32),
             shape(key_rows.shape, f32),
-        ] + [lined] * lines,
+        ] + [shape((len(group), *lined.shape[1:]), bf16) for group in GROUPS for _ in range(lines)],
         in_specs=[SMEM, SMEM, half_wide, half_wide, half_head, half_head] + [eighth] * lines,
-        out_specs=[half_wide, half_wide, half_head, half_head] + [eighth] * lines,
+        out_specs=[half_wide, half_wide, half_head, half_head]
+        + [pl.BlockSpec((len(group), *lined.shape[1:]), lambda i: (0, 0, 0)) for group in GROUPS for _ in range(lines)],
         scratch_shapes=[
             pltpu.VMEM((lines, *lined.shape), bf16),
             pltpu.VMEM((rows_all, HEAD_DIM), bf16),
@@ -273,19 +285,23 @@
         name="attend",
     )(me, picks, queries, grad_heads, key_rows, value_rows, *got)
 
-    back_line = over_lines(sent)
     attended_out = lax.all_to_all(attended, "head", split_axis=0, concat_axis=1, tiled=True)
-    line_sums = pl.pallas_call(
-        line_sum_kernel,
-        out_shape=[both] * RING,
-        in_specs=[SMEM, SMEM, ANY] + [VMEM] * lines,
-        out_specs=[VMEM] * RING,
-        compiler_params=params(),
-        name="line_sum",
-    )(me, table, attended_out, *back_line)
-    back = [line_sums[0]]
-    for far in (*(step for near in range(1, RING // 2) for step in (near, RING - near)), RING // 2):
-        back.append(shift(line_sums[far], 0, far))
+    back = []
+    for index, group in enumerate(GROUPS):
+        after = [attended_out] if index == 0 else []
+        later = sent[(index + 1) * lines:]
+        first = 2 + len(after)
+        sums = pl.pallas_call(
+            functools.partial(line_sum_kernel, group, len(later)),
+            out_shape=[both] * len(group) + [shape(part.shape, bf16) for part in later],
+            in_specs=[SMEM, SMEM] + [ANY] * (len(after) + len(later)) + [VMEM] * lines,
+            out_specs=[VMEM] * len(group) + [ANY] * len(later),
+            input_output_aliases={first + i: len(group) + i for i in range(len(later))},
+            compiler_params=params(),
+            name="line_sum",
+        )(me, table, *after, *later, *over_lines(sent[index * lines:(index + 1) * lines]))
+        sent[(index + 1) * lines:] = sums[len(group):]
+        back += [shift(part, 0, far) if far else part for far, part in zip(group, sums)]
     key_grad, value_grad = pl.pallas_call(
         add_kernel,
         out_shape=(shape(key_rows.shape, bf16), shape(value_rows.shape, bf16)),

time: 117 us -> 111 us (0.949)
  waiting for transfers between devices: 33.1 us -> 28 us
    ppermute x20 -> x23, waiting for transfers between devices: 33.1 us -> 28 us  [shift(): return lax.ppermute(array, 'seq', moves)]
    ppermute x20 -> x23, starting transfers between devices: 38.4 us -> 37.3 us  [shift(): return lax.ppermute(array, 'seq', moves)]
  transfers between devices with their start and end apart: 20 -> 23, of which waited for: 8 -> 12; matrix products, arithmetic and copies ran while one was open for 0% -> 0% of each run, Pallas kernels for 2% -> 3%
where the time goes in v3:
time: 111 us; the launch traced here: 110 us
  starting transfers between devices  37.3 us (34%)
  blocking collectives  29.1 us (26%)
  waiting for transfers between devices  28 us (25%)
  Pallas kernels  13.7 us (12%)
  local copies, waits for them, and re-layouts  1.7 us (2%)
    ppermute x23, starting transfers between devices, shift(): return lax.ppermute(array, 'seq', moves)  37.3 us
    ppermute x23, waiting for transfers between devices, shift(): return lax.ppermute(array, 'seq', moves)  28 us
    all_to_all x1, blocking collectives, body(): lax.all_to_all(columns, 'head', split_axis=0, concat_axis=0, tiled=True)  15.7 us
    all_to_all x1, blocking collectives, body(): lax.all_to_all(attended, 'head', split_axis=0, concat_axis=1, tiled=True)  13.4 us
    pallas_call x1, Pallas kernels, body(): pl.pallas_call(attend_kernel, grid=(2,), out_shape=[shape(queries.shape,...  7.63 us
    pallas_call x1, Pallas kernels, body(): pl.pallas_call(route_kernel, out_shape=(shape((2 * picked,), jnp.int32),...  2.44 us
  transfers between devices with their start and end apart: 23, of which 12 were waited for; matrix products, arithmetic and copies ran while one was open for 0% of the time, Pallas kernels for 3%

profile of v3, /device:TPU:1, one launch (start us, length us, event | category | flops | bytes accessed | tf_op | source)
XLA Modules:
  0.0 110.5 jit_solution(11878526061357572427)
XLA Ops:
  0.6 0.9 constant_dynamic-update-slice_fusion.1
  1.6 0.0 copy-start.6
  1.6 6.5 %collective-permute-start = (bf16[256,256]{1,0:T(8,128)(2,1)S(1)}, bf16[256,256]{1,0:T(8,128)(2,1)S(1)}, u32[]{:S(2)}, u32[]{:S(2)}) collective-permute-start(bf16[256,256]{1,0:T(8,128)(2,1)S(1)} %constant_dynamic-update-slice_fusion.refs_0_), channel_id=1, source_target_pairs={{0,56},{8,0},{16,8},{24,16},{32,24},{40,32},{48,40},{56,48},{64,12... | collective-permute-start | bytes 393224 | tf_op jit(solution)/shard_map/ppermute | solution.py:217
  8.1 0.0 collective-permute-start.4
  8.1 2.2 %collective-permute-done.refs_1_ = bf16[256,256]{1,0:T(8,128)(2,1)S(1)} collective-permute-done((bf16[256,256]{1,0:T(8,128)(2,1)S(1)}, bf16[256,256]{1,0:T(8,128)(2,1)S(1)}, u32[]{:S(2)}, u32[]{:S(2)}) %collective-permute-start) | collective-permute-done | bytes 131104 | tf_op jit(solution)/shard_map/ppermute | solution.py:217
  10.2 3.4 %collective-permute-start.1 = (bf16[256,256]{1,0:T(8,128)(2,1)S(1)}, bf16[256,256]{1,0:T(8,128)(2,1)S(1)}, u32[]{:S(2)}, u32[]{:S(2)}) collective-permute-start(bf16[256,256]{1,0:T(8,128)(2,1)S(1)} %collective-permute-done.refs_1_), channel_id=1, source_target_pairs={{0,56},{8,0},{16,8},{24,16},{32,24},{40,32},{48,40},{56,48},{64,12... | collective-permute-start | bytes 393224 | tf_op jit(solution)/shard_map/ppermute | solution.py:217
  13.6 1.9 %collective-permute-done.1.refs_2_ = bf16[256,256]{1,0:T(8,128)(2,1)S(1)} collective-permute-done((bf16[256,256]{1,0:T(8,128)(2,1)S(1)}, bf16[256,256]{1,0:T(8,128)(2,1)S(1)}, u32[]{:S(2)}, u32[]{:S(2)}) %collective-permute-start.1) | collective-permute-done | bytes 131104 | tf_op jit(solution)/shard_map/ppermute | solution.py:217
  15.6 3.1 %collective-permute-start.2 = (bf16[256,256]{1,0:T(8,128)(2,1)S(1)}, bf16[256,256]{1,0:T(8,128)(2,1)S(1)}, u32[]{:S(2)}, u32[]{:S(2)}) collective-permute-start(bf16[256,256]{1,0:T(8,128)(2,1)S(1)} %collective-permute-done.1.refs_2_), channel_id=1, source_target_pairs={{0,56},{8,0},{16,8},{24,16},{32,24},{40,32},{48,40},{56,48},{64,12... | collective-permute-start | bytes 393224 | tf_op jit(solution)/shard_map/ppermute | solution.py:217
  18.7 0.0 collective-permute-done.5.refs_6_
  18.7 1.9 %collective-permute-done.2.refs_3_ = bf16[256,256]{1,0:T(8,128)(2,1)S(1)} collective-permute-done((bf16[256,256]{1,0:T(8,128)(2,1)S(1)}, bf16[256,256]{1,0:T(8,128)(2,1)S(1)}, u32[]{:S(2)}, u32[]{:S(2)}) %collective-permute-start.2) | collective-permute-done | bytes 131104 | tf_op jit(solution)/shard_map/ppermute | solution.py:217
  20.6 3.1 %collective-permute-start.3 = (bf16[256,256]{1,0:T(8,128)(2,1)S(1)}, bf16[256,256]{1,0:T(8,128)(2,1)S(1)}, u32[]{:S(2)}, u32[]{:S(2)}) collective-permute-start(bf16[256,256]{1,0:T(8,128)(2,1)S(1)} %collective-permute-done.2.refs_3_), channel_id=1, source_target_pairs={{0,56},{8,0},{16,8},{24,16},{32,24},{40,32},{48,40},{56,48},{64,12... | collective-permute-start | bytes 393224 | tf_op jit(solution)/shard_map/ppermute | solution.py:217
  23.7 0.1 copy.16.lists_ref
  23.8 0.7 copy-done.5
  24.4 2.4 %route.1 = (s32[16]{0:T(128)S(1)}, s32[129]{0:T(256)S(1)}) custom-call(s32[1]{0:T(128)} %bitcast.me_ref, s32[64]{0:T(128)S(1)} %copy-done.5, s32[64,8]{1,0:T(8,128)S(1)} %copy.16.lists_ref), custom_call_target="tpu_custom_call" | custom-call | tf_op jit(solution)/shard_map/route/pallas_call | solution.py:231
  26.9 0.0 collective-permute-done.6.refs_5_
  26.9 0.0 copy-start.4
  26.9 0.8 line.1
  27.8 1.4 %collective-permute-start.7 = (bf16[8,128,256]{2,1,0:T(8,128)(2,1)S(1)}, bf16[8,128,256]{2,1,0:T(8,128)(2,1)S(1)}, u32[]{:S(2)}, u32[]{:S(2)}) collective-permute-start(bf16[8,128,256]{2,1,0:T(8,128)(2,1)S(1)} %get-tuple-element.39), channel_id=1, source_target_pairs={{0,64},{8,72},{16,80},{24,88},{32,96},{40,104},{48,112},{56,120},{... | collective-permute-start | bytes 1572872 | tf_op jit(solution)/shard_map/ppermute | solution.py:217
  29.1 2.6 %collective-permute-start.8 = (bf16[8,128,256]{2,1,0:T(8,128)(2,1)S(1)}, bf16[8,128,256]{2,1,0:T(8,128)(2,1)S(1)}, u32[]{:S(2)}, u32[]{:S(2)}) collective-permute-start(bf16[8,128,256]{2,1,0:T(8,128)(2,1)S(1)} %get-tuple-element.40), channel_id=1, source_target_pairs={{0,128},{8,136},{16,144},{24,152},{32,160},{40,168},{48,176},{56,1... | collective-permute-start | bytes 1572872 | tf_op jit(solution)/shard_map/ppermute | solution.py:217
  31.8 1.1 collective-permute-start.9
  32.9 0.0 copy-start.1
  32.9 0.0 copy-start.2
  32.9 15.7 %all_to_all.24 = bf16[8,32,512]{2,1,0:T(8,128)(2,1)S(1)} all-to-all(bf16[8,32,512]{2,1,0:T(8,128)(2,1)S(1)} %columns.1), channel_id=1, replica_groups=mesh['seq'=32,'head'=8] {'head'}, dimensions={0} | all-to-all | bytes 524288 | tf_op jit(solution)/shard_map/all_to_all | solution.py:257
  48.6 2.2 %collective-permute-done.8.refs_2_ = bf16[8,128,256]{2,1,0:T(8,128)(2,1)S(1)} collective-permute-done((bf16[8,128,256]{2,1,0:T(8,128)(2,1)S(1)}, bf16[8,128,256]{2,1,0:T(8,128)(2,1)S(1)}, u32[]{:S(2)}, u32[]{:S(2)}) %collective-permute-start.8) | collective-permute-done | bytes 524320 | tf_op jit(solution)/shard_map/ppermute | solution.py:217
  50.8 2.9 %collective-permute-done.9.refs_3_ = bf16[8,128,256]{2,1,0:T(8,128)(2,1)S(1)} collective-permute-done((bf16[8,128,256]{2,1,0:T(8,128)(2,1)S(1)}, bf16[8,128,256]{2,1,0:T(8,128)(2,1)S(1)}, u32[]{:S(2)}, u32[]{:S(2)}) %collective-permute-start.9) | collective-permute-done | bytes 524320 | tf_op jit(solution)/shard_map/ppermute | solution.py:217
  53.7 7.6 %attend.1 = (bf16[256,512]{1,0:T(8,128)(2,1)S(1)}, bf16[256,512]{1,0:T(8,128)(2,1)}, f32[256,128]{1,0:T(8,128)S(1)}, f32[256,128]{1,0:T(8,128)S(1)}, bf16[4,128,...) custom-call(s32[1]{0:T(128)} %bitcast.me_ref, ...), custom_call_target="tpu_custom_call" | custom-call | tf_op jit(solution)/shard_map/attend/pallas_call | solution.py:264
  61.3 1.9 %collective-permute-start.10 = (bf16[4,128,256]{2,1,0:T(8,128)(2,1)S(1)}, bf16[4,128,256]{2,1,0:T(8,128)(2,1)S(1)}, u32[]{:S(2)}, u32[]{:S(2)}) collective-permute-start(bf16[4,128,256]{2,1,0:T(8,128)(2,1)S(1)} %get-tuple-element.51), channel_id=1, source_target_pairs={{0,64},{8,72},{16,80},{24,88},{32,96},{40,104},{48,112},{56,120},{... | collective-permute-start | bytes 786440 | tf_op jit(solution)/shard_map/ppermute | solution.py:217
  63.2 2.7 %collective-permute-start.11 = (bf16[4,128,256]{2,1,0:T(8,128)(2,1)S(1)}, bf16[4,128,256]{2,1,0:T(8,128)(2,1)S(1)}, u32[]{:S(2)}, u32[]{:S(2)}) collective-permute-start(bf16[4,128,256]{2,1,0:T(8,128)(2,1)S(1)} %get-tuple-element.52), channel_id=1, source_target_pairs={{0,128},{8,136},{16,144},{24,152},{32,160},{40,168},{48,176},{56,1... | collective-permute-start | bytes 786440 | tf_op jit(solution)/shard_map/ppermute | solution.py:217
  65.9 13.4 %all_to_all.25 = bf16[8,32,512]{2,1,0:T(8,128)(2,1)S(1)} all-to-all(bf16[8,32,512]{2,1,0:T(8,128)(2,1)S(1)} %bitcast.9), channel_id=1, replica_groups=mesh['seq'=32,'head'=8] {'head'}, dimensions={0} | all-to-all | bytes 524288 | tf_op jit(solution)/shard_map/all_to_all | solution.py:288
  79.3 0.0 copy-start
  79.3 1.0 line_sum.2
  80.3 0.3 collective-permute-start.17
  80.6 1.5 %collective-permute-start.18 = (bf16[4,128,256]{2,1,0:T(8,128)(2,1)S(1)}, bf16[4,128,256]{2,1,0:T(8,128)(2,1)S(1)}, u32[]{:S(2)}, u32[]{:S(2)}) collective-permute-start(bf16[4,128,256]{2,1,0:T(8,128)(2,1)S(1)} %get-tuple-element.60), channel_id=1, source_target_pairs={{0,128},{8,136},{16,144},{24,152},{32,160},{40,168},{48,176},{56,1... | collective-permute-start | bytes 786440 | tf_op jit(solution)/shard_map/ppermute | solution.py:217
  82.1 1.2 %collective-permute-start.19 = (bf16[4,128,256]{2,1,0:T(8,128)(2,1)S(1)}, bf16[4,128,256]{2,1,0:T(8,128)(2,1)S(1)}, u32[]{:S(2)}, u32[]{:S(2)}) collective-permute-start(bf16[4,128,256]{2,1,0:T(8,128)(2,1)S(1)} %get-tuple-element.61), channel_id=1, source_target_pairs={{0,192},{8,200},{16,208},{24,216},{32,224},{40,232},{48,240},{56,2... | collective-permute-start | bytes 786440 | tf_op jit(solution)/shard_map/ppermute | solution.py:217
  83.2 0.9 collective-permute-start.13
  84.2 3.6 %collective-permute-start.14 = (bf16[256,256]{1,0:T(8,128)(2,1)S(1)}, bf16[256,256]{1,0:T(8,128)(2,1)S(1)}, u32[]{:S(2)}, u32[]{:S(2)}) collective-permute-start(bf16[256,256]{1,0:T(8,128)(2,1)S(1)} %get-tuple-element.55), channel_id=1, source_target_pairs={{0,40},{8,48},{16,56},{24,0},{32,8},{40,16},{48,24},{56,32},{64,10... | collective-permute-start | bytes 393224 | tf_op jit(solution)/shard_map/ppermute | solution.py:217
  87.7 1.3 %collective-permute-done.17.refs_1_ = bf16[4,128,256]{2,1,0:T(8,128)(2,1)S(1)} collective-permute-done((bf16[4,128,256]{2,1,0:T(8,128)(2,1)S(1)}, bf16[4,128,256]{2,1,0:T(8,128)(2,1)S(1)}, u32[]{:S(2)}, u32[]{:S(2)}) %collective-permute-start.17) | collective-permute-done | bytes 262176 | tf_op jit(solution)/shard_map/ppermute | solution.py:217
  89.0 4.4 %collective-permute-done.18.refs_2_ = bf16[4,128,256]{2,1,0:T(8,128)(2,1)S(1)} collective-permute-done((bf16[4,128,256]{2,1,0:T(8,128)(2,1)S(1)}, bf16[4,128,256]{2,1,0:T(8,128)(2,1)S(1)}, u32[]{:S(2)}, u32[]{:S(2)}) %collective-permute-start.18) | collective-permute-done | bytes 262176 | tf_op jit(solution)/shard_map/ppermute | solution.py:217
  93.4 1.4 %collective-permute-done.19.refs_3_ = bf16[4,128,256]{2,1,0:T(8,128)(2,1)S(1)} collective-permute-done((bf16[4,128,256]{2,1,0:T(8,128)(2,1)S(1)}, bf16[4,128,256]{2,1,0:T(8,128)(2,1)S(1)}, u32[]{:S(2)}, u32[]{:S(2)}) %collective-permute-start.19) | collective-permute-done | bytes 262176 | tf_op jit(solution)/shard_map/ppermute | solution.py:217
  94.8 1.0 line_sum.3
  95.7 1.5 %collective-permute-start.20 = (bf16[256,256]{1,0:T(8,128)(2,1)S(1)}, bf16[256,256]{1,0:T(8,128)(2,1)S(1)}, u32[]{:S(2)}, u32[]{:S(2)}) collective-permute-start(bf16[256,256]{1,0:T(8,128)(2,1)S(1)} %get-tuple-element.62), channel_id=1, source_target_pairs={{0,32},{8,40},{16,48},{24,56},{32,0},{40,8},{48,16},{56,24},{64,96... | collective-permute-start | bytes 393224 | tf_op jit(solution)/shard_map/ppermute | solution.py:217
  97.2 0.5 collective-permute-done.13.refs_0_
  97.7 0.3 collective-permute-start.21
  98.0 2.4 %collective-permute-start.22 = (bf16[256,256]{1,0:T(8,128)(2,1)S(1)}, bf16[256,256]{1,0:T(8,128)(2,1)S(1)}, u32[]{:S(2)}, u32[]{:S(2)}) collective-permute-start(bf16[256,256]{1,0:T(8,128)(2,1)S(1)} %get-tuple-element.64), channel_id=1, source_target_pairs={{0,56},{8,0},{16,8},{24,16},{32,24},{40,32},{48,40},{56,48},{64,12... | collective-permute-start | bytes 393224 | tf_op jit(solution)/shard_map/ppermute | solution.py:217
  100.4 4.1 %collective-permute-done.20.refs_4_ = bf16[256,256]{1,0:T(8,128)(2,1)S(1)} collective-permute-done((bf16[256,256]{1,0:T(8,128)(2,1)S(1)}, bf16[256,256]{1,0:T(8,128)(2,1)S(1)}, u32[]{:S(2)}, u32[]{:S(2)}) %collective-permute-start.20) | collective-permute-done | bytes 131104 | tf_op jit(solution)/shard_map/ppermute | solution.py:217
  104.5 2.2 %collective-permute-done.21.refs_5_ = bf16[256,256]{1,0:T(8,128)(2,1)S(1)} collective-permute-done((bf16[256,256]{1,0:T(8,128)(2,1)S(1)}, bf16[256,256]{1,0:T(8,128)(2,1)S(1)}, u32[]{:S(2)}, u32[]{:S(2)}) %collective-permute-start.21) | collective-permute-done | bytes 131104 | tf_op jit(solution)/shard_map/ppermute | solution.py:217
  106.7 3.0 %collective-permute-done.22.refs_6_ = bf16[256,256]{1,0:T(8,128)(2,1)S(1)} collective-permute-done((bf16[256,256]{1,0:T(8,128)(2,1)S(1)}, bf16[256,256]{1,0:T(8,128)(2,1)S(1)}, u32[]{:S(2)}, u32[]{:S(2)}) %collective-permute-start.22) | collective-permute-done | bytes 131104 | tf_op jit(solution)/shard_map/ppermute | solution.py:217
  109.7 0.8 add.1
  (25 shorter events, 0.1 us)
Async XLA Ops:
  0.6 0.9 copy-start.3
  1.6 22.1 %copy-start.6 = (s32[64,8]{0,1:T(8,128)S(1)}, s32[64,8]{0,1:T(8,128)}, u32[]{:S(2)}) copy-start(s32[64,8]{0,1:T(8,128)} %param.10) | copy-start | bytes 6148
  1.6 8.6 %collective-permute-start = (bf16[256,256]{1,0:T(8,128)(2,1)S(1)}, bf16[256,256]{1,0:T(8,128)(2,1)S(1)}, u32[]{:S(2)}, u32[]{:S(2)}) collective-permute-start(bf16[256,256]{1,0:T(8,128)(2,1)S(1)} %constant_dynamic-update-slice_fusion.refs_0_), channel_id=1, source_target_pairs={{0,56},{8,0},{16,8},{24,16},{32,24},{40,32},{48,40},{56,48},{64,12... | collective-permute-start | bytes 393224 | tf_op jit(solution)/shard_map/ppermute | solution.py:217
  8.1 5.6 %collective-permute-start.4 = (bf16[256,256]{1,0:T(8,128)(2,1)S(1)}, bf16[256,256]{1,0:T(8,128)(2,1)S(1)}, u32[]{:S(2)}, u32[]{:S(2)}) collective-permute-start(bf16[256,256]{1,0:T(8,128)(2,1)S(1)} %constant_dynamic-update-slice_fusion.refs_0_), channel_id=1, source_target_pairs={{0,8},{8,16},{16,24},{24,32},{32,40},{40,48},{48,56},{56,0},{64,72... | collective-permute-start | bytes 393224 | tf_op jit(solution)/shard_map/ppermute | solution.py:217
  10.2 5.4 %collective-permute-start.1 = (bf16[256,256]{1,0:T(8,128)(2,1)S(1)}, bf16[256,256]{1,0:T(8,128)(2,1)S(1)}, u32[]{:S(2)}, u32[]{:S(2)}) collective-permute-start(bf16[256,256]{1,0:T(8,128)(2,1)S(1)} %collective-permute-done.refs_1_), channel_id=1, source_target_pairs={{0,56},{8,0},{16,8},{24,16},{32,24},{40,32},{48,40},{56,48},{64,12... | collective-permute-start | bytes 393224 | tf_op jit(solution)/shard_map/ppermute | solution.py:217
  13.6 5.0 %collective-permute-start.5 = (bf16[256,256]{1,0:T(8,128)(2,1)S(1)}, bf16[256,256]{1,0:T(8,128)(2,1)S(1)}, u32[]{:S(2)}, u32[]{:S(2)}) collective-permute-start(bf16[256,256]{1,0:T(8,128)(2,1)S(1)} %collective-permute-done.4.refs_7_), channel_id=1, source_target_pairs={{0,8},{8,16},{16,24},{24,32},{32,40},{40,48},{48,56},{56,0},{64,72... | collective-permute-start | bytes 393224 | tf_op jit(solution)/shard_map/ppermute | solution.py:217
  15.6 5.0 %collective-permute-start.2 = (bf16[256,256]{1,0:T(8,128)(2,1)S(1)}, bf16[256,256]{1,0:T(8,128)(2,1)S(1)}, u32[]{:S(2)}, u32[]{:S(2)}) collective-permute-start(bf16[256,256]{1,0:T(8,128)(2,1)S(1)} %collective-permute-done.1.refs_2_), channel_id=1, source_target_pairs={{0,56},{8,0},{16,8},{24,16},{32,24},{40,32},{48,40},{56,48},{64,12... | collective-permute-start | bytes 393224 | tf_op jit(solution)/shard_map/ppermute | solution.py:217
  18.7 8.2 %collective-permute-start.6 = (bf16[256,256]{1,0:T(8,128)(2,1)S(1)}, bf16[256,256]{1,0:T(8,128)(2,1)S(1)}, u32[]{:S(2)}, u32[]{:S(2)}) collective-permute-start(bf16[256,256]{1,0:T(8,128)(2,1)S(1)} %collective-permute-done.5.refs_6_), channel_id=1, source_target_pairs={{0,8},{8,16},{16,24},{24,32},{32,40},{40,48},{48,56},{56,0},{64,72... | collective-permute-start | bytes 393224 | tf_op jit(solution)/shard_map/ppermute | solution.py:217
  20.6 6.3 %collective-permute-start.3 = (bf16[256,256]{1,0:T(8,128)(2,1)S(1)}, bf16[256,256]{1,0:T(8,128)(2,1)S(1)}, u32[]{:S(2)}, u32[]{:S(2)}) collective-permute-start(bf16[256,256]{1,0:T(8,128)(2,1)S(1)} %collective-permute-done.2.refs_3_), channel_id=1, source_target_pairs={{0,56},{8,0},{16,8},{24,16},{32,24},{40,32},{48,40},{56,48},{64,12... | collective-permute-start | bytes 393224 | tf_op jit(solution)/shard_map/ppermute | solution.py:217
  23.8 0.7 copy-start.5
  26.9 5.9 %copy-start.4 = (bf16[32,4096]{1,0:T(8,128)(2,1)S(1)}, bf16[32,4096]{1,0:T(8,128)(2,1)}, u32[]{:S(2)}) copy-start(bf16[32,4096]{1,0:T(8,128)(2,1)} %cot_ref.1) | copy-start | bytes 786436
  27.8 20.8 %collective-permute-start.7 = (bf16[8,128,256]{2,1,0:T(8,128)(2,1)S(1)}, bf16[8,128,256]{2,1,0:T(8,128)(2,1)S(1)}, u32[]{:S(2)}, u32[]{:S(2)}) collective-permute-start(bf16[8,128,256]{2,1,0:T(8,128)(2,1)S(1)} %get-tuple-element.39), channel_id=1, source_target_pairs={{0,64},{8,72},{16,80},{24,88},{32,96},{40,104},{48,112},{56,120},{... | collective-permute-start | bytes 1572872 | tf_op jit(solution)/shard_map/ppermute | solution.py:217
  29.1 21.7 %collective-permute-start.8 = (bf16[8,128,256]{2,1,0:T(8,128)(2,1)S(1)}, bf16[8,128,256]{2,1,0:T(8,128)(2,1)S(1)}, u32[]{:S(2)}, u32[]{:S(2)}) collective-permute-start(bf16[8,128,256]{2,1,0:T(8,128)(2,1)S(1)} %get-tuple-element.40), channel_id=1, source_target_pairs={{0,128},{8,136},{16,144},{24,152},{32,160},{40,168},{48,176},{56,1... | collective-permute-start | bytes 1572872 | tf_op jit(solution)/shard_map/ppermute | solution.py:217
  31.8 21.9 %collective-permute-start.9 = (bf16[8,128,256]{2,1,0:T(8,128)(2,1)S(1)}, bf16[8,128,256]{2,1,0:T(8,128)(2,1)S(1)}, u32[]{:S(2)}, u32[]{:S(2)}) collective-permute-start(bf16[8,128,256]{2,1,0:T(8,128)(2,1)S(1)} %get-tuple-element.41), channel_id=1, source_target_pairs={{0,192},{8,200},{16,208},{24,216},{32,224},{40,232},{48,240},{56,2... | collective-permute-start | bytes 1572872 | tf_op jit(solution)/shard_map/ppermute | solution.py:217
  32.9 20.8 %copy-start.1 = (bf16[256,512]{1,0:T(8,128)(2,1)S(1)}, bf16[256,512]{1,0:T(8,128)(2,1)}, u32[]{:S(2)}) copy-start(bf16[256,512]{1,0:T(8,128)(2,1)} %q_ref.1) | copy-start | bytes 786436
  32.9 20.8 %copy-start.2 = (bf16[256,128]{1,0:T(8,128)(2,1)S(1)}, bf16[256,128]{1,0:T(8,128)(2,1)}, u32[]{:S(2)}) copy-start(bf16[256,128]{1,0:T(8,128)(2,1)} %k_ref.1) | copy-start | bytes 196612
  61.3 18.0 %collective-permute-start.10 = (bf16[4,128,256]{2,1,0:T(8,128)(2,1)S(1)}, bf16[4,128,256]{2,1,0:T(8,128)(2,1)S(1)}, u32[]{:S(2)}, u32[]{:S(2)}) collective-permute-start(bf16[4,128,256]{2,1,0:T(8,128)(2,1)S(1)} %get-tuple-element.51), channel_id=1, source_target_pairs={{0,64},{8,72},{16,80},{24,88},{32,96},{40,104},{48,112},{56,120},{... | collective-permute-start | bytes 786440 | tf_op jit(solution)/shard_map/ppermute | solution.py:217
  63.2 16.1 %collective-permute-start.11 = (bf16[4,128,256]{2,1,0:T(8,128)(2,1)S(1)}, bf16[4,128,256]{2,1,0:T(8,128)(2,1)S(1)}, u32[]{:S(2)}, u32[]{:S(2)}) collective-permute-start(bf16[4,128,256]{2,1,0:T(8,128)(2,1)S(1)} %get-tuple-element.52), channel_id=1, source_target_pairs={{0,128},{8,136},{16,144},{24,152},{32,160},{40,168},{48,176},{56,1... | collective-permute-start | bytes 786440 | tf_op jit(solution)/shard_map/ppermute | solution.py:217
  65.9 13.4 %collective-permute-start.12 = (bf16[4,128,256]{2,1,0:T(8,128)(2,1)S(1)}, bf16[4,128,256]{2,1,0:T(8,128)(2,1)S(1)}, u32[]{:S(2)}, u32[]{:S(2)}) collective-permute-start(bf16[4,128,256]{2,1,0:T(8,128)(2,1)S(1)} %get-tuple-element.53), channel_id=1, source_target_pairs={{0,192},{8,200},{16,208},{24,216},{32,224},{40,232},{48,240},{56,2... | collective-permute-start | bytes 786440 | tf_op jit(solution)/shard_map/ppermute | solution.py:217
  79.3 1.0 copy-start
  80.3 8.7 %collective-permute-start.17 = (bf16[4,128,256]{2,1,0:T(8,128)(2,1)S(1)}, bf16[4,128,256]{2,1,0:T(8,128)(2,1)S(1)}, u32[]{:S(2)}, u32[]{:S(2)}) collective-permute-start(bf16[4,128,256]{2,1,0:T(8,128)(2,1)S(1)} %get-tuple-element.59), channel_id=1, source_target_pairs={{0,64},{8,72},{16,80},{24,88},{32,96},{40,104},{48,112},{56,120},{... | collective-permute-start | bytes 786440 | tf_op jit(solution)/shard_map/ppermute | solution.py:217
  80.6 12.8 %collective-permute-start.18 = (bf16[4,128,256]{2,1,0:T(8,128)(2,1)S(1)}, bf16[4,128,256]{2,1,0:T(8,128)(2,1)S(1)}, u32[]{:S(2)}, u32[]{:S(2)}) collective-permute-start(bf16[4,128,256]{2,1,0:T(8,128)(2,1)S(1)} %get-tuple-element.60), channel_id=1, source_target_pairs={{0,128},{8,136},{16,144},{24,152},{32,160},{40,168},{48,176},{56,1... | collective-permute-start | bytes 786440 | tf_op jit(solution)/shard_map/ppermute | solution.py:217
  82.1 12.7 %collective-permute-start.19 = (bf16[4,128,256]{2,1,0:T(8,128)(2,1)S(1)}, bf16[4,128,256]{2,1,0:T(8,128)(2,1)S(1)}, u32[]{:S(2)}, u32[]{:S(2)}) collective-permute-start(bf16[4,128,256]{2,1,0:T(8,128)(2,1)S(1)} %get-tuple-element.61), channel_id=1, source_target_pairs={{0,192},{8,200},{16,208},{24,216},{32,224},{40,232},{48,240},{56,2... | collective-permute-start | bytes 786440 | tf_op jit(solution)/shard_map/ppermute | solution.py:217
  83.2 14.5 %collective-permute-start.13 = (bf16[256,256]{1,0:T(8,128)(2,1)S(1)}, bf16[256,256]{1,0:T(8,128)(2,1)S(1)}, u32[]{:S(2)}, u32[]{:S(2)}) collective-permute-start(bf16[256,256]{1,0:T(8,128)(2,1)S(1)} %get-tuple-element.54), channel_id=1, source_target_pairs={{0,24},{8,32},{16,40},{24,48},{32,56},{40,0},{48,8},{56,16},{64,88... | collective-permute-start | bytes 393224 | tf_op jit(solution)/shard_map/ppermute | solution.py:217
  84.2 13.9 %collective-permute-start.14 = (bf16[256,256]{1,0:T(8,128)(2,1)S(1)}, bf16[256,256]{1,0:T(8,128)(2,1)S(1)}, u32[]{:S(2)}, u32[]{:S(2)}) collective-permute-start(bf16[256,256]{1,0:T(8,128)(2,1)S(1)} %get-tuple-element.55), channel_id=1, source_target_pairs={{0,40},{8,48},{16,56},{24,0},{32,8},{40,16},{48,24},{56,32},{64,10... | collective-permute-start | bytes 393224 | tf_op jit(solution)/shard_map/ppermute | solution.py:217
  89.0 11.4 %collective-permute-start.15 = (bf16[256,256]{1,0:T(8,128)(2,1)S(1)}, bf16[256,256]{1,0:T(8,128)(2,1)S(1)}, u32[]{:S(2)}, u32[]{:S(2)}) collective-permute-start(bf16[256,256]{1,0:T(8,128)(2,1)S(1)} %get-tuple-element.56), channel_id=1, source_target_pairs={{0,16},{8,24},{16,32},{24,40},{32,48},{40,56},{48,0},{56,8},{64,80... | collective-permute-start | bytes 393224 | tf_op jit(solution)/shard_map/ppermute | solution.py:217
  93.4 7.0 %collective-permute-start.16 = (bf16[256,256]{1,0:T(8,128)(2,1)S(1)}, bf16[256,256]{1,0:T(8,128)(2,1)S(1)}, u32[]{:S(2)}, u32[]{:S(2)}) collective-permute-start(bf16[256,256]{1,0:T(8,128)(2,1)S(1)} %get-tuple-element.57), channel_id=1, source_target_pairs={{0,48},{8,56},{16,0},{24,8},{32,16},{40,24},{48,32},{56,40},{64,11... | collective-permute-start | bytes 393224 | tf_op jit(solution)/shard_map/ppermute | solution.py:217
  95.7 8.8 %collective-permute-start.20 = (bf16[256,256]{1,0:T(8,128)(2,1)S(1)}, bf16[256,256]{1,0:T(8,128)(2,1)S(1)}, u32[]{:S(2)}, u32[]{:S(2)}) collective-permute-start(bf16[256,256]{1,0:T(8,128)(2,1)S(1)} %get-tuple-element.62), channel_id=1, source_target_pairs={{0,32},{8,40},{16,48},{24,56},{32,0},{40,8},{48,16},{56,24},{64,96... | collective-permute-start | bytes 393224 | tf_op jit(solution)/shard_map/ppermute | solution.py:217
  97.7 9.0 %collective-permute-start.21 = (bf16[256,256]{1,0:T(8,128)(2,1)S(1)}, bf16[256,256]{1,0:T(8,128)(2,1)S(1)}, u32[]{:S(2)}, u32[]{:S(2)}) collective-permute-start(bf16[256,256]{1,0:T(8,128)(2,1)S(1)} %get-tuple-element.63), channel_id=1, source_target_pairs={{0,8},{8,16},{16,24},{24,32},{32,40},{40,48},{48,56},{56,0},{64,72... | collective-permute-start | bytes 393224 | tf_op jit(solution)/shard_map/ppermute | solution.py:217
  98.0 11.7 %collective-permute-start.22 = (bf16[256,256]{1,0:T(8,128)(2,1)S(1)}, bf16[256,256]{1,0:T(8,128)(2,1)S(1)}, u32[]{:S(2)}, u32[]{:S(2)}) collective-permute-start(bf16[256,256]{1,0:T(8,128)(2,1)S(1)} %get-tuple-element.64), channel_id=1, source_target_pairs={{0,56},{8,0},{16,8},{24,16},{32,24},{40,32},{48,40},{56,48},{64,12... | collective-permute-start | bytes 393224 | tf_op jit(solution)/shard_map/ppermute | solution.py:217

commit v4 on v3

--- a/solution.py
+++ b/solution.py
@@ -12,7 +12,7 @@
 SPAN = 128
 RING = 8
 HIDDEN = -1.0e30
-GROUPS = ((3, 5, 2, 6), (4, 1, 7, 0))
+GROUPS = ((3, 5, 4, 0), (2, 6, 1, 7))
 SCALE = 1.0 / math.sqrt(HEAD_DIM)
 SMEM = pl.BlockSpec(memory_space=pltpu.SMEM)
 VMEM = pl.BlockSpec(memory_space=pltpu.VMEM)
@@ -167,8 +167,7 @@
                     ref[place, :, HEAD_DIM:] = value_part[rows].astype(bf16)
 
 
-def line_sum_kernel(group, passed, me_ref, table_ref, *refs):
-    refs = refs[:len(refs) - passed]
+def line_sum_kernel(group, me_ref, table_ref, *refs):
     outs = refs[-len(group):]
     lines = math.isqrt((table_ref.shape[0] - 1) // RING)
     backs = refs[-len(group) - lines:-len(group)]
@@ -186,6 +185,10 @@
             for half, part in zip(halves, parts):
                 total += jnp.where(half == side, part, 0.0)
             out[side * SPAN:(side + 1) * SPAN, :] = total.astype(bf16)
+
+
+def hold_kernel(*refs):
+    pass
 
 
 def add_kernel(ownk_ref, ownv_ref, *refs):
@@ -287,20 +290,26 @@
 
     attended_out = lax.all_to_all(attended, "head", split_axis=0, concat_axis=1, tiled=True)
     back = []
+    later = sent[lines:]
+    sent[lines:] = pl.pallas_call(
+        hold_kernel,
+        out_shape=[shape(part.shape, bf16) for part in later],
+        in_specs=[ANY] * len(later),
+        out_specs=[ANY] * len(later),
+        input_output_aliases={i: i for i in range(len(later))},
+        compiler_params=params(),
+        cost_estimate=pl.CostEstimate(flops=5_000_000_000, bytes_accessed=0, transcendentals=0),
+        name="hold",
+    )(*later)
     for index, group in enumerate(GROUPS):
-        after = [attended_out] if index == 0 else []
-        later = sent[(index + 1) * lines:]
-        first = 2 + len(after)
         sums = pl.pallas_call(
-            functools.partial(line_sum_kernel, group, len(later)),
-            out_shape=[both] * len(group) + [shape(part.shape, bf16) for part in later],
-            in_specs=[SMEM, SMEM] + [ANY] * (len(after) + len(later)) + [VMEM] * lines,
-            out_specs=[VMEM] * len(group) + [ANY] * len(later),
-            input_output_aliases={first + i: len(group) + i for i in range(len(later))},
+            functools.partial(line_sum_kernel, group),
+            out_shape=[both] * len(group),
+            in_specs=[SMEM, SMEM] + [VMEM] * lines,
+            out_specs=[VMEM] * len(group),
             compiler_params=params(),
             name="line_sum",
-        )(me, table, *after, *later, *over_lines(sent[index * lines:(index + 1) * lines]))
-        sent[(index + 1) * lines:] = sums[len(group):]
+        )(me, table, *over_lines(sent[index * lines:(index + 1) * lines]))
         back += [shift(part, 0, far) if far else part for far, part in zip(group, sums)]
     key_grad, value_grad = pl.pallas_call(
         add_kernel,

time: 111 us -> 110 us (level)
  blocking collectives: 29.1 us -> 15.7 us
  starting transfers between devices: 37.3 us -> 49.7 us
    all_to_all x1 -> x0, blocking collectives: 13.4 us -> none  [body(): lax.all_to_all(attended, 'head', split_axis=0, concat_axis=1, tiled=True)]
    all_to_all x0 -> x1, starting transfers between devices: none -> 7.47 us  [body(): lax.all_to_all(attended, 'head', split_axis=0, concat_axis=1, tiled=True)]
    ppermute x23, starting transfers between devices: 37.3 us -> 42.3 us  [shift(): return lax.ppermute(array, 'seq', moves)]
  transfers between devices with their start and end apart: 23 -> 24, of which waited for: 12 -> 11; matrix products, arithmetic and copies ran while one was open for 0% -> 1% of each run, Pallas kernels for 3% -> 4%
where the time goes in v4:
time: 110 us
  starting transfers between devices  49.7 us (45%)
  waiting for transfers between devices  27.4 us (25%)
  blocking collectives  15.7 us (14%)
  Pallas kernels  13.7 us (12%)
  local copies, waits for them, and re-layouts  2.4 us (2%)
    ppermute x23, starting transfers between devices, shift(): return lax.ppermute(array, 'seq', moves)  42.3 us
    ppermute x23, waiting for transfers between devices, shift(): return lax.ppermute(array, 'seq', moves)  27.4 us
    all_to_all x1, blocking collectives, body(): lax.all_to_all(columns, 'head', split_axis=0, concat_axis=0, tiled=True)  15.7 us
    pallas_call x1, Pallas kernels, body(): pl.pallas_call(attend_kernel, grid=(2,), out_shape=[shape(queries.shape,...  7.68 us
    all_to_all x1, starting transfers between devices, body(): lax.all_to_all(attended, 'head', split_axis=0, concat_axis=1, tiled=True)  7.47 us
    pallas_call x1, Pallas kernels, body(): pl.pallas_call(route_kernel, out_shape=(shape((2 * picked,), jnp.int32),...  2.44 us
  transfers between devices with their start and end apart: 24, of which 11 were waited for; matrix products, arithmetic and copies ran while one was open for 1% of the time, Pallas kernels for 4%

profile of v4, /device:TPU:1, one launch (start us, length us, event | category | flops | bytes accessed | tf_op | source)
XLA Modules:
  0.0 109.7 jit_solution(11007756886998953659)
XLA Ops:
  0.6 0.9 constant_dynamic-update-slice_fusion.1
  1.6 0.0 copy-start.5
  1.6 6.5 %collective-permute-start = (bf16[256,256]{1,0:T(8,128)(2,1)S(1)}, bf16[256,256]{1,0:T(8,128)(2,1)S(1)}, u32[]{:S(2)}, u32[]{:S(2)}) collective-permute-start(bf16[256,256]{1,0:T(8,128)(2,1)S(1)} %constant_dynamic-update-slice_fusion.refs_0_), channel_id=1, source_target_pairs={{0,56},{8,0},{16,8},{24,16},{32,24},{40,32},{48,40},{56,48},{64,12... | collective-permute-start | bytes 393224 | tf_op jit(solution)/shard_map/ppermute | solution.py:220
  8.1 0.0 collective-permute-start.4
  8.1 2.2 %collective-permute-done.refs_1_ = bf16[256,256]{1,0:T(8,128)(2,1)S(1)} collective-permute-done((bf16[256,256]{1,0:T(8,128)(2,1)S(1)}, bf16[256,256]{1,0:T(8,128)(2,1)S(1)}, u32[]{:S(2)}, u32[]{:S(2)}) %collective-permute-start) | collective-permute-done | bytes 131104 | tf_op jit(solution)/shard_map/ppermute | solution.py:220
  10.2 3.4 %collective-permute-start.1 = (bf16[256,256]{1,0:T(8,128)(2,1)S(1)}, bf16[256,256]{1,0:T(8,128)(2,1)S(1)}, u32[]{:S(2)}, u32[]{:S(2)}) collective-permute-start(bf16[256,256]{1,0:T(8,128)(2,1)S(1)} %collective-permute-done.refs_1_), channel_id=1, source_target_pairs={{0,56},{8,0},{16,8},{24,16},{32,24},{40,32},{48,40},{56,48},{64,12... | collective-permute-start | bytes 393224 | tf_op jit(solution)/shard_map/ppermute | solution.py:220
  13.6 0.0 collective-permute-done.4.refs_7_
  13.6 1.9 %collective-permute-done.1.refs_2_ = bf16[256,256]{1,0:T(8,128)(2,1)S(1)} collective-permute-done((bf16[256,256]{1,0:T(8,128)(2,1)S(1)}, bf16[256,256]{1,0:T(8,128)(2,1)S(1)}, u32[]{:S(2)}, u32[]{:S(2)}) %collective-permute-start.1) | collective-permute-done | bytes 131104 | tf_op jit(solution)/shard_map/ppermute | solution.py:220
  15.6 3.1 %collective-permute-start.2 = (bf16[256,256]{1,0:T(8,128)(2,1)S(1)}, bf16[256,256]{1,0:T(8,128)(2,1)S(1)}, u32[]{:S(2)}, u32[]{:S(2)}) collective-permute-start(bf16[256,256]{1,0:T(8,128)(2,1)S(1)} %collective-permute-done.1.refs_2_), channel_id=1, source_target_pairs={{0,56},{8,0},{16,8},{24,16},{32,24},{40,32},{48,40},{56,48},{64,12... | collective-permute-start | bytes 393224 | tf_op jit(solution)/shard_map/ppermute | solution.py:220
  18.7 0.0 collective-permute-done.5.refs_6_
  18.7 1.9 %collective-permute-done.2.refs_3_ = bf16[256,256]{1,0:T(8,128)(2,1)S(1)} collective-permute-done((bf16[256,256]{1,0:T(8,128)(2,1)S(1)}, bf16[256,256]{1,0:T(8,128)(2,1)S(1)}, u32[]{:S(2)}, u32[]{:S(2)}) %collective-permute-start.2) | collective-permute-done | bytes 131104 | tf_op jit(solution)/shard_map/ppermute | solution.py:220
  20.6 3.1 %collective-permute-start.3 = (bf16[256,256]{1,0:T(8,128)(2,1)S(1)}, bf16[256,256]{1,0:T(8,128)(2,1)S(1)}, u32[]{:S(2)}, u32[]{:S(2)}) collective-permute-start(bf16[256,256]{1,0:T(8,128)(2,1)S(1)} %collective-permute-done.2.refs_3_), channel_id=1, source_target_pairs={{0,56},{8,0},{16,8},{24,16},{32,24},{40,32},{48,40},{56,48},{64,12... | collective-permute-start | bytes 393224 | tf_op jit(solution)/shard_map/ppermute | solution.py:220
  23.7 0.1 copy.14.lists_ref
  23.8 0.7 copy-done.4
  24.4 2.4 %route.1 = (s32[16]{0:T(128)S(1)}, s32[129]{0:T(256)S(1)}) custom-call(s32[1]{0:T(128)} %bitcast.me_ref, s32[64]{0:T(128)S(1)} %copy-done.4, s32[64,8]{1,0:T(8,128)S(1)} %copy.14.lists_ref), custom_call_target="tpu_custom_call" | custom-call | tf_op jit(solution)/shard_map/route/pallas_call | solution.py:234
  26.9 0.0 copy-start.3
  26.9 0.8 line.1
  27.8 1.4 %collective-permute-start.7 = (bf16[8,128,256]{2,1,0:T(8,128)(2,1)S(1)}, bf16[8,128,256]{2,1,0:T(8,128)(2,1)S(1)}, u32[]{:S(2)}, u32[]{:S(2)}) collective-permute-start(bf16[8,128,256]{2,1,0:T(8,128)(2,1)S(1)} %get-tuple-element.39), channel_id=1, source_target_pairs={{0,64},{8,72},{16,80},{24,88},{32,96},{40,104},{48,112},{56,120},{... | collective-permute-start | bytes 1572872 | tf_op jit(solution)/shard_map/ppermute | solution.py:220
  29.1 2.6 %collective-permute-start.8 = (bf16[8,128,256]{2,1,0:T(8,128)(2,1)S(1)}, bf16[8,128,256]{2,1,0:T(8,128)(2,1)S(1)}, u32[]{:S(2)}, u32[]{:S(2)}) collective-permute-start(bf16[8,128,256]{2,1,0:T(8,128)(2,1)S(1)} %get-tuple-element.40), channel_id=1, source_target_pairs={{0,128},{8,136},{16,144},{24,152},{32,160},{40,168},{48,176},{56,1... | collective-permute-start | bytes 1572872 | tf_op jit(solution)/shard_map/ppermute | solution.py:220
  31.8 1.1 collective-permute-start.9
  32.9 0.0 copy-start
  32.9 0.0 copy-start.1
  32.9 15.7 %all_to_all.24 = bf16[8,32,512]{2,1,0:T(8,128)(2,1)S(1)} all-to-all(bf16[8,32,512]{2,1,0:T(8,128)(2,1)S(1)} %columns.1), channel_id=1, replica_groups=mesh['seq'=32,'head'=8] {'head'}, dimensions={0} | all-to-all | bytes 524288 | tf_op jit(solution)/shard_map/all_to_all | solution.py:260
  48.6 2.2 %collective-permute-done.8.refs_2_ = bf16[8,128,256]{2,1,0:T(8,128)(2,1)S(1)} collective-permute-done((bf16[8,128,256]{2,1,0:T(8,128)(2,1)S(1)}, bf16[8,128,256]{2,1,0:T(8,128)(2,1)S(1)}, u32[]{:S(2)}, u32[]{:S(2)}) %collective-permute-start.8) | collective-permute-done | bytes 524320 | tf_op jit(solution)/shard_map/ppermute | solution.py:220
  50.8 2.9 %collective-permute-done.9.refs_3_ = bf16[8,128,256]{2,1,0:T(8,128)(2,1)S(1)} collective-permute-done((bf16[8,128,256]{2,1,0:T(8,128)(2,1)S(1)}, bf16[8,128,256]{2,1,0:T(8,128)(2,1)S(1)}, u32[]{:S(2)}, u32[]{:S(2)}) %collective-permute-start.9) | collective-permute-done | bytes 524320 | tf_op jit(solution)/shard_map/ppermute | solution.py:220
  53.7 7.7 %attend.1 = (bf16[256,512]{1,0:T(8,128)(2,1)}, bf16[256,512]{1,0:T(8,128)(2,1)}, f32[256,128]{1,0:T(8,128)S(1)}, f32[256,128]{1,0:T(8,128)S(1)}, bf16[4,128,256]...) custom-call(s32[1]{0:T(128)} %bitcast.me_ref, ...), custom_call_target="tpu_custom_call" | custom-call | tf_op jit(solution)/shard_map/attend/pallas_call | solution.py:267
  61.4 1.9 %collective-permute-start.10 = (bf16[4,128,256]{2,1,0:T(8,128)(2,1)S(1)}, bf16[4,128,256]{2,1,0:T(8,128)(2,1)S(1)}, u32[]{:S(2)}, u32[]{:S(2)}) collective-permute-start(bf16[4,128,256]{2,1,0:T(8,128)(2,1)S(1)} %get-tuple-element.47), channel_id=1, source_target_pairs={{0,64},{8,72},{16,80},{24,88},{32,96},{40,104},{48,112},{56,120},{... | collective-permute-start | bytes 786440 | tf_op jit(solution)/shard_map/ppermute | solution.py:220
  63.3 2.7 %collective-permute-start.11 = (bf16[4,128,256]{2,1,0:T(8,128)(2,1)S(1)}, bf16[4,128,256]{2,1,0:T(8,128)(2,1)S(1)}, u32[]{:S(2)}, u32[]{:S(2)}) collective-permute-start(bf16[4,128,256]{2,1,0:T(8,128)(2,1)S(1)} %get-tuple-element.48), channel_id=1, source_target_pairs={{0,128},{8,136},{16,144},{24,152},{32,160},{40,168},{48,176},{56,1... | collective-permute-start | bytes 786440 | tf_op jit(solution)/shard_map/ppermute | solution.py:220
  66.0 1.5 %collective-permute-start.16 = (bf16[4,128,256]{2,1,0:T(8,128)(2,1)S(1)}, bf16[4,128,256]{2,1,0:T(8,128)(2,1)S(1)}, u32[]{:S(2)}, u32[]{:S(2)}) collective-permute-start(bf16[4,128,256]{2,1,0:T(8,128)(2,1)S(1)} %get-tuple-element.59), channel_id=1, source_target_pairs={{0,64},{8,72},{16,80},{24,88},{32,96},{40,104},{48,112},{56,120},{... | collective-permute-start | bytes 786440 | tf_op jit(solution)/shard_map/ppermute | solution.py:220
  67.4 0.3 collective-permute-start.17
  67.7 1.9 %collective-permute-done.10.refs_1_ = bf16[4,128,256]{2,1,0:T(8,128)(2,1)S(1)} collective-permute-done((bf16[4,128,256]{2,1,0:T(8,128)(2,1)S(1)}, bf16[4,128,256]{2,1,0:T(8,128)(2,1)S(1)}, u32[]{:S(2)}, u32[]{:S(2)}) %collective-permute-start.10) | collective-permute-done | bytes 262176 | tf_op jit(solution)/shard_map/ppermute | solution.py:220
  69.6 2.3 %collective-permute-start.18 = (bf16[4,128,256]{2,1,0:T(8,128)(2,1)S(1)}, bf16[4,128,256]{2,1,0:T(8,128)(2,1)S(1)}, u32[]{:S(2)}, u32[]{:S(2)}) collective-permute-start(bf16[4,128,256]{2,1,0:T(8,128)(2,1)S(1)} %get-tuple-element.61), channel_id=1, source_target_pairs={{0,192},{8,200},{16,208},{24,216},{32,224},{40,232},{48,240},{56,2... | collective-permute-start | bytes 786440 | tf_op jit(solution)/shard_map/ppermute | solution.py:220
  72.0 5.4 %collective-permute-done.11.refs_2_ = bf16[4,128,256]{2,1,0:T(8,128)(2,1)S(1)} collective-permute-done((bf16[4,128,256]{2,1,0:T(8,128)(2,1)S(1)}, bf16[4,128,256]{2,1,0:T(8,128)(2,1)S(1)}, u32[]{:S(2)}, u32[]{:S(2)}) %collective-permute-start.11) | collective-permute-done | bytes 262176 | tf_op jit(solution)/shard_map/ppermute | solution.py:220
  77.4 0.6 collective-permute-done.12.refs_3_
  78.0 1.0 line_sum.2
  78.9 0.1 collective-permute-start.13
  79.0 4.5 %collective-permute-start.14 = (bf16[256,256]{1,0:T(8,128)(2,1)S(1)}, bf16[256,256]{1,0:T(8,128)(2,1)S(1)}, u32[]{:S(2)}, u32[]{:S(2)}) collective-permute-start(bf16[256,256]{1,0:T(8,128)(2,1)S(1)} %get-tuple-element.51), channel_id=1, source_target_pairs={{0,40},{8,48},{16,56},{24,0},{32,8},{40,16},{48,24},{56,32},{64,10... | collective-permute-start | bytes 393224 | tf_op jit(solution)/shard_map/ppermute | solution.py:220
  83.5 7.5 %all-to-all-start.1 = ((bf16[8,32,512]{2,1,0:T(8,128)(2,1)}), bf16[8,32,512]{2,1,0:T(8,128)(2,1)S(1)}, u32[]{:S(2)}, u32[]{:S(2)}) async-start(bf16[8,32,512]{2,1,0:T(8,128)(2,1)} %bitcast.2), calls=%async_computation.1 | async-start | bytes 524288 | tf_op jit(solution)/shard_map/all_to_all | solution.py:291
  91.0 1.6 %collective-permute-start.15 = (bf16[256,256]{1,0:T(8,128)(2,1)S(1)}, bf16[256,256]{1,0:T(8,128)(2,1)S(1)}, u32[]{:S(2)}, u32[]{:S(2)}) collective-permute-start(bf16[256,256]{1,0:T(8,128)(2,1)S(1)} %get-tuple-element.52), channel_id=1, source_target_pairs={{0,32},{8,40},{16,48},{24,56},{32,0},{40,8},{48,16},{56,24},{64,96... | collective-permute-start | bytes 393224 | tf_op jit(solution)/shard_map/ppermute | solution.py:220
  92.5 1.0 line_sum.3
  93.5 1.0 collective-permute-start.19
  94.5 2.6 %collective-permute-start.20 = (bf16[256,256]{1,0:T(8,128)(2,1)S(1)}, bf16[256,256]{1,0:T(8,128)(2,1)S(1)}, u32[]{:S(2)}, u32[]{:S(2)}) collective-permute-start(bf16[256,256]{1,0:T(8,128)(2,1)S(1)} %get-tuple-element.63), channel_id=1, source_target_pairs={{0,48},{8,56},{16,0},{24,8},{32,16},{40,24},{48,32},{56,40},{64,11... | collective-permute-start | bytes 393224 | tf_op jit(solution)/shard_map/ppermute | solution.py:220
  97.2 2.7 %collective-permute-start.22 = (bf16[256,256]{1,0:T(8,128)(2,1)S(1)}, bf16[256,256]{1,0:T(8,128)(2,1)S(1)}, u32[]{:S(2)}, u32[]{:S(2)}) collective-permute-start(bf16[256,256]{1,0:T(8,128)(2,1)S(1)} %get-tuple-element.65), channel_id=1, source_target_pairs={{0,56},{8,0},{16,8},{24,16},{32,24},{40,32},{48,40},{56,48},{64,12... | collective-permute-start | bytes 393224 | tf_op jit(solution)/shard_map/ppermute | solution.py:220
  99.9 0.7 copy.16
  100.6 3.3 %collective-permute-done.15.refs_2_ = bf16[256,256]{1,0:T(8,128)(2,1)S(1)} collective-permute-done((bf16[256,256]{1,0:T(8,128)(2,1)S(1)}, bf16[256,256]{1,0:T(8,128)(2,1)S(1)}, u32[]{:S(2)}, u32[]{:S(2)}) %collective-permute-start.15) | collective-permute-done | bytes 131104 | tf_op jit(solution)/shard_map/ppermute | solution.py:220
  103.9 3.0 %collective-permute-done.20.refs_5_ = bf16[256,256]{1,0:T(8,128)(2,1)S(1)} collective-permute-done((bf16[256,256]{1,0:T(8,128)(2,1)S(1)}, bf16[256,256]{1,0:T(8,128)(2,1)S(1)}, u32[]{:S(2)}, u32[]{:S(2)}) %collective-permute-start.20) | collective-permute-done | bytes 131104 | tf_op jit(solution)/shard_map/ppermute | solution.py:220
  106.9 1.9 %collective-permute-done.21.refs_6_ = bf16[256,256]{1,0:T(8,128)(2,1)S(1)} collective-permute-done((bf16[256,256]{1,0:T(8,128)(2,1)S(1)}, bf16[256,256]{1,0:T(8,128)(2,1)S(1)}, u32[]{:S(2)}, u32[]{:S(2)}) %collective-permute-start.21) | collective-permute-done | bytes 131104 | tf_op jit(solution)/shard_map/ppermute | solution.py:220
  108.9 0.8 add.1
  (25 shorter events, 0.1 us)
Async XLA Ops:
  0.6 0.9 copy-start.2
  1.6 22.1 %copy-start.5 = (s32[64,8]{0,1:T(8,128)S(1)}, s32[64,8]{0,1:T(8,128)}, u32[]{:S(2)}) copy-start(s32[64,8]{0,1:T(8,128)} %param.10) | copy-start | bytes 6148
  1.6 8.6 %collective-permute-start = (bf16[256,256]{1,0:T(8,128)(2,1)S(1)}, bf16[256,256]{1,0:T(8,128)(2,1)S(1)}, u32[]{:S(2)}, u32[]{:S(2)}) collective-permute-start(bf16[256,256]{1,0:T(8,128)(2,1)S(1)} %constant_dynamic-update-slice_fusion.refs_0_), channel_id=1, source_target_pairs={{0,56},{8,0},{16,8},{24,16},{32,24},{40,32},{48,40},{56,48},{64,12... | collective-permute-start | bytes 393224 | tf_op jit(solution)/shard_map/ppermute | solution.py:220
  8.1 5.6 %collective-permute-start.4 = (bf16[256,256]{1,0:T(8,128)(2,1)S(1)}, bf16[256,256]{1,0:T(8,128)(2,1)S(1)}, u32[]{:S(2)}, u32[]{:S(2)}) collective-permute-start(bf16[256,256]{1,0:T(8,128)(2,1)S(1)} %constant_dynamic-update-slice_fusion.refs_0_), channel_id=1, source_target_pairs={{0,8},{8,16},{16,24},{24,32},{32,40},{40,48},{48,56},{56,0},{64,72... | collective-permute-start | bytes 393224 | tf_op jit(solution)/shard_map/ppermute | solution.py:220
  10.2 5.4 %collective-permute-start.1 = (bf16[256,256]{1,0:T(8,128)(2,1)S(1)}, bf16[256,256]{1,0:T(8,128)(2,1)S(1)}, u32[]{:S(2)}, u32[]{:S(2)}) collective-permute-start(bf16[256,256]{1,0:T(8,128)(2,1)S(1)} %collective-permute-done.refs_1_), channel_id=1, source_target_pairs={{0,56},{8,0},{16,8},{24,16},{32,24},{40,32},{48,40},{56,48},{64,12... | collective-permute-start | bytes 393224 | tf_op jit(solution)/shard_map/ppermute | solution.py:220
  13.6 5.0 %collective-permute-start.5 = (bf16[256,256]{1,0:T(8,128)(2,1)S(1)}, bf16[256,256]{1,0:T(8,128)(2,1)S(1)}, u32[]{:S(2)}, u32[]{:S(2)}) collective-permute-start(bf16[256,256]{1,0:T(8,128)(2,1)S(1)} %collective-permute-done.4.refs_7_), channel_id=1, source_target_pairs={{0,8},{8,16},{16,24},{24,32},{32,40},{40,48},{48,56},{56,0},{64,72... | collective-permute-start | bytes 393224 | tf_op jit(solution)/shard_map/ppermute | solution.py:220
  15.6 5.0 %collective-permute-start.2 = (bf16[256,256]{1,0:T(8,128)(2,1)S(1)}, bf16[256,256]{1,0:T(8,128)(2,1)S(1)}, u32[]{:S(2)}, u32[]{:S(2)}) collective-permute-start(bf16[256,256]{1,0:T(8,128)(2,1)S(1)} %collective-permute-done.1.refs_2_), channel_id=1, source_target_pairs={{0,56},{8,0},{16,8},{24,16},{32,24},{40,32},{48,40},{56,48},{64,12... | collective-permute-start | bytes 393224 | tf_op jit(solution)/shard_map/ppermute | solution.py:220
  18.7 8.2 %collective-permute-start.6 = (bf16[256,256]{1,0:T(8,128)(2,1)S(1)}, bf16[256,256]{1,0:T(8,128)(2,1)S(1)}, u32[]{:S(2)}, u32[]{:S(2)}) collective-permute-start(bf16[256,256]{1,0:T(8,128)(2,1)S(1)} %collective-permute-done.5.refs_6_), channel_id=1, source_target_pairs={{0,8},{8,16},{16,24},{24,32},{32,40},{40,48},{48,56},{56,0},{64,72... | collective-permute-start | bytes 393224 | tf_op jit(solution)/shard_map/ppermute | solution.py:220
  20.6 6.3 %collective-permute-start.3 = (bf16[256,256]{1,0:T(8,128)(2,1)S(1)}, bf16[256,256]{1,0:T(8,128)(2,1)S(1)}, u32[]{:S(2)}, u32[]{:S(2)}) collective-permute-start(bf16[256,256]{1,0:T(8,128)(2,1)S(1)} %collective-permute-done.2.refs_3_), channel_id=1, source_target_pairs={{0,56},{8,0},{16,8},{24,16},{32,24},{40,32},{48,40},{56,48},{64,12... | collective-permute-start | bytes 393224 | tf_op jit(solution)/shard_map/ppermute | solution.py:220
  23.8 0.7 copy-start.4
  26.9 5.9 %copy-start.3 = (bf16[32,4096]{1,0:T(8,128)(2,1)S(1)}, bf16[32,4096]{1,0:T(8,128)(2,1)}, u32[]{:S(2)}) copy-start(bf16[32,4096]{1,0:T(8,128)(2,1)} %cot_ref.1) | copy-start | bytes 786436
  27.8 20.8 %collective-permute-start.7 = (bf16[8,128,256]{2,1,0:T(8,128)(2,1)S(1)}, bf16[8,128,256]{2,1,0:T(8,128)(2,1)S(1)}, u32[]{:S(2)}, u32[]{:S(2)}) collective-permute-start(bf16[8,128,256]{2,1,0:T(8,128)(2,1)S(1)} %get-tuple-element.39), channel_id=1, source_target_pairs={{0,64},{8,72},{16,80},{24,88},{32,96},{40,104},{48,112},{56,120},{... | collective-permute-start | bytes 1572872 | tf_op jit(solution)/shard_map/ppermute | solution.py:220
  29.1 21.7 %collective-permute-start.8 = (bf16[8,128,256]{2,1,0:T(8,128)(2,1)S(1)}, bf16[8,128,256]{2,1,0:T(8,128)(2,1)S(1)}, u32[]{:S(2)}, u32[]{:S(2)}) collective-permute-start(bf16[8,128,256]{2,1,0:T(8,128)(2,1)S(1)} %get-tuple-element.40), channel_id=1, source_target_pairs={{0,128},{8,136},{16,144},{24,152},{32,160},{40,168},{48,176},{56,1... | collective-permute-start | bytes 1572872 | tf_op jit(solution)/shard_map/ppermute | solution.py:220
  31.8 21.9 %collective-permute-start.9 = (bf16[8,128,256]{2,1,0:T(8,128)(2,1)S(1)}, bf16[8,128,256]{2,1,0:T(8,128)(2,1)S(1)}, u32[]{:S(2)}, u32[]{:S(2)}) collective-permute-start(bf16[8,128,256]{2,1,0:T(8,128)(2,1)S(1)} %get-tuple-element.41), channel_id=1, source_target_pairs={{0,192},{8,200},{16,208},{24,216},{32,224},{40,232},{48,240},{56,2... | collective-permute-start | bytes 1572872 | tf_op jit(solution)/shard_map/ppermute | solution.py:220
  32.9 20.8 %copy-start = (bf16[256,512]{1,0:T(8,128)(2,1)S(1)}, bf16[256,512]{1,0:T(8,128)(2,1)}, u32[]{:S(2)}) copy-start(bf16[256,512]{1,0:T(8,128)(2,1)} %q_ref.1) | copy-start | bytes 786436
  32.9 20.8 %copy-start.1 = (bf16[256,128]{1,0:T(8,128)(2,1)S(1)}, bf16[256,128]{1,0:T(8,128)(2,1)}, u32[]{:S(2)}) copy-start(bf16[256,128]{1,0:T(8,128)(2,1)} %k_ref.1) | copy-start | bytes 196612
  61.4 8.3 %collective-permute-start.10 = (bf16[4,128,256]{2,1,0:T(8,128)(2,1)S(1)}, bf16[4,128,256]{2,1,0:T(8,128)(2,1)S(1)}, u32[]{:S(2)}, u32[]{:S(2)}) collective-permute-start(bf16[4,128,256]{2,1,0:T(8,128)(2,1)S(1)} %get-tuple-element.47), channel_id=1, source_target_pairs={{0,64},{8,72},{16,80},{24,88},{32,96},{40,104},{48,112},{56,120},{... | collective-permute-start | bytes 786440 | tf_op jit(solution)/shard_map/ppermute | solution.py:220
  63.3 14.1 %collective-permute-start.11 = (bf16[4,128,256]{2,1,0:T(8,128)(2,1)S(1)}, bf16[4,128,256]{2,1,0:T(8,128)(2,1)S(1)}, u32[]{:S(2)}, u32[]{:S(2)}) collective-permute-start(bf16[4,128,256]{2,1,0:T(8,128)(2,1)S(1)} %get-tuple-element.48), channel_id=1, source_target_pairs={{0,128},{8,136},{16,144},{24,152},{32,160},{40,168},{48,176},{56,1... | collective-permute-start | bytes 786440 | tf_op jit(solution)/shard_map/ppermute | solution.py:220
  66.0 12.0 %collective-permute-start.12 = (bf16[4,128,256]{2,1,0:T(8,128)(2,1)S(1)}, bf16[4,128,256]{2,1,0:T(8,128)(2,1)S(1)}, u32[]{:S(2)}, u32[]{:S(2)}) collective-permute-start(bf16[4,128,256]{2,1,0:T(8,128)(2,1)S(1)} %get-tuple-element.49), channel_id=1, source_target_pairs={{0,192},{8,200},{16,208},{24,216},{32,224},{40,232},{48,240},{56,2... | collective-permute-start | bytes 786440 | tf_op jit(solution)/shard_map/ppermute | solution.py:220
  66.0 25.0 %collective-permute-start.16 = (bf16[4,128,256]{2,1,0:T(8,128)(2,1)S(1)}, bf16[4,128,256]{2,1,0:T(8,128)(2,1)S(1)}, u32[]{:S(2)}, u32[]{:S(2)}) collective-permute-start(bf16[4,128,256]{2,1,0:T(8,128)(2,1)S(1)} %get-tuple-element.59), channel_id=1, source_target_pairs={{0,64},{8,72},{16,80},{24,88},{32,96},{40,104},{48,112},{56,120},{... | collective-permute-start | bytes 786440 | tf_op jit(solution)/shard_map/ppermute | solution.py:220
  67.4 25.1 %collective-permute-start.17 = (bf16[4,128,256]{2,1,0:T(8,128)(2,1)S(1)}, bf16[4,128,256]{2,1,0:T(8,128)(2,1)S(1)}, u32[]{:S(2)}, u32[]{:S(2)}) collective-permute-start(bf16[4,128,256]{2,1,0:T(8,128)(2,1)S(1)} %get-tuple-element.60), channel_id=1, source_target_pairs={{0,128},{8,136},{16,144},{24,152},{32,160},{40,168},{48,176},{56,1... | collective-permute-start | bytes 786440 | tf_op jit(solution)/shard_map/ppermute | solution.py:220
  69.6 22.9 %collective-permute-start.18 = (bf16[4,128,256]{2,1,0:T(8,128)(2,1)S(1)}, bf16[4,128,256]{2,1,0:T(8,128)(2,1)S(1)}, u32[]{:S(2)}, u32[]{:S(2)}) collective-permute-start(bf16[4,128,256]{2,1,0:T(8,128)(2,1)S(1)} %get-tuple-element.61), channel_id=1, source_target_pairs={{0,192},{8,200},{16,208},{24,216},{32,224},{40,232},{48,240},{56,2... | collective-permute-start | bytes 786440 | tf_op jit(solution)/shard_map/ppermute | solution.py:220
  78.9 18.2 %collective-permute-start.13 = (bf16[256,256]{1,0:T(8,128)(2,1)S(1)}, bf16[256,256]{1,0:T(8,128)(2,1)S(1)}, u32[]{:S(2)}, u32[]{:S(2)}) collective-permute-start(bf16[256,256]{1,0:T(8,128)(2,1)S(1)} %get-tuple-element.50), channel_id=1, source_target_pairs={{0,24},{8,32},{16,40},{24,48},{32,56},{40,0},{48,8},{56,16},{64,88... | collective-permute-start | bytes 393224 | tf_op jit(solution)/shard_map/ppermute | solution.py:220
  79.0 18.1 %collective-permute-start.14 = (bf16[256,256]{1,0:T(8,128)(2,1)S(1)}, bf16[256,256]{1,0:T(8,128)(2,1)S(1)}, u32[]{:S(2)}, u32[]{:S(2)}) collective-permute-start(bf16[256,256]{1,0:T(8,128)(2,1)S(1)} %get-tuple-element.51), channel_id=1, source_target_pairs={{0,40},{8,48},{16,56},{24,0},{32,8},{40,16},{48,24},{56,32},{64,10... | collective-permute-start | bytes 393224 | tf_op jit(solution)/shard_map/ppermute | solution.py:220
  83.5 16.4 %all-to-all-start.1 = ((bf16[8,32,512]{2,1,0:T(8,128)(2,1)}), bf16[8,32,512]{2,1,0:T(8,128)(2,1)S(1)}, u32[]{:S(2)}, u32[]{:S(2)}) async-start(bf16[8,32,512]{2,1,0:T(8,128)(2,1)} %bitcast.2), calls=%async_computation.1 | async-start | bytes 524288 | tf_op jit(solution)/shard_map/all_to_all | solution.py:291
  91.0 13.0 %collective-permute-start.15 = (bf16[256,256]{1,0:T(8,128)(2,1)S(1)}, bf16[256,256]{1,0:T(8,128)(2,1)S(1)}, u32[]{:S(2)}, u32[]{:S(2)}) collective-permute-start(bf16[256,256]{1,0:T(8,128)(2,1)S(1)} %get-tuple-element.52), channel_id=1, source_target_pairs={{0,32},{8,40},{16,48},{24,56},{32,0},{40,8},{48,16},{56,24},{64,96... | collective-permute-start | bytes 393224 | tf_op jit(solution)/shard_map/ppermute | solution.py:220
  93.5 10.4 %collective-permute-start.19 = (bf16[256,256]{1,0:T(8,128)(2,1)S(1)}, bf16[256,256]{1,0:T(8,128)(2,1)S(1)}, u32[]{:S(2)}, u32[]{:S(2)}) collective-permute-start(bf16[256,256]{1,0:T(8,128)(2,1)S(1)} %get-tuple-element.62), channel_id=1, source_target_pairs={{0,16},{8,24},{16,32},{24,40},{32,48},{40,56},{48,0},{56,8},{64,80... | collective-permute-start | bytes 393224 | tf_op jit(solution)/shard_map/ppermute | solution.py:220
  94.5 12.4 %collective-permute-start.20 = (bf16[256,256]{1,0:T(8,128)(2,1)S(1)}, bf16[256,256]{1,0:T(8,128)(2,1)S(1)}, u32[]{:S(2)}, u32[]{:S(2)}) collective-permute-start(bf16[256,256]{1,0:T(8,128)(2,1)S(1)} %get-tuple-element.63), channel_id=1, source_target_pairs={{0,48},{8,56},{16,0},{24,8},{32,16},{40,24},{48,32},{56,40},{64,11... | collective-permute-start | bytes 393224 | tf_op jit(solution)/shard_map/ppermute | solution.py:220
  97.2 11.7 %collective-permute-start.21 = (bf16[256,256]{1,0:T(8,128)(2,1)S(1)}, bf16[256,256]{1,0:T(8,128)(2,1)S(1)}, u32[]{:S(2)}, u32[]{:S(2)}) collective-permute-start(bf16[256,256]{1,0:T(8,128)(2,1)S(1)} %get-tuple-element.64), channel_id=1, source_target_pairs={{0,8},{8,16},{16,24},{24,32},{32,40},{40,48},{48,56},{56,0},{64,72... | collective-permute-start | bytes 393224 | tf_op jit(solution)/shard_map/ppermute | solution.py:220
  97.2 11.7 %collective-permute-start.22 = (bf16[256,256]{1,0:T(8,128)(2,1)S(1)}, bf16[256,256]{1,0:T(8,128)(2,1)S(1)}, u32[]{:S(2)}, u32[]{:S(2)}) collective-permute-start(bf16[256,256]{1,0:T(8,128)(2,1)S(1)} %get-tuple-element.65), channel_id=1, source_target_pairs={{0,56},{8,0},{16,8},{24,16},{32,24},{40,32},{48,40},{56,48},{64,12... | collective-permute-start | bytes 393224 | tf_op jit(solution)/shard_map/ppermute | solution.py:220

commit v5 on v4

--- a/solution.py
+++ b/solution.py
@@ -12,6 +12,7 @@
 SPAN = 128
 RING = 8
 HIDDEN = -1.0e30
+STEPS = (0, 1, 3, 2)
 GROUPS = ((3, 5, 4, 0), (2, 6, 1, 7))
 SCALE = 1.0 / math.sqrt(HEAD_DIM)
 SMEM = pl.BlockSpec(memory_space=pltpu.SMEM)
@@ -99,7 +100,7 @@
 
     @pl.when(slot == 0)
     def _():
-        for far, ref in enumerate(got):
+        for far, ref in zip(STEPS, got):
             pool[far] = ref[...]
 
     keys[:SPAN] = k_ref[...]
@@ -177,7 +178,7 @@
     for entry, (far, out) in enumerate(zip(group, outs)):
         owner = (at + far) % RING
         halves = [
-            table_ref[(mine - step + lines) % lines * pairs + mine * RING + owner] for step in range(lines)
+            table_ref[(mine - step + lines) % lines * pairs + mine * RING + owner] for step in STEPS
         ]
         parts = [back[entry].astype(f32) for back in backs]
         for side in range(2):
@@ -220,10 +221,7 @@
         return lax.ppermute(array, "seq", moves)
 
     def over_lines(parts):
-        got = list(parts)
-        for step in (1, lines - 1, *range(2, lines - 1)):
-            got[step] = shift(parts[step], step, 0)
-        return got
+        return [shift(parts[step], step, 0) if step else parts[step] for step in STEPS]
 
     own = jnp.concatenate([key_rows, value_rows], axis=1)
     below, above = [own], [own]

time: 110 us -> 108 us (0.982)
  waiting for transfers between devices: 27.4 us -> 19.1 us
  starting transfers between devices: 49.7 us -> 55.5 us
    all_to_all x1, starting transfers between devices: 7.47 us -> 16.5 us  [body(): lax.all_to_all(attended, 'head', split_axis=0, concat_axis=1, tiled=True)]
    ppermute x23, waiting for transfers between devices: 27.4 us -> 19.1 us  [shift(): return lax.ppermute(array, 'seq', moves)]
    ppermute x23, starting transfers between devices: 42.3 us -> 39 us  [shift(): return lax.ppermute(array, 'seq', moves)]
  transfers between devices with their start and end apart: 24 -> 24, of which waited for: 11 -> 10; matrix products, arithmetic and copies ran while one was open for 1% -> 1% of each run, Pallas kernels for 4% -> 4%
where the time goes in v5:
time: 108 us; the launch traced here: 107 us
  starting transfers between devices  55.5 us (51%)
  waiting for transfers between devices  19.1 us (18%)
  blocking collectives  15.7 us (15%)
  Pallas kernels  13.7 us (13%)
  local copies, waits for them, and re-layouts  2.4 us (2%)
    ppermute x23, starting transfers between devices, shift(): return lax.ppermute(array, 'seq', moves)  39 us
    ppermute x23, waiting for transfers between devices, shift(): return lax.ppermute(array, 'seq', moves)  19.1 us
    all_to_all x1, starting transfers between devices, body(): lax.all_to_all(attended, 'head', split_axis=0, concat_axis=1, tiled=True)  16.5 us
    all_to_all x1, blocking collectives, body(): lax.all_to_all(columns, 'head', split_axis=0, concat_axis=0, tiled=True)  15.7 us
    pallas_call x1, Pallas kernels, body(): pl.pallas_call(attend_kernel, grid=(2,), out_shape=[shape(queries.shape,...  7.72 us
    pallas_call x1, Pallas kernels, body(): pl.pallas_call(route_kernel, out_shape=(shape((2 * picked,), jnp.int32),...  2.44 us
  transfers between devices with their start and end apart: 24, of which 10 were waited for; matrix products, arithmetic and copies ran while one was open for 1% of the time, Pallas kernels for 4%

profile of v5, /device:TPU:1, one launch (start us, length us, event | category | flops | bytes accessed | tf_op | source)
XLA Modules:
  0.0 107.3 jit_solution(15121397116687349359)
XLA Ops:
  0.6 0.9 constant_dynamic-update-slice_fusion.1
  1.6 0.0 copy-start.5
  1.6 6.5 %collective-permute-start = (bf16[256,256]{1,0:T(8,128)(2,1)S(1)}, bf16[256,256]{1,0:T(8,128)(2,1)S(1)}, u32[]{:S(2)}, u32[]{:S(2)}) collective-permute-start(bf16[256,256]{1,0:T(8,128)(2,1)S(1)} %constant_dynamic-update-slice_fusion.refs_0_), channel_id=1, source_target_pairs={{0,56},{8,0},{16,8},{24,16},{32,24},{40,32},{48,40},{56,48},{64,12... | collective-permute-start | bytes 393224 | tf_op jit(solution)/shard_map/ppermute | solution.py:221
  8.1 0.0 collective-permute-start.4
  8.1 2.2 %collective-permute-done.refs_1_ = bf16[256,256]{1,0:T(8,128)(2,1)S(1)} collective-permute-done((bf16[256,256]{1,0:T(8,128)(2,1)S(1)}, bf16[256,256]{1,0:T(8,128)(2,1)S(1)}, u32[]{:S(2)}, u32[]{:S(2)}) %collective-permute-start) | collective-permute-done | bytes 131104 | tf_op jit(solution)/shard_map/ppermute | solution.py:221
  10.2 3.4 %collective-permute-start.1 = (bf16[256,256]{1,0:T(8,128)(2,1)S(1)}, bf16[256,256]{1,0:T(8,128)(2,1)S(1)}, u32[]{:S(2)}, u32[]{:S(2)}) collective-permute-start(bf16[256,256]{1,0:T(8,128)(2,1)S(1)} %collective-permute-done.refs_1_), channel_id=1, source_target_pairs={{0,56},{8,0},{16,8},{24,16},{32,24},{40,32},{48,40},{56,48},{64,12... | collective-permute-start | bytes 393224 | tf_op jit(solution)/shard_map/ppermute | solution.py:221
  13.6 0.0 collective-permute-done.4.refs_7_
  13.6 1.9 %collective-permute-done.1.refs_2_ = bf16[256,256]{1,0:T(8,128)(2,1)S(1)} collective-permute-done((bf16[256,256]{1,0:T(8,128)(2,1)S(1)}, bf16[256,256]{1,0:T(8,128)(2,1)S(1)}, u32[]{:S(2)}, u32[]{:S(2)}) %collective-permute-start.1) | collective-permute-done | bytes 131104 | tf_op jit(solution)/shard_map/ppermute | solution.py:221
  15.6 3.1 %collective-permute-start.2 = (bf16[256,256]{1,0:T(8,128)(2,1)S(1)}, bf16[256,256]{1,0:T(8,128)(2,1)S(1)}, u32[]{:S(2)}, u32[]{:S(2)}) collective-permute-start(bf16[256,256]{1,0:T(8,128)(2,1)S(1)} %collective-permute-done.1.refs_2_), channel_id=1, source_target_pairs={{0,56},{8,0},{16,8},{24,16},{32,24},{40,32},{48,40},{56,48},{64,12... | collective-permute-start | bytes 393224 | tf_op jit(solution)/shard_map/ppermute | solution.py:221
  18.7 0.0 collective-permute-done.5.refs_6_
  18.7 1.9 %collective-permute-done.2.refs_3_ = bf16[256,256]{1,0:T(8,128)(2,1)S(1)} collective-permute-done((bf16[256,256]{1,0:T(8,128)(2,1)S(1)}, bf16[256,256]{1,0:T(8,128)(2,1)S(1)}, u32[]{:S(2)}, u32[]{:S(2)}) %collective-permute-start.2) | collective-permute-done | bytes 131104 | tf_op jit(solution)/shard_map/ppermute | solution.py:221
  20.6 3.1 %collective-permute-start.3 = (bf16[256,256]{1,0:T(8,128)(2,1)S(1)}, bf16[256,256]{1,0:T(8,128)(2,1)S(1)}, u32[]{:S(2)}, u32[]{:S(2)}) collective-permute-start(bf16[256,256]{1,0:T(8,128)(2,1)S(1)} %collective-permute-done.2.refs_3_), channel_id=1, source_target_pairs={{0,56},{8,0},{16,8},{24,16},{32,24},{40,32},{48,40},{56,48},{64,12... | collective-permute-start | bytes 393224 | tf_op jit(solution)/shard_map/ppermute | solution.py:221
  23.7 0.1 copy.14.lists_ref
  23.8 0.7 copy-done.4
  24.4 2.4 %route.1 = (s32[16]{0:T(128)S(1)}, s32[129]{0:T(256)S(1)}) custom-call(s32[1]{0:T(128)} %bitcast.me_ref, s32[64]{0:T(128)S(1)} %copy-done.4, s32[64,8]{1,0:T(8,128)S(1)} %copy.14.lists_ref), custom_call_target="tpu_custom_call" | custom-call | tf_op jit(solution)/shard_map/route/pallas_call | solution.py:232
  26.9 0.0 collective-permute-done.3.refs_4_
  26.9 0.0 copy-start.3
  26.9 0.8 line.1
  27.8 1.4 %collective-permute-start.7 = (bf16[8,128,256]{2,1,0:T(8,128)(2,1)S(1)}, bf16[8,128,256]{2,1,0:T(8,128)(2,1)S(1)}, u32[]{:S(2)}, u32[]{:S(2)}) collective-permute-start(bf16[8,128,256]{2,1,0:T(8,128)(2,1)S(1)} %get-tuple-element.39), channel_id=1, source_target_pairs={{0,64},{8,72},{16,80},{24,88},{32,96},{40,104},{48,112},{56,120},{... | collective-permute-start | bytes 1572872 | tf_op jit(solution)/shard_map/ppermute | solution.py:221
  29.1 1.5 %collective-permute-start.8 = (bf16[8,128,256]{2,1,0:T(8,128)(2,1)S(1)}, bf16[8,128,256]{2,1,0:T(8,128)(2,1)S(1)}, u32[]{:S(2)}, u32[]{:S(2)}) collective-permute-start(bf16[8,128,256]{2,1,0:T(8,128)(2,1)S(1)} %get-tuple-element.40), channel_id=1, source_target_pairs={{0,192},{8,200},{16,208},{24,216},{32,224},{40,232},{48,240},{56,2... | collective-permute-start | bytes 1572872 | tf_op jit(solution)/shard_map/ppermute | solution.py:221
  30.7 1.6 %collective-permute-start.9 = (bf16[8,128,256]{2,1,0:T(8,128)(2,1)S(1)}, bf16[8,128,256]{2,1,0:T(8,128)(2,1)S(1)}, u32[]{:S(2)}, u32[]{:S(2)}) collective-permute-start(bf16[8,128,256]{2,1,0:T(8,128)(2,1)S(1)} %get-tuple-element.41), channel_id=1, source_target_pairs={{0,128},{8,136},{16,144},{24,152},{32,160},{40,168},{48,176},{56,1... | collective-permute-start | bytes 1572872 | tf_op jit(solution)/shard_map/ppermute | solution.py:221
  32.2 0.0 copy-start
  32.3 0.0 copy-start.1
  32.3 15.7 %all_to_all.24 = bf16[8,32,512]{2,1,0:T(8,128)(2,1)S(1)} all-to-all(bf16[8,32,512]{2,1,0:T(8,128)(2,1)S(1)} %columns.1), channel_id=1, replica_groups=mesh['seq'=32,'head'=8] {'head'}, dimensions={0} | all-to-all | bytes 524288 | tf_op jit(solution)/shard_map/all_to_all | solution.py:258
  48.0 2.8 %collective-permute-done.9.refs_3_ = bf16[8,128,256]{2,1,0:T(8,128)(2,1)S(1)} collective-permute-done((bf16[8,128,256]{2,1,0:T(8,128)(2,1)S(1)}, bf16[8,128,256]{2,1,0:T(8,128)(2,1)S(1)}, u32[]{:S(2)}, u32[]{:S(2)}) %collective-permute-start.9) | collective-permute-done | bytes 524320 | tf_op jit(solution)/shard_map/ppermute | solution.py:221
  50.8 7.7 %attend.1 = (bf16[256,512]{1,0:T(8,128)(2,1)}, bf16[256,512]{1,0:T(8,128)(2,1)}, f32[256,128]{1,0:T(8,128)S(1)}, f32[256,128]{1,0:T(8,128)S(1)}, bf16[4,128,256]...) custom-call(s32[1]{0:T(128)} %bitcast.me_ref, ...), custom_call_target="tpu_custom_call" | custom-call | tf_op jit(solution)/shard_map/attend/pallas_call | solution.py:265
  58.5 0.5 collective-permute-start.10
  59.0 2.2 %collective-permute-start.11 = (bf16[4,128,256]{2,1,0:T(8,128)(2,1)S(1)}, bf16[4,128,256]{2,1,0:T(8,128)(2,1)S(1)}, u32[]{:S(2)}, u32[]{:S(2)}) collective-permute-start(bf16[4,128,256]{2,1,0:T(8,128)(2,1)S(1)} %get-tuple-element.48), channel_id=1, source_target_pairs={{0,192},{8,200},{16,208},{24,216},{32,224},{40,232},{48,240},{56,2... | collective-permute-start | bytes 786440 | tf_op jit(solution)/shard_map/ppermute | solution.py:221
  61.2 0.6 collective-permute-start.16
  61.8 2.1 %collective-permute-start.17 = (bf16[4,128,256]{2,1,0:T(8,128)(2,1)S(1)}, bf16[4,128,256]{2,1,0:T(8,128)(2,1)S(1)}, u32[]{:S(2)}, u32[]{:S(2)}) collective-permute-start(bf16[4,128,256]{2,1,0:T(8,128)(2,1)S(1)} %get-tuple-element.60), channel_id=1, source_target_pairs={{0,192},{8,200},{16,208},{24,216},{32,224},{40,232},{48,240},{56,2... | collective-permute-start | bytes 786440 | tf_op jit(solution)/shard_map/ppermute | solution.py:221
  63.9 1.1 %collective-permute-done.10.refs_1_ = bf16[4,128,256]{2,1,0:T(8,128)(2,1)S(1)} collective-permute-done((bf16[4,128,256]{2,1,0:T(8,128)(2,1)S(1)}, bf16[4,128,256]{2,1,0:T(8,128)(2,1)S(1)}, u32[]{:S(2)}, u32[]{:S(2)}) %collective-permute-start.10) | collective-permute-done | bytes 262176 | tf_op jit(solution)/shard_map/ppermute | solution.py:221
  65.0 0.7 collective-permute-start.18
  65.7 1.7 %collective-permute-done.11.refs_2_ = bf16[4,128,256]{2,1,0:T(8,128)(2,1)S(1)} collective-permute-done((bf16[4,128,256]{2,1,0:T(8,128)(2,1)S(1)}, bf16[4,128,256]{2,1,0:T(8,128)(2,1)S(1)}, u32[]{:S(2)}, u32[]{:S(2)}) %collective-permute-start.11) | collective-permute-done | bytes 262176 | tf_op jit(solution)/shard_map/ppermute | solution.py:221
  67.3 0.8 collective-permute-done.12.refs_3_
  68.2 1.0 line_sum.2
  69.1 0.2 collective-permute-start.13
  69.4 4.3 %collective-permute-start.14 = (bf16[256,256]{1,0:T(8,128)(2,1)S(1)}, bf16[256,256]{1,0:T(8,128)(2,1)S(1)}, u32[]{:S(2)}, u32[]{:S(2)}) collective-permute-start(bf16[256,256]{1,0:T(8,128)(2,1)S(1)} %get-tuple-element.51), channel_id=1, source_target_pairs={{0,40},{8,48},{16,56},{24,0},{32,8},{40,16},{48,24},{56,32},{64,10... | collective-permute-start | bytes 393224 | tf_op jit(solution)/shard_map/ppermute | solution.py:221
  73.7 16.5 %all-to-all-start.1 = ((bf16[8,32,512]{2,1,0:T(8,128)(2,1)}), bf16[8,32,512]{2,1,0:T(8,128)(2,1)S(1)}, u32[]{:S(2)}, u32[]{:S(2)}) async-start(bf16[8,32,512]{2,1,0:T(8,128)(2,1)} %bitcast.2), calls=%async_computation.1 | async-start | bytes 524288 | tf_op jit(solution)/shard_map/all_to_all | solution.py:289
  90.2 1.6 %collective-permute-start.15 = (bf16[256,256]{1,0:T(8,128)(2,1)S(1)}, bf16[256,256]{1,0:T(8,128)(2,1)S(1)}, u32[]{:S(2)}, u32[]{:S(2)}) collective-permute-start(bf16[256,256]{1,0:T(8,128)(2,1)S(1)} %get-tuple-element.52), channel_id=1, source_target_pairs={{0,32},{8,40},{16,48},{24,56},{32,0},{40,8},{48,16},{56,24},{64,96... | collective-permute-start | bytes 393224 | tf_op jit(solution)/shard_map/ppermute | solution.py:221
  91.8 1.0 line_sum.3
  92.8 0.5 collective-permute-start.19
  93.3 3.2 %collective-permute-start.20 = (bf16[256,256]{1,0:T(8,128)(2,1)S(1)}, bf16[256,256]{1,0:T(8,128)(2,1)S(1)}, u32[]{:S(2)}, u32[]{:S(2)}) collective-permute-start(bf16[256,256]{1,0:T(8,128)(2,1)S(1)} %get-tuple-element.63), channel_id=1, source_target_pairs={{0,48},{8,56},{16,0},{24,8},{32,16},{40,24},{48,32},{56,40},{64,11... | collective-permute-start | bytes 393224 | tf_op jit(solution)/shard_map/ppermute | solution.py:221
  96.5 2.7 %collective-permute-start.22 = (bf16[256,256]{1,0:T(8,128)(2,1)S(1)}, bf16[256,256]{1,0:T(8,128)(2,1)S(1)}, u32[]{:S(2)}, u32[]{:S(2)}) collective-permute-start(bf16[256,256]{1,0:T(8,128)(2,1)S(1)} %get-tuple-element.65), channel_id=1, source_target_pairs={{0,56},{8,0},{16,8},{24,16},{32,24},{40,32},{48,40},{56,48},{64,12... | collective-permute-start | bytes 393224 | tf_op jit(solution)/shard_map/ppermute | solution.py:221
  99.1 0.7 copy.16
  99.9 5.0 %collective-permute-done.15.refs_2_ = bf16[256,256]{1,0:T(8,128)(2,1)S(1)} collective-permute-done((bf16[256,256]{1,0:T(8,128)(2,1)S(1)}, bf16[256,256]{1,0:T(8,128)(2,1)S(1)}, u32[]{:S(2)}, u32[]{:S(2)}) %collective-permute-start.15) | collective-permute-done | bytes 131104 | tf_op jit(solution)/shard_map/ppermute | solution.py:221
  104.9 0.6 collective-permute-done.20.refs_5_
  105.5 1.0 collective-permute-done.21.refs_6_
  106.5 0.8 add.1
  (25 shorter events, 0.1 us)
Async XLA Ops:
  0.6 0.9 copy-start.2
  1.6 22.1 %copy-start.5 = (s32[64,8]{0,1:T(8,128)S(1)}, s32[64,8]{0,1:T(8,128)}, u32[]{:S(2)}) copy-start(s32[64,8]{0,1:T(8,128)} %param.10) | copy-start | bytes 6148
  1.6 8.6 %collective-permute-start = (bf16[256,256]{1,0:T(8,128)(2,1)S(1)}, bf16[256,256]{1,0:T(8,128)(2,1)S(1)}, u32[]{:S(2)}, u32[]{:S(2)}) collective-permute-start(bf16[256,256]{1,0:T(8,128)(2,1)S(1)} %constant_dynamic-update-slice_fusion.refs_0_), channel_id=1, source_target_pairs={{0,56},{8,0},{16,8},{24,16},{32,24},{40,32},{48,40},{56,48},{64,12... | collective-permute-start | bytes 393224 | tf_op jit(solution)/shard_map/ppermute | solution.py:221
  8.1 5.6 %collective-permute-start.4 = (bf16[256,256]{1,0:T(8,128)(2,1)S(1)}, bf16[256,256]{1,0:T(8,128)(2,1)S(1)}, u32[]{:S(2)}, u32[]{:S(2)}) collective-permute-start(bf16[256,256]{1,0:T(8,128)(2,1)S(1)} %constant_dynamic-update-slice_fusion.refs_0_), channel_id=1, source_target_pairs={{0,8},{8,16},{16,24},{24,32},{32,40},{40,48},{48,56},{56,0},{64,72... | collective-permute-start | bytes 393224 | tf_op jit(solution)/shard_map/ppermute | solution.py:221
  10.2 5.4 %collective-permute-start.1 = (bf16[256,256]{1,0:T(8,128)(2,1)S(1)}, bf16[256,256]{1,0:T(8,128)(2,1)S(1)}, u32[]{:S(2)}, u32[]{:S(2)}) collective-permute-start(bf16[256,256]{1,0:T(8,128)(2,1)S(1)} %collective-permute-done.refs_1_), channel_id=1, source_target_pairs={{0,56},{8,0},{16,8},{24,16},{32,24},{40,32},{48,40},{56,48},{64,12... | collective-permute-start | bytes 393224 | tf_op jit(solution)/shard_map/ppermute | solution.py:221
  13.6 5.0 %collective-permute-start.5 = (bf16[256,256]{1,0:T(8,128)(2,1)S(1)}, bf16[256,256]{1,0:T(8,128)(2,1)S(1)}, u32[]{:S(2)}, u32[]{:S(2)}) collective-permute-start(bf16[256,256]{1,0:T(8,128)(2,1)S(1)} %collective-permute-done.4.refs_7_), channel_id=1, source_target_pairs={{0,8},{8,16},{16,24},{24,32},{32,40},{40,48},{48,56},{56,0},{64,72... | collective-permute-start | bytes 393224 | tf_op jit(solution)/shard_map/ppermute | solution.py:221
  15.6 5.0 %collective-permute-start.2 = (bf16[256,256]{1,0:T(8,128)(2,1)S(1)}, bf16[256,256]{1,0:T(8,128)(2,1)S(1)}, u32[]{:S(2)}, u32[]{:S(2)}) collective-permute-start(bf16[256,256]{1,0:T(8,128)(2,1)S(1)} %collective-permute-done.1.refs_2_), channel_id=1, source_target_pairs={{0,56},{8,0},{16,8},{24,16},{32,24},{40,32},{48,40},{56,48},{64,12... | collective-permute-start | bytes 393224 | tf_op jit(solution)/shard_map/ppermute | solution.py:221
  18.7 8.2 %collective-permute-start.6 = (bf16[256,256]{1,0:T(8,128)(2,1)S(1)}, bf16[256,256]{1,0:T(8,128)(2,1)S(1)}, u32[]{:S(2)}, u32[]{:S(2)}) collective-permute-start(bf16[256,256]{1,0:T(8,128)(2,1)S(1)} %collective-permute-done.5.refs_6_), channel_id=1, source_target_pairs={{0,8},{8,16},{16,24},{24,32},{32,40},{40,48},{48,56},{56,0},{64,72... | collective-permute-start | bytes 393224 | tf_op jit(solution)/shard_map/ppermute | solution.py:221
  20.6 6.3 %collective-permute-start.3 = (bf16[256,256]{1,0:T(8,128)(2,1)S(1)}, bf16[256,256]{1,0:T(8,128)(2,1)S(1)}, u32[]{:S(2)}, u32[]{:S(2)}) collective-permute-start(bf16[256,256]{1,0:T(8,128)(2,1)S(1)} %collective-permute-done.2.refs_3_), channel_id=1, source_target_pairs={{0,56},{8,0},{16,8},{24,16},{32,24},{40,32},{48,40},{56,48},{64,12... | collective-permute-start | bytes 393224 | tf_op jit(solution)/shard_map/ppermute | solution.py:221
  23.8 0.7 copy-start.4
  26.9 5.3 %copy-start.3 = (bf16[32,4096]{1,0:T(8,128)(2,1)S(1)}, bf16[32,4096]{1,0:T(8,128)(2,1)}, u32[]{:S(2)}) copy-start(bf16[32,4096]{1,0:T(8,128)(2,1)} %cot_ref.1) | copy-start | bytes 786436
  27.8 20.2 %collective-permute-start.7 = (bf16[8,128,256]{2,1,0:T(8,128)(2,1)S(1)}, bf16[8,128,256]{2,1,0:T(8,128)(2,1)S(1)}, u32[]{:S(2)}, u32[]{:S(2)}) collective-permute-start(bf16[8,128,256]{2,1,0:T(8,128)(2,1)S(1)} %get-tuple-element.39), channel_id=1, source_target_pairs={{0,64},{8,72},{16,80},{24,88},{32,96},{40,104},{48,112},{56,120},{... | collective-permute-start | bytes 1572872 | tf_op jit(solution)/shard_map/ppermute | solution.py:221
  29.1 18.8 %collective-permute-start.8 = (bf16[8,128,256]{2,1,0:T(8,128)(2,1)S(1)}, bf16[8,128,256]{2,1,0:T(8,128)(2,1)S(1)}, u32[]{:S(2)}, u32[]{:S(2)}) collective-permute-start(bf16[8,128,256]{2,1,0:T(8,128)(2,1)S(1)} %get-tuple-element.40), channel_id=1, source_target_pairs={{0,192},{8,200},{16,208},{24,216},{32,224},{40,232},{48,240},{56,2... | collective-permute-start | bytes 1572872 | tf_op jit(solution)/shard_map/ppermute | solution.py:221
  30.7 20.2 %collective-permute-start.9 = (bf16[8,128,256]{2,1,0:T(8,128)(2,1)S(1)}, bf16[8,128,256]{2,1,0:T(8,128)(2,1)S(1)}, u32[]{:S(2)}, u32[]{:S(2)}) collective-permute-start(bf16[8,128,256]{2,1,0:T(8,128)(2,1)S(1)} %get-tuple-element.41), channel_id=1, source_target_pairs={{0,128},{8,136},{16,144},{24,152},{32,160},{40,168},{48,176},{56,1... | collective-permute-start | bytes 1572872 | tf_op jit(solution)/shard_map/ppermute | solution.py:221
  32.2 18.6 %copy-start = (bf16[256,512]{1,0:T(8,128)(2,1)S(1)}, bf16[256,512]{1,0:T(8,128)(2,1)}, u32[]{:S(2)}) copy-start(bf16[256,512]{1,0:T(8,128)(2,1)} %q_ref.1) | copy-start | bytes 786436
  32.3 18.6 %copy-start.1 = (bf16[256,128]{1,0:T(8,128)(2,1)S(1)}, bf16[256,128]{1,0:T(8,128)(2,1)}, u32[]{:S(2)}) copy-start(bf16[256,128]{1,0:T(8,128)(2,1)} %k_ref.1) | copy-start | bytes 196612
  58.5 6.4 %collective-permute-start.10 = (bf16[4,128,256]{2,1,0:T(8,128)(2,1)S(1)}, bf16[4,128,256]{2,1,0:T(8,128)(2,1)S(1)}, u32[]{:S(2)}, u32[]{:S(2)}) collective-permute-start(bf16[4,128,256]{2,1,0:T(8,128)(2,1)S(1)} %get-tuple-element.47), channel_id=1, source_target_pairs={{0,64},{8,72},{16,80},{24,88},{32,96},{40,104},{48,112},{56,120},{... | collective-permute-start | bytes 786440 | tf_op jit(solution)/shard_map/ppermute | solution.py:221
  59.0 8.3 %collective-permute-start.11 = (bf16[4,128,256]{2,1,0:T(8,128)(2,1)S(1)}, bf16[4,128,256]{2,1,0:T(8,128)(2,1)S(1)}, u32[]{:S(2)}, u32[]{:S(2)}) collective-permute-start(bf16[4,128,256]{2,1,0:T(8,128)(2,1)S(1)} %get-tuple-element.48), channel_id=1, source_target_pairs={{0,192},{8,200},{16,208},{24,216},{32,224},{40,232},{48,240},{56,2... | collective-permute-start | bytes 786440 | tf_op jit(solution)/shard_map/ppermute | solution.py:221
  61.2 6.9 %collective-permute-start.12 = (bf16[4,128,256]{2,1,0:T(8,128)(2,1)S(1)}, bf16[4,128,256]{2,1,0:T(8,128)(2,1)S(1)}, u32[]{:S(2)}, u32[]{:S(2)}) collective-permute-start(bf16[4,128,256]{2,1,0:T(8,128)(2,1)S(1)} %get-tuple-element.49), channel_id=1, source_target_pairs={{0,128},{8,136},{16,144},{24,152},{32,160},{40,168},{48,176},{56,1... | collective-permute-start | bytes 786440 | tf_op jit(solution)/shard_map/ppermute | solution.py:221
  61.2 29.0 %collective-permute-start.16 = (bf16[4,128,256]{2,1,0:T(8,128)(2,1)S(1)}, bf16[4,128,256]{2,1,0:T(8,128)(2,1)S(1)}, u32[]{:S(2)}, u32[]{:S(2)}) collective-permute-start(bf16[4,128,256]{2,1,0:T(8,128)(2,1)S(1)} %get-tuple-element.59), channel_id=1, source_target_pairs={{0,64},{8,72},{16,80},{24,88},{32,96},{40,104},{48,112},{56,120},{... | collective-permute-start | bytes 786440 | tf_op jit(solution)/shard_map/ppermute | solution.py:221
  61.8 30.0 %collective-permute-start.17 = (bf16[4,128,256]{2,1,0:T(8,128)(2,1)S(1)}, bf16[4,128,256]{2,1,0:T(8,128)(2,1)S(1)}, u32[]{:S(2)}, u32[]{:S(2)}) collective-permute-start(bf16[4,128,256]{2,1,0:T(8,128)(2,1)S(1)} %get-tuple-element.60), channel_id=1, source_target_pairs={{0,192},{8,200},{16,208},{24,216},{32,224},{40,232},{48,240},{56,2... | collective-permute-start | bytes 786440 | tf_op jit(solution)/shard_map/ppermute | solution.py:221
  65.0 26.8 %collective-permute-start.18 = (bf16[4,128,256]{2,1,0:T(8,128)(2,1)S(1)}, bf16[4,128,256]{2,1,0:T(8,128)(2,1)S(1)}, u32[]{:S(2)}, u32[]{:S(2)}) collective-permute-start(bf16[4,128,256]{2,1,0:T(8,128)(2,1)S(1)} %get-tuple-element.61), channel_id=1, source_target_pairs={{0,128},{8,136},{16,144},{24,152},{32,160},{40,168},{48,176},{56,1... | collective-permute-start | bytes 786440 | tf_op jit(solution)/shard_map/ppermute | solution.py:221
  69.1 27.3 %collective-permute-start.13 = (bf16[256,256]{1,0:T(8,128)(2,1)S(1)}, bf16[256,256]{1,0:T(8,128)(2,1)S(1)}, u32[]{:S(2)}, u32[]{:S(2)}) collective-permute-start(bf16[256,256]{1,0:T(8,128)(2,1)S(1)} %get-tuple-element.50), channel_id=1, source_target_pairs={{0,24},{8,32},{16,40},{24,48},{32,56},{40,0},{48,8},{56,16},{64,88... | collective-permute-start | bytes 393224 | tf_op jit(solution)/shard_map/ppermute | solution.py:221
  69.4 27.1 %collective-permute-start.14 = (bf16[256,256]{1,0:T(8,128)(2,1)S(1)}, bf16[256,256]{1,0:T(8,128)(2,1)S(1)}, u32[]{:S(2)}, u32[]{:S(2)}) collective-permute-start(bf16[256,256]{1,0:T(8,128)(2,1)S(1)} %get-tuple-element.51), channel_id=1, source_target_pairs={{0,40},{8,48},{16,56},{24,0},{32,8},{40,16},{48,24},{56,32},{64,10... | collective-permute-start | bytes 393224 | tf_op jit(solution)/shard_map/ppermute | solution.py:221
  73.7 25.4 %all-to-all-start.1 = ((bf16[8,32,512]{2,1,0:T(8,128)(2,1)}), bf16[8,32,512]{2,1,0:T(8,128)(2,1)S(1)}, u32[]{:S(2)}, u32[]{:S(2)}) async-start(bf16[8,32,512]{2,1,0:T(8,128)(2,1)} %bitcast.2), calls=%async_computation.1 | async-start | bytes 524288 | tf_op jit(solution)/shard_map/all_to_all | solution.py:289
  90.2 14.7 %collective-permute-start.15 = (bf16[256,256]{1,0:T(8,128)(2,1)S(1)}, bf16[256,256]{1,0:T(8,128)(2,1)S(1)}, u32[]{:S(2)}, u32[]{:S(2)}) collective-permute-start(bf16[256,256]{1,0:T(8,128)(2,1)S(1)} %get-tuple-element.52), channel_id=1, source_target_pairs={{0,32},{8,40},{16,48},{24,56},{32,0},{40,8},{48,16},{56,24},{64,96... | collective-permute-start | bytes 393224 | tf_op jit(solution)/shard_map/ppermute | solution.py:221
  92.8 12.1 %collective-permute-start.19 = (bf16[256,256]{1,0:T(8,128)(2,1)S(1)}, bf16[256,256]{1,0:T(8,128)(2,1)S(1)}, u32[]{:S(2)}, u32[]{:S(2)}) collective-permute-start(bf16[256,256]{1,0:T(8,128)(2,1)S(1)} %get-tuple-element.62), channel_id=1, source_target_pairs={{0,16},{8,24},{16,32},{24,40},{32,48},{40,56},{48,0},{56,8},{64,80... | collective-permute-start | bytes 393224 | tf_op jit(solution)/shard_map/ppermute | solution.py:221
  93.3 12.2 %collective-permute-start.20 = (bf16[256,256]{1,0:T(8,128)(2,1)S(1)}, bf16[256,256]{1,0:T(8,128)(2,1)S(1)}, u32[]{:S(2)}, u32[]{:S(2)}) collective-permute-start(bf16[256,256]{1,0:T(8,128)(2,1)S(1)} %get-tuple-element.63), channel_id=1, source_target_pairs={{0,48},{8,56},{16,0},{24,8},{32,16},{40,24},{48,32},{56,40},{64,11... | collective-permute-start | bytes 393224 | tf_op jit(solution)/shard_map/ppermute | solution.py:221
  96.5 10.0 %collective-permute-start.21 = (bf16[256,256]{1,0:T(8,128)(2,1)S(1)}, bf16[256,256]{1,0:T(8,128)(2,1)S(1)}, u32[]{:S(2)}, u32[]{:S(2)}) collective-permute-start(bf16[256,256]{1,0:T(8,128)(2,1)S(1)} %get-tuple-element.64), channel_id=1, source_target_pairs={{0,8},{8,16},{16,24},{24,32},{32,40},{40,48},{48,56},{56,0},{64,72... | collective-permute-start | bytes 393224 | tf_op jit(solution)/shard_map/ppermute | solution.py:221
  96.5 10.0 %collective-permute-start.22 = (bf16[256,256]{1,0:T(8,128)(2,1)S(1)}, bf16[256,256]{1,0:T(8,128)(2,1)S(1)}, u32[]{:S(2)}, u32[]{:S(2)}) collective-permute-start(bf16[256,256]{1,0:T(8,128)(2,1)S(1)} %get-tuple-element.65), channel_id=1, source_target_pairs={{0,56},{8,0},{16,8},{24,16},{32,24},{40,32},{48,40},{56,48},{64,12... | collective-permute-start | bytes 393224 | tf_op jit(solution)/shard_map/ppermute | solution.py:221

commit v6 on v5

--- a/solution.py
+++ b/solution.py
@@ -13,7 +13,7 @@
 RING = 8
 HIDDEN = -1.0e30
 STEPS = (0, 1, 3, 2)
-GROUPS = ((3, 5, 4, 0), (2, 6, 1, 7))
+GROUPS = ((3, 5, 4, 0), (1, 7, 2, 6))
 SCALE = 1.0 / math.sqrt(HEAD_DIM)
 SMEM = pl.BlockSpec(memory_space=pltpu.SMEM)
 VMEM = pl.BlockSpec(memory_space=pltpu.VMEM)

time: 108 us -> 109 us (level)
  waiting for transfers between devices: 19.1 us -> 20.9 us
    ppermute x23, waiting for transfers between devices: 19.1 us -> 20.9 us  [shift(): return lax.ppermute(array, 'seq', moves)]
where the time goes in v6:
time: 109 us
  starting transfers between devices  55.6 us (51%)
  waiting for transfers between devices  20.9 us (19%)
  blocking collectives  15.7 us (14%)
  Pallas kernels  13.7 us (13%)
  local copies, waits for them, and re-layouts  2.4 us (2%)
    ppermute x23, starting transfers between devices, shift(): return lax.ppermute(array, 'seq', moves)  39 us
    ppermute x23, waiting for transfers between devices, shift(): return lax.ppermute(array, 'seq', moves)  20.9 us
    all_to_all x1, starting transfers between devices, body(): lax.all_to_all(attended, 'head', split_axis=0, concat_axis=1, tiled=True)  16.5 us
    all_to_all x1, blocking collectives, body(): lax.all_to_all(columns, 'head', split_axis=0, concat_axis=0, tiled=True)  15.7 us
    pallas_call x1, Pallas kernels, body(): pl.pallas_call(attend_kernel, grid=(2,), out_shape=[shape(queries.shape,...  7.68 us
    pallas_call x1, Pallas kernels, body(): pl.pallas_call(route_kernel, out_shape=(shape((2 * picked,), jnp.int32),...  2.44 us
  transfers between devices with their start and end apart: 24, of which 10 were waited for; matrix products, arithmetic and copies ran while one was open for 1% of the time, Pallas kernels for 4%

profile of v6, /device:TPU:1, one launch (start us, length us, event | category | flops | bytes accessed | tf_op | source)
XLA Modules:
  0.0 109.0 jit_solution(1628021411643100198)
XLA Ops:
  0.6 0.9 constant_dynamic-update-slice_fusion.1
  1.6 0.0 copy-start.5
  1.6 6.5 %collective-permute-start = (bf16[256,256]{1,0:T(8,128)(2,1)S(1)}, bf16[256,256]{1,0:T(8,128)(2,1)S(1)}, u32[]{:S(2)}, u32[]{:S(2)}) collective-permute-start(bf16[256,256]{1,0:T(8,128)(2,1)S(1)} %constant_dynamic-update-slice_fusion.refs_0_), channel_id=1, source_target_pairs={{0,56},{8,0},{16,8},{24,16},{32,24},{40,32},{48,40},{56,48},{64,12... | collective-permute-start | bytes 393224 | tf_op jit(solution)/shard_map/ppermute | solution.py:221
  8.1 0.0 collective-permute-start.4
  8.1 2.2 %collective-permute-done.refs_1_ = bf16[256,256]{1,0:T(8,128)(2,1)S(1)} collective-permute-done((bf16[256,256]{1,0:T(8,128)(2,1)S(1)}, bf16[256,256]{1,0:T(8,128)(2,1)S(1)}, u32[]{:S(2)}, u32[]{:S(2)}) %collective-permute-start) | collective-permute-done | bytes 131104 | tf_op jit(solution)/shard_map/ppermute | solution.py:221
  10.2 3.4 %collective-permute-start.1 = (bf16[256,256]{1,0:T(8,128)(2,1)S(1)}, bf16[256,256]{1,0:T(8,128)(2,1)S(1)}, u32[]{:S(2)}, u32[]{:S(2)}) collective-permute-start(bf16[256,256]{1,0:T(8,128)(2,1)S(1)} %collective-permute-done.refs_1_), channel_id=1, source_target_pairs={{0,56},{8,0},{16,8},{24,16},{32,24},{40,32},{48,40},{56,48},{64,12... | collective-permute-start | bytes 393224 | tf_op jit(solution)/shard_map/ppermute | solution.py:221
  13.6 0.0 collective-permute-done.4.refs_7_
  13.6 0.0 collective-permute-start.5
  13.6 1.9 %collective-permute-done.1.refs_2_ = bf16[256,256]{1,0:T(8,128)(2,1)S(1)} collective-permute-done((bf16[256,256]{1,0:T(8,128)(2,1)S(1)}, bf16[256,256]{1,0:T(8,128)(2,1)S(1)}, u32[]{:S(2)}, u32[]{:S(2)}) %collective-permute-start.1) | collective-permute-done | bytes 131104 | tf_op jit(solution)/shard_map/ppermute | solution.py:221
  15.6 3.1 %collective-permute-start.2 = (bf16[256,256]{1,0:T(8,128)(2,1)S(1)}, bf16[256,256]{1,0:T(8,128)(2,1)S(1)}, u32[]{:S(2)}, u32[]{:S(2)}) collective-permute-start(bf16[256,256]{1,0:T(8,128)(2,1)S(1)} %collective-permute-done.1.refs_2_), channel_id=1, source_target_pairs={{0,56},{8,0},{16,8},{24,16},{32,24},{40,32},{48,40},{56,48},{64,12... | collective-permute-start | bytes 393224 | tf_op jit(solution)/shard_map/ppermute | solution.py:221
  18.7 0.0 collective-permute-done.5.refs_6_
  18.7 1.9 %collective-permute-done.2.refs_3_ = bf16[256,256]{1,0:T(8,128)(2,1)S(1)} collective-permute-done((bf16[256,256]{1,0:T(8,128)(2,1)S(1)}, bf16[256,256]{1,0:T(8,128)(2,1)S(1)}, u32[]{:S(2)}, u32[]{:S(2)}) %collective-permute-start.2) | collective-permute-done | bytes 131104 | tf_op jit(solution)/shard_map/ppermute | solution.py:221
  20.6 3.1 %collective-permute-start.3 = (bf16[256,256]{1,0:T(8,128)(2,1)S(1)}, bf16[256,256]{1,0:T(8,128)(2,1)S(1)}, u32[]{:S(2)}, u32[]{:S(2)}) collective-permute-start(bf16[256,256]{1,0:T(8,128)(2,1)S(1)} %collective-permute-done.2.refs_3_), channel_id=1, source_target_pairs={{0,56},{8,0},{16,8},{24,16},{32,24},{40,32},{48,40},{56,48},{64,12... | collective-permute-start | bytes 393224 | tf_op jit(solution)/shard_map/ppermute | solution.py:221
  23.7 0.1 copy.14.lists_ref
  23.8 0.7 copy-done.4
  24.4 2.4 %route.1 = (s32[16]{0:T(128)S(1)}, s32[129]{0:T(256)S(1)}) custom-call(s32[1]{0:T(128)} %bitcast.me_ref, s32[64]{0:T(128)S(1)} %copy-done.4, s32[64,8]{1,0:T(8,128)S(1)} %copy.14.lists_ref), custom_call_target="tpu_custom_call" | custom-call | tf_op jit(solution)/shard_map/route/pallas_call | solution.py:232
  26.9 0.0 copy-start.3
  26.9 0.8 line.1
  27.8 1.4 %collective-permute-start.7 = (bf16[8,128,256]{2,1,0:T(8,128)(2,1)S(1)}, bf16[8,128,256]{2,1,0:T(8,128)(2,1)S(1)}, u32[]{:S(2)}, u32[]{:S(2)}) collective-permute-start(bf16[8,128,256]{2,1,0:T(8,128)(2,1)S(1)} %get-tuple-element.39), channel_id=1, source_target_pairs={{0,64},{8,72},{16,80},{24,88},{32,96},{40,104},{48,112},{56,120},{... | collective-permute-start | bytes 1572872 | tf_op jit(solution)/shard_map/ppermute | solution.py:221
  29.1 1.5 %collective-permute-start.8 = (bf16[8,128,256]{2,1,0:T(8,128)(2,1)S(1)}, bf16[8,128,256]{2,1,0:T(8,128)(2,1)S(1)}, u32[]{:S(2)}, u32[]{:S(2)}) collective-permute-start(bf16[8,128,256]{2,1,0:T(8,128)(2,1)S(1)} %get-tuple-element.40), channel_id=1, source_target_pairs={{0,192},{8,200},{16,208},{24,216},{32,224},{40,232},{48,240},{56,2... | collective-permute-start | bytes 1572872 | tf_op jit(solution)/shard_map/ppermute | solution.py:221
  30.7 1.6 %collective-permute-start.9 = (bf16[8,128,256]{2,1,0:T(8,128)(2,1)S(1)}, bf16[8,128,256]{2,1,0:T(8,128)(2,1)S(1)}, u32[]{:S(2)}, u32[]{:S(2)}) collective-permute-start(bf16[8,128,256]{2,1,0:T(8,128)(2,1)S(1)} %get-tuple-element.41), channel_id=1, source_target_pairs={{0,128},{8,136},{16,144},{24,152},{32,160},{40,168},{48,176},{56,1... | collective-permute-start | bytes 1572872 | tf_op jit(solution)/shard_map/ppermute | solution.py:221
  32.2 0.0 copy-start
  32.3 0.0 copy-start.1
  32.3 15.7 %all_to_all.24 = bf16[8,32,512]{2,1,0:T(8,128)(2,1)S(1)} all-to-all(bf16[8,32,512]{2,1,0:T(8,128)(2,1)S(1)} %columns.1), channel_id=1, replica_groups=mesh['seq'=32,'head'=8] {'head'}, dimensions={0} | all-to-all | bytes 524288 | tf_op jit(solution)/shard_map/all_to_all | solution.py:258
  48.0 2.8 %collective-permute-done.9.refs_3_ = bf16[8,128,256]{2,1,0:T(8,128)(2,1)S(1)} collective-permute-done((bf16[8,128,256]{2,1,0:T(8,128)(2,1)S(1)}, bf16[8,128,256]{2,1,0:T(8,128)(2,1)S(1)}, u32[]{:S(2)}, u32[]{:S(2)}) %collective-permute-start.9) | collective-permute-done | bytes 524320 | tf_op jit(solution)/shard_map/ppermute | solution.py:221
  50.8 7.7 %attend.1 = (bf16[256,512]{1,0:T(8,128)(2,1)}, bf16[256,512]{1,0:T(8,128)(2,1)}, f32[256,128]{1,0:T(8,128)S(1)}, f32[256,128]{1,0:T(8,128)S(1)}, bf16[4,128,256]...) custom-call(s32[1]{0:T(128)} %bitcast.me_ref, ...), custom_call_target="tpu_custom_call" | custom-call | tf_op jit(solution)/shard_map/attend/pallas_call | solution.py:265
  58.5 0.6 collective-permute-start.10
  59.1 2.1 %collective-permute-start.11 = (bf16[4,128,256]{2,1,0:T(8,128)(2,1)S(1)}, bf16[4,128,256]{2,1,0:T(8,128)(2,1)S(1)}, u32[]{:S(2)}, u32[]{:S(2)}) collective-permute-start(bf16[4,128,256]{2,1,0:T(8,128)(2,1)S(1)} %get-tuple-element.48), channel_id=1, source_target_pairs={{0,192},{8,200},{16,208},{24,216},{32,224},{40,232},{48,240},{56,2... | collective-permute-start | bytes 786440 | tf_op jit(solution)/shard_map/ppermute | solution.py:221
  61.2 0.6 collective-permute-start.16
  61.8 2.1 %collective-permute-start.17 = (bf16[4,128,256]{2,1,0:T(8,128)(2,1)S(1)}, bf16[4,128,256]{2,1,0:T(8,128)(2,1)S(1)}, u32[]{:S(2)}, u32[]{:S(2)}) collective-permute-start(bf16[4,128,256]{2,1,0:T(8,128)(2,1)S(1)} %get-tuple-element.60), channel_id=1, source_target_pairs={{0,192},{8,200},{16,208},{24,216},{32,224},{40,232},{48,240},{56,2... | collective-permute-start | bytes 786440 | tf_op jit(solution)/shard_map/ppermute | solution.py:221
  63.9 1.1 collective-permute-done.10.refs_1_
  64.9 0.7 collective-permute-start.18
  65.6 1.7 %collective-permute-done.11.refs_2_ = bf16[4,128,256]{2,1,0:T(8,128)(2,1)S(1)} collective-permute-done((bf16[4,128,256]{2,1,0:T(8,128)(2,1)S(1)}, bf16[4,128,256]{2,1,0:T(8,128)(2,1)S(1)}, u32[]{:S(2)}, u32[]{:S(2)}) %collective-permute-start.11) | collective-permute-done | bytes 262176 | tf_op jit(solution)/shard_map/ppermute | solution.py:221
  67.3 0.8 collective-permute-done.12.refs_3_
  68.1 1.0 line_sum.2
  69.1 0.3 collective-permute-start.13
  69.4 4.3 %collective-permute-start.14 = (bf16[256,256]{1,0:T(8,128)(2,1)S(1)}, bf16[256,256]{1,0:T(8,128)(2,1)S(1)}, u32[]{:S(2)}, u32[]{:S(2)}) collective-permute-start(bf16[256,256]{1,0:T(8,128)(2,1)S(1)} %get-tuple-element.51), channel_id=1, source_target_pairs={{0,40},{8,48},{16,56},{24,0},{32,8},{40,16},{48,24},{56,32},{64,10... | collective-permute-start | bytes 393224 | tf_op jit(solution)/shard_map/ppermute | solution.py:221
  73.7 16.5 %all-to-all-start.1 = ((bf16[8,32,512]{2,1,0:T(8,128)(2,1)}), bf16[8,32,512]{2,1,0:T(8,128)(2,1)S(1)}, u32[]{:S(2)}, u32[]{:S(2)}) async-start(bf16[8,32,512]{2,1,0:T(8,128)(2,1)} %bitcast.2), calls=%async_computation.1 | async-start | bytes 524288 | tf_op jit(solution)/shard_map/all_to_all | solution.py:289
  90.2 1.6 %collective-permute-start.15 = (bf16[256,256]{1,0:T(8,128)(2,1)S(1)}, bf16[256,256]{1,0:T(8,128)(2,1)S(1)}, u32[]{:S(2)}, u32[]{:S(2)}) collective-permute-start(bf16[256,256]{1,0:T(8,128)(2,1)S(1)} %get-tuple-element.52), channel_id=1, source_target_pairs={{0,32},{8,40},{16,48},{24,56},{32,0},{40,8},{48,16},{56,24},{64,96... | collective-permute-start | bytes 393224 | tf_op jit(solution)/shard_map/ppermute | solution.py:221
  91.8 1.0 line_sum.3
  92.8 0.1 collective-permute-start.19
  92.9 2.7 %collective-permute-start.20 = (bf16[256,256]{1,0:T(8,128)(2,1)S(1)}, bf16[256,256]{1,0:T(8,128)(2,1)S(1)}, u32[]{:S(2)}, u32[]{:S(2)}) collective-permute-start(bf16[256,256]{1,0:T(8,128)(2,1)S(1)} %get-tuple-element.63), channel_id=1, source_target_pairs={{0,56},{8,0},{16,8},{24,16},{32,24},{40,32},{48,40},{56,48},{64,12... | collective-permute-start | bytes 393224 | tf_op jit(solution)/shard_map/ppermute | solution.py:221
  95.6 3.6 %collective-permute-start.22 = (bf16[256,256]{1,0:T(8,128)(2,1)S(1)}, bf16[256,256]{1,0:T(8,128)(2,1)S(1)}, u32[]{:S(2)}, u32[]{:S(2)}) collective-permute-start(bf16[256,256]{1,0:T(8,128)(2,1)S(1)} %get-tuple-element.65), channel_id=1, source_target_pairs={{0,48},{8,56},{16,0},{24,8},{32,16},{40,24},{48,32},{56,40},{64,11... | collective-permute-start | bytes 393224 | tf_op jit(solution)/shard_map/ppermute | solution.py:221
  99.1 0.7 copy.16
  99.9 2.2 %collective-permute-done.15.refs_2_ = bf16[256,256]{1,0:T(8,128)(2,1)S(1)} collective-permute-done((bf16[256,256]{1,0:T(8,128)(2,1)S(1)}, bf16[256,256]{1,0:T(8,128)(2,1)S(1)}, u32[]{:S(2)}, u32[]{:S(2)}) %collective-permute-start.15) | collective-permute-done | bytes 131104 | tf_op jit(solution)/shard_map/ppermute | solution.py:221
  102.1 3.9 %collective-permute-done.21.refs_6_ = bf16[256,256]{1,0:T(8,128)(2,1)S(1)} collective-permute-done((bf16[256,256]{1,0:T(8,128)(2,1)S(1)}, bf16[256,256]{1,0:T(8,128)(2,1)S(1)}, u32[]{:S(2)}, u32[]{:S(2)}) %collective-permute-start.21) | collective-permute-done | bytes 131104 | tf_op jit(solution)/shard_map/ppermute | solution.py:221
  106.0 2.2 %collective-permute-done.22.refs_7_ = bf16[256,256]{1,0:T(8,128)(2,1)S(1)} collective-permute-done((bf16[256,256]{1,0:T(8,128)(2,1)S(1)}, bf16[256,256]{1,0:T(8,128)(2,1)S(1)}, u32[]{:S(2)}, u32[]{:S(2)}) %collective-permute-start.22) | collective-permute-done | bytes 131104 | tf_op jit(solution)/shard_map/ppermute | solution.py:221
  108.2 0.8 add.1
  (25 shorter events, 0.1 us)
Async XLA Ops:
  0.6 0.9 copy-start.2
  1.6 22.1 %copy-start.5 = (s32[64,8]{0,1:T(8,128)S(1)}, s32[64,8]{0,1:T(8,128)}, u32[]{:S(2)}) copy-start(s32[64,8]{0,1:T(8,128)} %param.10) | copy-start | bytes 6148
  1.6 8.6 %collective-permute-start = (bf16[256,256]{1,0:T(8,128)(2,1)S(1)}, bf16[256,256]{1,0:T(8,128)(2,1)S(1)}, u32[]{:S(2)}, u32[]{:S(2)}) collective-permute-start(bf16[256,256]{1,0:T(8,128)(2,1)S(1)} %constant_dynamic-update-slice_fusion.refs_0_), channel_id=1, source_target_pairs={{0,56},{8,0},{16,8},{24,16},{32,24},{40,32},{48,40},{56,48},{64,12... | collective-permute-start | bytes 393224 | tf_op jit(solution)/shard_map/ppermute | solution.py:221
  8.1 5.6 %collective-permute-start.4 = (bf16[256,256]{1,0:T(8,128)(2,1)S(1)}, bf16[256,256]{1,0:T(8,128)(2,1)S(1)}, u32[]{:S(2)}, u32[]{:S(2)}) collective-permute-start(bf16[256,256]{1,0:T(8,128)(2,1)S(1)} %constant_dynamic-update-slice_fusion.refs_0_), channel_id=1, source_target_pairs={{0,8},{8,16},{16,24},{24,32},{32,40},{40,48},{48,56},{56,0},{64,72... | collective-permute-start | bytes 393224 | tf_op jit(solution)/shard_map/ppermute | solution.py:221
  10.2 5.4 %collective-permute-start.1 = (bf16[256,256]{1,0:T(8,128)(2,1)S(1)}, bf16[256,256]{1,0:T(8,128)(2,1)S(1)}, u32[]{:S(2)}, u32[]{:S(2)}) collective-permute-start(bf16[256,256]{1,0:T(8,128)(2,1)S(1)} %collective-permute-done.refs_1_), channel_id=1, source_target_pairs={{0,56},{8,0},{16,8},{24,16},{32,24},{40,32},{48,40},{56,48},{64,12... | collective-permute-start | bytes 393224 | tf_op jit(solution)/shard_map/ppermute | solution.py:221
  13.6 5.0 %collective-permute-start.5 = (bf16[256,256]{1,0:T(8,128)(2,1)S(1)}, bf16[256,256]{1,0:T(8,128)(2,1)S(1)}, u32[]{:S(2)}, u32[]{:S(2)}) collective-permute-start(bf16[256,256]{1,0:T(8,128)(2,1)S(1)} %collective-permute-done.4.refs_7_), channel_id=1, source_target_pairs={{0,8},{8,16},{16,24},{24,32},{32,40},{40,48},{48,56},{56,0},{64,72... | collective-permute-start | bytes 393224 | tf_op jit(solution)/shard_map/ppermute | solution.py:221
  15.6 5.0 %collective-permute-start.2 = (bf16[256,256]{1,0:T(8,128)(2,1)S(1)}, bf16[256,256]{1,0:T(8,128)(2,1)S(1)}, u32[]{:S(2)}, u32[]{:S(2)}) collective-permute-start(bf16[256,256]{1,0:T(8,128)(2,1)S(1)} %collective-permute-done.1.refs_2_), channel_id=1, source_target_pairs={{0,56},{8,0},{16,8},{24,16},{32,24},{40,32},{48,40},{56,48},{64,12... | collective-permute-start | bytes 393224 | tf_op jit(solution)/shard_map/ppermute | solution.py:221
  18.7 8.2 %collective-permute-start.6 = (bf16[256,256]{1,0:T(8,128)(2,1)S(1)}, bf16[256,256]{1,0:T(8,128)(2,1)S(1)}, u32[]{:S(2)}, u32[]{:S(2)}) collective-permute-start(bf16[256,256]{1,0:T(8,128)(2,1)S(1)} %collective-permute-done.5.refs_6_), channel_id=1, source_target_pairs={{0,8},{8,16},{16,24},{24,32},{32,40},{40,48},{48,56},{56,0},{64,72... | collective-permute-start | bytes 393224 | tf_op jit(solution)/shard_map/ppermute | solution.py:221
  20.6 6.3 %collective-permute-start.3 = (bf16[256,256]{1,0:T(8,128)(2,1)S(1)}, bf16[256,256]{1,0:T(8,128)(2,1)S(1)}, u32[]{:S(2)}, u32[]{:S(2)}) collective-permute-start(bf16[256,256]{1,0:T(8,128)(2,1)S(1)} %collective-permute-done.2.refs_3_), channel_id=1, source_target_pairs={{0,56},{8,0},{16,8},{24,16},{32,24},{40,32},{48,40},{56,48},{64,12... | collective-permute-start | bytes 393224 | tf_op jit(solution)/shard_map/ppermute | solution.py:221
  23.8 0.7 copy-start.4
  26.9 5.3 %copy-start.3 = (bf16[32,4096]{1,0:T(8,128)(2,1)S(1)}, bf16[32,4096]{1,0:T(8,128)(2,1)}, u32[]{:S(2)}) copy-start(bf16[32,4096]{1,0:T(8,128)(2,1)} %cot_ref.1) | copy-start | bytes 786436
  27.8 20.2 %collective-permute-start.7 = (bf16[8,128,256]{2,1,0:T(8,128)(2,1)S(1)}, bf16[8,128,256]{2,1,0:T(8,128)(2,1)S(1)}, u32[]{:S(2)}, u32[]{:S(2)}) collective-permute-start(bf16[8,128,256]{2,1,0:T(8,128)(2,1)S(1)} %get-tuple-element.39), channel_id=1, source_target_pairs={{0,64},{8,72},{16,80},{24,88},{32,96},{40,104},{48,112},{56,120},{... | collective-permute-start | bytes 1572872 | tf_op jit(solution)/shard_map/ppermute | solution.py:221
  29.1 18.8 %collective-permute-start.8 = (bf16[8,128,256]{2,1,0:T(8,128)(2,1)S(1)}, bf16[8,128,256]{2,1,0:T(8,128)(2,1)S(1)}, u32[]{:S(2)}, u32[]{:S(2)}) collective-permute-start(bf16[8,128,256]{2,1,0:T(8,128)(2,1)S(1)} %get-tuple-element.40), channel_id=1, source_target_pairs={{0,192},{8,200},{16,208},{24,216},{32,224},{40,232},{48,240},{56,2... | collective-permute-start | bytes 1572872 | tf_op jit(solution)/shard_map/ppermute | solution.py:221
  30.7 20.2 %collective-permute-start.9 = (bf16[8,128,256]{2,1,0:T(8,128)(2,1)S(1)}, bf16[8,128,256]{2,1,0:T(8,128)(2,1)S(1)}, u32[]{:S(2)}, u32[]{:S(2)}) collective-permute-start(bf16[8,128,256]{2,1,0:T(8,128)(2,1)S(1)} %get-tuple-element.41), channel_id=1, source_target_pairs={{0,128},{8,136},{16,144},{24,152},{32,160},{40,168},{48,176},{56,1... | collective-permute-start | bytes 1572872 | tf_op jit(solution)/shard_map/ppermute | solution.py:221
  32.2 18.6 %copy-start = (bf16[256,512]{1,0:T(8,128)(2,1)S(1)}, bf16[256,512]{1,0:T(8,128)(2,1)}, u32[]{:S(2)}) copy-start(bf16[256,512]{1,0:T(8,128)(2,1)} %q_ref.1) | copy-start | bytes 786436
  32.3 18.6 %copy-start.1 = (bf16[256,128]{1,0:T(8,128)(2,1)S(1)}, bf16[256,128]{1,0:T(8,128)(2,1)}, u32[]{:S(2)}) copy-start(bf16[256,128]{1,0:T(8,128)(2,1)} %k_ref.1) | copy-start | bytes 196612
  58.5 6.4 %collective-permute-start.10 = (bf16[4,128,256]{2,1,0:T(8,128)(2,1)S(1)}, bf16[4,128,256]{2,1,0:T(8,128)(2,1)S(1)}, u32[]{:S(2)}, u32[]{:S(2)}) collective-permute-start(bf16[4,128,256]{2,1,0:T(8,128)(2,1)S(1)} %get-tuple-element.47), channel_id=1, source_target_pairs={{0,64},{8,72},{16,80},{24,88},{32,96},{40,104},{48,112},{56,120},{... | collective-permute-start | bytes 786440 | tf_op jit(solution)/shard_map/ppermute | solution.py:221
  59.1 8.2 %collective-permute-start.11 = (bf16[4,128,256]{2,1,0:T(8,128)(2,1)S(1)}, bf16[4,128,256]{2,1,0:T(8,128)(2,1)S(1)}, u32[]{:S(2)}, u32[]{:S(2)}) collective-permute-start(bf16[4,128,256]{2,1,0:T(8,128)(2,1)S(1)} %get-tuple-element.48), channel_id=1, source_target_pairs={{0,192},{8,200},{16,208},{24,216},{32,224},{40,232},{48,240},{56,2... | collective-permute-start | bytes 786440 | tf_op jit(solution)/shard_map/ppermute | solution.py:221
  61.2 6.9 %collective-permute-start.12 = (bf16[4,128,256]{2,1,0:T(8,128)(2,1)S(1)}, bf16[4,128,256]{2,1,0:T(8,128)(2,1)S(1)}, u32[]{:S(2)}, u32[]{:S(2)}) collective-permute-start(bf16[4,128,256]{2,1,0:T(8,128)(2,1)S(1)} %get-tuple-element.49), channel_id=1, source_target_pairs={{0,128},{8,136},{16,144},{24,152},{32,160},{40,168},{48,176},{56,1... | collective-permute-start | bytes 786440 | tf_op jit(solution)/shard_map/ppermute | solution.py:221
  61.2 29.0 %collective-permute-start.16 = (bf16[4,128,256]{2,1,0:T(8,128)(2,1)S(1)}, bf16[4,128,256]{2,1,0:T(8,128)(2,1)S(1)}, u32[]{:S(2)}, u32[]{:S(2)}) collective-permute-start(bf16[4,128,256]{2,1,0:T(8,128)(2,1)S(1)} %get-tuple-element.59), channel_id=1, source_target_pairs={{0,64},{8,72},{16,80},{24,88},{32,96},{40,104},{48,112},{56,120},{... | collective-permute-start | bytes 786440 | tf_op jit(solution)/shard_map/ppermute | solution.py:221
  61.8 30.0 %collective-permute-start.17 = (bf16[4,128,256]{2,1,0:T(8,128)(2,1)S(1)}, bf16[4,128,256]{2,1,0:T(8,128)(2,1)S(1)}, u32[]{:S(2)}, u32[]{:S(2)}) collective-permute-start(bf16[4,128,256]{2,1,0:T(8,128)(2,1)S(1)} %get-tuple-element.60), channel_id=1, source_target_pairs={{0,192},{8,200},{16,208},{24,216},{32,224},{40,232},{48,240},{56,2... | collective-permute-start | bytes 786440 | tf_op jit(solution)/shard_map/ppermute | solution.py:221
  64.9 26.9 %collective-permute-start.18 = (bf16[4,128,256]{2,1,0:T(8,128)(2,1)S(1)}, bf16[4,128,256]{2,1,0:T(8,128)(2,1)S(1)}, u32[]{:S(2)}, u32[]{:S(2)}) collective-permute-start(bf16[4,128,256]{2,1,0:T(8,128)(2,1)S(1)} %get-tuple-element.61), channel_id=1, source_target_pairs={{0,128},{8,136},{16,144},{24,152},{32,160},{40,168},{48,176},{56,1... | collective-permute-start | bytes 786440 | tf_op jit(solution)/shard_map/ppermute | solution.py:221
  69.1 26.5 %collective-permute-start.13 = (bf16[256,256]{1,0:T(8,128)(2,1)S(1)}, bf16[256,256]{1,0:T(8,128)(2,1)S(1)}, u32[]{:S(2)}, u32[]{:S(2)}) collective-permute-start(bf16[256,256]{1,0:T(8,128)(2,1)S(1)} %get-tuple-element.50), channel_id=1, source_target_pairs={{0,24},{8,32},{16,40},{24,48},{32,56},{40,0},{48,8},{56,16},{64,88... | collective-permute-start | bytes 393224 | tf_op jit(solution)/shard_map/ppermute | solution.py:221
  69.4 26.2 %collective-permute-start.14 = (bf16[256,256]{1,0:T(8,128)(2,1)S(1)}, bf16[256,256]{1,0:T(8,128)(2,1)S(1)}, u32[]{:S(2)}, u32[]{:S(2)}) collective-permute-start(bf16[256,256]{1,0:T(8,128)(2,1)S(1)} %get-tuple-element.51), channel_id=1, source_target_pairs={{0,40},{8,48},{16,56},{24,0},{32,8},{40,16},{48,24},{56,32},{64,10... | collective-permute-start | bytes 393224 | tf_op jit(solution)/shard_map/ppermute | solution.py:221
  73.7 25.5 %all-to-all-start.1 = ((bf16[8,32,512]{2,1,0:T(8,128)(2,1)}), bf16[8,32,512]{2,1,0:T(8,128)(2,1)S(1)}, u32[]{:S(2)}, u32[]{:S(2)}) async-start(bf16[8,32,512]{2,1,0:T(8,128)(2,1)} %bitcast.2), calls=%async_computation.1 | async-start | bytes 524288 | tf_op jit(solution)/shard_map/all_to_all | solution.py:289
  90.2 11.9 %collective-permute-start.15 = (bf16[256,256]{1,0:T(8,128)(2,1)S(1)}, bf16[256,256]{1,0:T(8,128)(2,1)S(1)}, u32[]{:S(2)}, u32[]{:S(2)}) collective-permute-start(bf16[256,256]{1,0:T(8,128)(2,1)S(1)} %get-tuple-element.52), channel_id=1, source_target_pairs={{0,32},{8,40},{16,48},{24,56},{32,0},{40,8},{48,16},{56,24},{64,96... | collective-permute-start | bytes 393224 | tf_op jit(solution)/shard_map/ppermute | solution.py:221
  92.8 9.3 %collective-permute-start.19 = (bf16[256,256]{1,0:T(8,128)(2,1)S(1)}, bf16[256,256]{1,0:T(8,128)(2,1)S(1)}, u32[]{:S(2)}, u32[]{:S(2)}) collective-permute-start(bf16[256,256]{1,0:T(8,128)(2,1)S(1)} %get-tuple-element.62), channel_id=1, source_target_pairs={{0,8},{8,16},{16,24},{24,32},{32,40},{40,48},{48,56},{56,0},{64,72... | collective-permute-start | bytes 393224 | tf_op jit(solution)/shard_map/ppermute | solution.py:221
  92.9 9.2 %collective-permute-start.20 = (bf16[256,256]{1,0:T(8,128)(2,1)S(1)}, bf16[256,256]{1,0:T(8,128)(2,1)S(1)}, u32[]{:S(2)}, u32[]{:S(2)}) collective-permute-start(bf16[256,256]{1,0:T(8,128)(2,1)S(1)} %get-tuple-element.63), channel_id=1, source_target_pairs={{0,56},{8,0},{16,8},{24,16},{32,24},{40,32},{48,40},{56,48},{64,12... | collective-permute-start | bytes 393224 | tf_op jit(solution)/shard_map/ppermute | solution.py:221
  95.6 10.5 %collective-permute-start.21 = (bf16[256,256]{1,0:T(8,128)(2,1)S(1)}, bf16[256,256]{1,0:T(8,128)(2,1)S(1)}, u32[]{:S(2)}, u32[]{:S(2)}) collective-permute-start(bf16[256,256]{1,0:T(8,128)(2,1)S(1)} %get-tuple-element.64), channel_id=1, source_target_pairs={{0,16},{8,24},{16,32},{24,40},{32,48},{40,56},{48,0},{56,8},{64,80... | collective-permute-start | bytes 393224 | tf_op jit(solution)/shard_map/ppermute | solution.py:221
  95.6 12.7 %collective-permute-start.22 = (bf16[256,256]{1,0:T(8,128)(2,1)S(1)}, bf16[256,256]{1,0:T(8,128)(2,1)S(1)}, u32[]{:S(2)}, u32[]{:S(2)}) collective-permute-start(bf16[256,256]{1,0:T(8,128)(2,1)S(1)} %get-tuple-element.65), channel_id=1, source_target_pairs={{0,48},{8,56},{16,0},{24,8},{32,16},{40,24},{48,32},{56,40},{64,11... | collective-permute-start | bytes 393224 | tf_op jit(solution)/shard_map/ppermute | solution.py:221
